TPU v7x, 32 devices: a whole 2x2x4 slice. The times are simulated.
32 devices in a mesh: sensor: 16 (over z, y, core), tm: 2 (over x).
Axes of the slice: x: 2, y: 2, z: 4, core: 2. Of those that a mesh axis runs over, the one named last changes fastest.
Arguments:
- tokens: bfloat16 [2048, 32, 256], P(('sensor', 'tm')), may hold values from -6 to 6
- gain_time: float32 [256], replicated, may hold values from 0.1 to 1.9
- wq_time: bfloat16 [256, 256], replicated
- wkv_time: bfloat16 [256, 512], replicated
- wo_time: bfloat16 [256, 256], replicated, may hold values from -0.375 to 0.375
- gain_graph: float32 [256], replicated, may hold values from 0.1 to 1.9
- wq_graph: bfloat16 [256, 256], replicated
- wkv_graph: bfloat16 [256, 512], replicated
- wo_graph: bfloat16 [256, 256], replicated, may hold values from -0.375 to 0.375
- gain_ffn: float32 [256], replicated, may hold values from 0.1 to 1.9
- w_in: bfloat16 [256, 1024], replicated, may hold values from -0.375 to 0.375
- w_out: bfloat16 [1024, 256], replicated, may hold values from -0.1875 to 0.1875
- neighbour_blocks: int32 [16, 8], replicated, may hold values from 0 to 15, all different within a row
- slot_used_mask: int32 [16, 8], P('sensor'), may hold values 0 or 1
- neighbour_rows: int32 [16, 8, 4], replicated, may hold values from 0 to 127
Outputs:
- layer_out: bfloat16 [2048, 32, 256], P('sensor', 'tm')
Inputs may be any that keep to these rules, and one draw needn't show every extreme that they name: `neighbour_blocks`: each row names 8 different sensor blocks, and every block is named by some row.
All inputs are finite; a program needn't handle non-finite values. No bound on the sum of `slot_used_mask` on one device may be relied on, other than what follows from the above.
Results may differ from a plain program's by a relative error of at most 0.0075.
Values may be sent and summed in bfloat16 or wider, within the bound.
No kernel may reach another device: no remote copies, remote signals or barrier semaphores. Data moves between devices by JAX's collectives and lax.ppermute only.
A program may use at most 64 MiB of HBM per device.

v0:
```python
import math

import jax
import jax.numpy as jnp
from jax import lax
from jax.sharding import PartitionSpec as P

H = 8
REMOTE_SENSORS = 4


EPSILON = 1e-06


def rms_norm(values, gain_vec):
    widened = values.astype(jnp.float32)
    inverse = lax.rsqrt(jnp.mean(widened * widened, axis=-1, keepdims=True) + EPSILON)
    return (widened * inverse * gain_vec).astype(jnp.bfloat16)


def project(row_data, weight):
    flattened = row_data.reshape(-1, row_data.shape[-1])
    result = jnp.dot(flattened, weight, preferred_element_type=jnp.float32).astype(jnp.bfloat16)
    return result.reshape(row_data.shape[:-1] + (weight.shape[1],))


def softmax_bf16(scores, allowed):
    masked = jnp.where(allowed, scores, jnp.float32(-1e30))
    highest = jnp.max(masked, axis=-1, keepdims=True)
    exponent = jnp.exp(masked - highest)
    return (exponent / jnp.sum(exponent, axis=-1, keepdims=True)).astype(jnp.bfloat16)


def local(
    tokens,
    gain_time,
    wq_time,
    wkv_time,
    wo_time,
    gain_graph,
    wq_graph,
    wkv_graph,
    wo_graph,
    gain_ffn,
    w_in,
    w_out,
    neighbour_blocks,
    slot_used_mask,
    neighbour_rows,
):
    sensors_here, time_len, model_width = tokens.shape
    head_size = model_width // H
    normed = rms_norm(tokens, gain_time)
    queries = project(normed, wq_time).reshape(sensors_here, time_len, H, head_size)
    key_val = project(normed, wkv_time)
    keys_all = key_val[..., :model_width].reshape(sensors_here, time_len, H, head_size)
    vals_all = key_val[..., model_width:].reshape(sensors_here, time_len, H, head_size)
    scores = jnp.einsum(
        "stha,suha->shtu", queries, keys_all, preferred_element_type=jnp.float32
    ) / math.sqrt(head_size)
    positions = jnp.arange(time_len)
    causal = positions[None, :] <= positions[:, None]
    weights = softmax_bf16(scores, causal)
    context = jnp.einsum(
        "shtu,suha->stha", weights, vals_all, preferred_element_type=jnp.float32
    ).astype(jnp.bfloat16)
    context = context.reshape(sensors_here * time_len, model_width)
    mixed_out = jnp.dot(context, wo_time, preferred_element_type=jnp.float32).reshape(tokens.shape)
    temporal_output = (tokens.astype(jnp.float32) + mixed_out).astype(jnp.bfloat16)
    moved = lax.all_to_all(temporal_output, "tm", split_axis=1, concat_axis=0, tiled=True)
    block_len, group_len = (moved.shape[0], moved.shape[1])
    normed_graph = rms_norm(moved, gain_graph)
    queries_graph = project(normed_graph, wq_graph)
    local_kv = project(normed_graph, wkv_graph)
    block_index = lax.axis_index("sensor")
    block_count = neighbour_blocks.shape[0]
    matches = (neighbour_blocks == block_index).astype(jnp.int32)
    wanted = jnp.sum(matches[:, :, None] * neighbour_rows, axis=1).reshape(-1)
    own_list = lax.dynamic_index_in_dim(neighbour_blocks, block_index, 0, keepdims=False)
    outgoing = jnp.take(local_kv, wanted, axis=0).reshape(
        block_count, REMOTE_SENSORS, group_len, 2 * model_width
    )
    incoming = lax.all_to_all(outgoing, "sensor", split_axis=0, concat_axis=0, tiled=True)
    remote_kv = jnp.take(incoming, own_list, axis=0).reshape(-1, group_len, 2 * model_width)
    all_kv = jnp.concatenate([local_kv, remote_kv], axis=0)
    key_count = all_kv.shape[0]
    live_row = slot_used_mask[0] > 0
    allowed = jnp.concatenate(
        [jnp.ones((block_len,), jnp.bool_), jnp.repeat(live_row, REMOTE_SENSORS)]
    )
    stepwise_q = queries_graph.reshape(block_len, group_len, H, head_size).transpose(1, 0, 2, 3)
    stepwise_kv = all_kv.transpose(1, 0, 2)

    def one_step(carried):
        query_step, kv_step = carried
        key_step = kv_step[:, :model_width].reshape(key_count, H, head_size)
        val_step = kv_step[:, model_width:].reshape(key_count, H, head_size)
        scores_step = jnp.einsum(
            "sha,uha->hsu", query_step, key_step, preferred_element_type=jnp.float32
        ) / math.sqrt(head_size)
        weights_step = softmax_bf16(scores_step, allowed)
        return jnp.einsum(
            "hsu,uha->sha", weights_step, val_step, preferred_element_type=jnp.float32
        ).astype(jnp.bfloat16)

    context_graph = lax.map(one_step, (stepwise_q, stepwise_kv))
    context_graph = context_graph.transpose(1, 0, 2, 3).reshape(block_len * group_len, model_width)
    after_graph = moved.astype(jnp.float32) + jnp.dot(
        context_graph, wo_graph, preferred_element_type=jnp.float32
    ).reshape(moved.shape)
    normed_ffn = rms_norm(after_graph, gain_ffn).reshape(-1, model_width)
    hidden = jax.nn.gelu(jnp.dot(normed_ffn, w_in, preferred_element_type=jnp.float32)).astype(
        jnp.bfloat16
    )
    return (
        after_graph
        + jnp.dot(hidden, w_out, preferred_element_type=jnp.float32).reshape(moved.shape)
    ).astype(jnp.bfloat16)


def solution(mesh):
    in_specs = (
        P(("sensor", "tm"), None, None),
        P(),
        P(),
        P(),
        P(),
        P(),
        P(),
        P(),
        P(),
        P(),
        P(),
        P(),
        P(),
        P("sensor", None),
        P(),
    )
    out_specs = P("sensor", "tm", None)
    return jax.shard_map(local, mesh=mesh, in_specs=in_specs, out_specs=out_specs, check_vma=False)
```

profile of v0, /device:TPU:0, one launch (start us, length us, event | category | flops | bytes accessed | tf_op | source)
XLA Modules:
  0.0 197.9 jit_solution(13552114543759602185)
XLA Ops:
  0.0 1.6 fusion.39
  1.7 1.6 fusion.41
  3.2 1.7 convolution_convert_fusion.2
  4.9 1.3 fusion.60
  6.2 2.2 %copy.86 = bf16[64,32,256]{0,2,1:T(8,128)(2,1)} copy(bf16[64,32,256]{2,1,0:T(8,128)(2,1)S(1)} %get-tuple-element.60) | data formatting | bytes 2097152
  8.4 7.7 %copy.65 = bf16[64,32,8,32]{3,1,2,0:T(8,128)(2,1)} copy(bf16[64,32,8,32]{0,3,2,1:T(8,128)(2,1)} %bitcast.114) | data formatting | bytes 2097152 | tf_op jit(solution)/shard_map/reshape | solution.py:56
  16.5 3.3 %reshape_reshape.6 = bf16[64,32,8,32]{3,2,1,0:T(8,128)(2,1)} reshape(bf16[2048,256]{1,0:T(8,128)(2,1)S(1)} %convolution_convert_fusion.4) | data formatting | bytes 2097152 | tf_op jit(solution)/shard_map/reshape;reshape | solution.py:54
  19.9 3.2 %copy.62 = bf16[64,32,256]{1,2,0:T(8,128)(2,1)} copy(bf16[64,32,256]{2,1,0:T(8,128)(2,1)S(1)} %copy-done.5) | data formatting | bytes 2097152 | tf_op jit(solution)/shard_map/slice | solution.py:57
  23.0 5.8 %fusion.28 = f32[64,8,32,32]{2,3,1,0:T(8,128)S(1)} fusion(bf16[64,32,8,32]{3,1,2,0:T(8,128)(2,1)} %copy.65, bf16[64,32,8,32]{3,2,1,0:T(8,128)(2,1)} %reshape_reshape.6), kind=kOutput, calls=%fused_computation.36 | convolution fusion | flops 33554432 | bytes 4194304 | tf_op jit(solution)/shard_map/stha,suha->shtu/dot_general | solution.py:58
  28.8 4.9 %fusion.61 = (f32[64,8,32]{2,1,0:T(8,128)S(1)}, f32[64,8,32,32]{2,3,1,0:T(8,128)}) fusion(f32[64,8,32,32]{2,3,1,0:T(8,128)S(1)} %fusion.28, pred[32,32]{0,1:T(8,128)(4,1)S(1)} %iota_compare_fusion), kind=kOutput, calls=%fused_computation.97 | output fusion | flops 3145759 | bytes 4260864 | tf_op jit(solution)/shard_map/sub | solution.py:30
  33.7 4.7 %fusion.38 = bf16[64,8,32,32]{3,2,1,0:T(8,128)(2,1)S(1)} fusion(bf16[64,32,8,32]{1,3,2,0:T(8,128)(2,1)S(1)} %bitcast.116, f32[64,8,32,32]{2,3,1,0:T(8,128)} %get-tuple-element.63, f32[64,8,32]{2,1,0:T(8,128)S(1)} %get-tuple-element.62), kind=kOutput, calls=%fused_computation.49 | convolution fusion | flops 35127296 | bytes 4259840 | tf_op jit(solution)/shard_map/shtu,suha->stha/dot_general | solution.py:64
  39.7 1.6 copy.68
  41.3 4.6 %all-to-all-start = ((bf16[64,32,256]{2,0,1:T(8,128)(2,1)}), bf16[64,32,256]{2,0,1:T(8,128)(2,1)}, u32[]{:S(2)}, u32[]{:S(2)}) async-start(bf16[64,32,256]{2,0,1:T(8,128)(2,1)} %copy.68), calls=%async_computation | async-start | bytes 2097152 | tf_op jit(solution)/shard_map/all_to_all | solution.py:70
  46.3 14.8 %all-to-all-done = bf16[64,32,256]{2,0,1:T(8,128)(2,1)} async-done(((bf16[64,32,256]{2,0,1:T(8,128)(2,1)}), bf16[64,32,256]{2,0,1:T(8,128)(2,1)}, u32[]{:S(2)}, u32[]{:S(2)}) %all-to-all-start) | async-done | bytes 1048608 | tf_op jit(solution)/shard_map/all_to_all | solution.py:70
  61.1 1.8 copy_convert_fusion
  62.9 1.6 copy.71
  64.5 1.9 multiply_reduce_fusion.1
  66.6 1.9 fusion.44
  69.6 2.1 %convolution_convert_fusion.1 = bf16[2048,512]{1,0:T(8,128)(2,1)} fusion(bf16[2048,256]{1,0:T(8,128)(2,1)S(1)} %fusion.44, bf16[256,512]{1,0:T(8,128)(2,1)S(1)} %copy-done.6), kind=kOutput, calls=%fused_computation.47 | convolution fusion | flops 537919488 | bytes 3407872 | tf_op jit(solution)/shard_map/dot_general | solution.py:23
  71.7 3.2 %gather_fusion = bf16[64,16,512]{2,1,0:T(8,128)(2,1)} fusion(bf16[128,16,512]{2,1,0:T(8,128)(2,1)} %bitcast.108, s32[1024]{0:T(1024)S(1)} %pad_clamp_fusion.1), kind=kCustom, calls=%fused_computation | custom fusion | bytes 2097408 | tf_op jit(solution)/shard_map/jit(_take)/gather | solution.py:80
  74.9 2.4 %broadcast_select_fusion = bf16[16,4,16,512]{3,2,1,0:T(8,128)(2,1)} fusion(bf16[16,4,16,512]{3,2,1,0:T(8,128)(2,1)} %bitcast.117, pred[16,4]{1,0:T(8,128)(4,1)S(1)} %copy.74), kind=kLoop, calls=%fused_computation.66 | loop fusion | flops 524288 | bytes 2097216 | tf_op jit(solution)/shard_map/jit(_take)/select_n | solution.py:80
  77.2 6.0 %all-to-all-start.1 = ((bf16[16,4,16,512]{3,2,1,0:T(8,128)(2,1)}), bf16[16,4,16,512]{3,2,1,0:T(8,128)(2,1)}, u32[]{:S(2)}, u32[]{:S(2)}) async-start(bf16[16,4,16,512]{3,2,1,0:T(8,128)(2,1)} %broadcast_select_fusion), calls=%async_computation.1 | async-start | bytes 2097152 | tf_op jit(solution)/shard_map/all_to_all | solution.py:83
  83.9 4.6 %copy.76 = bf16[128,16,512]{0,2,1:T(8,128)(2,1)} copy(bf16[128,16,512]{2,1,0:T(8,128)(2,1)} %bitcast.109) | data formatting | bytes 4194304 | tf_op jit(solution)/shard_map/reshape | solution.py:24
  88.5 2.5 %copy.70 = f32[2,64,16,256]{3,1,0,2:T(8,128)} copy(f32[2,64,16,256]{3,2,0,1:T(8,128)S(1)} %bitcast.106) | data formatting | bytes 4194304 | tf_op jit(solution)/shard_map/convert_element_type | solution.py:108
  91.4 3.4 %reshape_reshape.7 = bf16[128,16,8,32]{3,2,1,0:T(8,128)(2,1)} reshape(bf16[2048,256]{1,0:T(8,128)(2,1)S(1)} %convolution_convert_fusion.3) | data formatting | bytes 2097152 | tf_op jit(solution)/shard_map/reshape;reshape | solution.py:91
  94.8 6.3 %copy.78 = bf16[16,128,8,32]{1,3,2,0:T(8,128)(2,1)} copy(bf16[16,128,8,32]{3,2,0,1:T(8,128)(2,1)} %bitcast.107) | data formatting | bytes 2097152 | tf_op jit(solution)/shard_map/while | solution.py:106
  101.1 5.2 %all-to-all-done.1 = bf16[16,4,16,512]{3,2,1,0:T(8,128)(2,1)} async-done(((bf16[16,4,16,512]{3,2,1,0:T(8,128)(2,1)}), bf16[16,4,16,512]{3,2,1,0:T(8,128)(2,1)}, u32[]{:S(2)}, u32[]{:S(2)}) %all-to-all-start.1) | async-done | bytes 1048608 | tf_op jit(solution)/shard_map/all_to_all | solution.py:83
  106.3 1.8 gather_fusion.1
  109.3 4.4 %maximum_bitcast_fusion = bf16[16,160,512]{1,2,0:T(8,128)(2,1)} fusion(bf16[32,16,512]{0,2,1:T(8,128)(2,1)S(1)} %copy.77, bf16[128,16,512]{0,2,1:T(8,128)(2,1)} %copy.76), kind=kLoop, calls=%fused_computation.35 | loop fusion | flops 5242880 | bytes 5242880 | tf_op jit(solution)/shard_map/transpose | solution.py:92
  113.7 69.6 %while.10 = (s32[]{:T(128)}, bf16[16,128,8,32]{1,3,2,0:T(8,128)(2,1)}, bf16[16,160,512]{1,2,0:T(8,128)(2,1)}, pred[160]{0:T(512)(128)(4,1)S(1)}, bf16[16,128,8,32]{1,3,2,0:T(8,128)(2,1)}, /*index=5*/s32[]{:T(128)}) while((s32[]{:T(128)}, bf16[16,128,8,32]{1,3,2,0:T(8,128)(2,1)}, bf16[16,160,512]{1,2,0:T(8,128)(2,1)}, ...), condition=%wide.region_8.9_spmd, body=%wide.region_5.8_spmd.sunk | while | flops 32965952 | bytes 3123081 | solution.py:106
  124.6 1.3 fusion.98
  129.0 1.3 fusion.98
  133.3 1.3 fusion.98
  137.7 1.3 fusion.98
  142.0 1.3 fusion.98
  146.3 1.3 fusion.98
  150.7 1.3 fusion.98
  155.0 1.3 fusion.98
  159.4 1.3 fusion.98
  163.7 1.3 fusion.98
  168.1 1.3 fusion.98
  172.4 1.3 fusion.98
  181.1 1.3 fusion.98
  183.3 2.7 %multiply_reduce_fusion = (f32[128,16]{0,1:T(8,128)S(1)}, f32[128,16,256]{2,0,1:T(8,128)S(1)}) fusion(bf16[128,16,256]{0,2,1:T(8,128)(2,1)} %bitcast.122, bf16[256,256]{1,0:T(8,128)(2,1)S(1)} %copy-done.10, f32[2,64,16,256]{3,1,0,2:T(8,128)} %copy.70), kind=kOutput, calls=%fused_computation.63 | convolution fusion | flops 270006272 | bytes 5382144 | tf_op jit(solution)/shard_map/dot_general | solution.py:108
  186.4 1.6 copy.80
  188.0 5.6 %fusion.33 = f32[2048,256]{1,0:T(8,128)} fusion(bf16[1024,256]{1,0:T(8,128)(2,1)S(1)} %copy-done, bf16[2048,256]{1,0:T(8,128)(2,1)} %bitcast.121, bf16[256,1024]{1,0:T(8,128)(2,1)S(1)} %copy-done.15), kind=kOutput, calls=%fused_computation.41 | convolution fusion | flops 2166358016 | bytes 4194304 | tf_op jit(solution)/shard_map/dot_general | solution.py:117
  193.6 2.8 %fusion.45 = bf16[128,16,256]{2,0,1:T(8,128)(2,1)S(1)} fusion(f32[128,16,256]{2,0,1:T(8,128)S(1)} %get-tuple-element.65, f32[128,16,256]{2,1,0:T(8,128)} %bitcast.120), kind=kLoop, calls=%fused_computation.61 | loop fusion | flops 1048576 | bytes 5242880 | tf_op jit(solution)/shard_map/convert_element_type | solution.py:118
  196.3 1.6 copy.82
  (133 shorter events, 58.9 us)
Async XLA Ops:
  0.0 188.0 %copy-start = (bf16[1024,256]{1,0:T(8,128)(2,1)S(1)}, bf16[1024,256]{1,0:T(8,128)(2,1)}, u32[]{:S(2)}) copy-start(bf16[1024,256]{1,0:T(8,128)(2,1)} %param.28) | copy-start | bytes 1572868
  6.2 9.9 %copy-start.7 = (bf16[256,256]{1,0:T(8,128)(2,1)S(1)}, bf16[256,256]{1,0:T(8,128)(2,1)}, u32[]{:S(2)}) copy-start(bf16[256,256]{1,0:T(8,128)(2,1)} %param.19) | copy-start | bytes 393220
  16.5 3.3 %copy-start.5 = (bf16[64,32,256]{2,1,0:T(8,128)(2,1)S(1)}, bf16[64,32,256]{2,1,0:T(8,128)(2,1)}, u32[]{:S(2)}) copy-start(bf16[64,32,256]{2,1,0:T(8,128)(2,1)} %get-tuple-element.61) | copy-start | bytes 3145732
  28.8 4.9 %copy-start.4 = (bf16[64,32,256]{1,2,0:T(8,128)(2,1)S(1)}, bf16[64,32,256]{1,2,0:T(8,128)(2,1)}, u32[]{:S(2)}) copy-start(bf16[64,32,256]{1,2,0:T(8,128)(2,1)} %copy.62) | copy-start | bytes 3145732
  33.7 4.8 %copy-start.1 = (bf16[64,32,256]{2,1,0:T(8,128)(2,1)S(1)}, bf16[64,32,256]{2,1,0:T(8,128)(2,1)}, u32[]{:S(2)}) copy-start(bf16[64,32,256]{2,1,0:T(8,128)(2,1)} %param.17) | copy-start | bytes 3145732
  33.7 4.8 %copy-start.8 = (bf16[256,256]{1,0:T(8,128)(2,1)S(1)}, bf16[256,256]{1,0:T(8,128)(2,1)}, u32[]{:S(2)}) copy-start(bf16[256,256]{1,0:T(8,128)(2,1)} %param.21) | copy-start | bytes 393220
  38.4 7.4 %copy-start.11 = (s32[16,8]{0,1:T(8,128)S(1)}, s32[16,8]{0,1:T(8,128)}, u32[]{:S(2)}) copy-start(s32[16,8]{0,1:T(8,128)} %param.29) | copy-start | bytes 1540
  38.5 7.5 %copy-start.12 = (s32[16,8,4]{0,2,1:T(4,128)S(1)}, s32[16,8,4]{0,2,1:T(4,128)}, u32[]{:S(2)}) copy-start(s32[16,8,4]{0,2,1:T(4,128)} %param.31) | copy-start | bytes 6148
  41.3 19.8 %all-to-all-start = ((bf16[64,32,256]{2,0,1:T(8,128)(2,1)}), bf16[64,32,256]{2,0,1:T(8,128)(2,1)}, u32[]{:S(2)}, u32[]{:S(2)}) async-start(bf16[64,32,256]{2,0,1:T(8,128)(2,1)} %copy.68), calls=%async_computation | async-start | bytes 2097152 | tf_op jit(solution)/shard_map/all_to_all | solution.py:70
  46.2 20.4 %copy-start.13 = (f32[256]{0:T(256)S(1)}, f32[256]{0:T(256)}, u32[]{:S(2)}) copy-start(f32[256]{0:T(256)} %param.22) | copy-start | bytes 3076
  62.9 6.7 %copy-start.6 = (bf16[256,512]{1,0:T(8,128)(2,1)S(1)}, bf16[256,512]{1,0:T(8,128)(2,1)}, u32[]{:S(2)}) copy-start(bf16[256,512]{1,0:T(8,128)(2,1)} %param.24) | copy-start | bytes 786436
  68.6 1.1 copy-start.2
  69.6 14.0 %copy-start.16 = (s32[1,8]{1,0:T(1,128)S(1)}, s32[1,8]{1,0:T(1,128)}, u32[]{:S(2)}) copy-start(s32[1,8]{1,0:T(1,128)} %param.30) | copy-start | bytes 100
  77.2 29.0 %all-to-all-start.1 = ((bf16[16,4,16,512]{3,2,1,0:T(8,128)(2,1)}), bf16[16,4,16,512]{3,2,1,0:T(8,128)(2,1)}, u32[]{:S(2)}, u32[]{:S(2)}) async-start(bf16[16,4,16,512]{3,2,1,0:T(8,128)(2,1)} %broadcast_select_fusion), calls=%async_computation.1 | async-start | bytes 2097152 | tf_op jit(solution)/shard_map/all_to_all | solution.py:83
  83.9 7.1 %copy-start.9 = (bf16[256,256]{1,0:T(8,128)(2,1)S(1)}, bf16[256,256]{1,0:T(8,128)(2,1)}, u32[]{:S(2)}) copy-start(bf16[256,256]{1,0:T(8,128)(2,1)} %param.23) | copy-start | bytes 393220
  88.5 2.6 %copy-start.3 = (bf16[2048,256]{1,0:T(8,128)(2,1)S(1)}, bf16[2048,256]{1,0:T(8,128)(2,1)}, u32[]{:S(2)}) copy-start(bf16[2048,256]{1,0:T(8,128)(2,1)} %copy-done.2) | copy-start | bytes 3145732
  113.7 69.6 %copy-start.10 = (bf16[256,256]{1,0:T(8,128)(2,1)S(1)}, bf16[256,256]{1,0:T(8,128)(2,1)}, u32[]{:S(2)}) copy-start(bf16[256,256]{1,0:T(8,128)(2,1)} %param.25) | copy-start | bytes 393220
  183.3 2.7 %copy-start.14 = (f32[256]{0:T(256)S(1)}, f32[256]{0:T(256)}, u32[]{:S(2)}) copy-start(f32[256]{0:T(256)} %param.26) | copy-start | bytes 3076
  183.3 4.7 %copy-start.15 = (bf16[256,1024]{1,0:T(8,128)(2,1)S(1)}, bf16[256,1024]{1,0:T(8,128)(2,1)}, u32[]{:S(2)}) copy-start(bf16[256,1024]{1,0:T(8,128)(2,1)} %param.27) | copy-start | bytes 1572868
where the time goes:
time: 202 us; the launch traced here: 198 us
  matrix products  78 us (39%)
  local copies, waits for them, and re-layouts  64.8 us (32%)
  other arithmetic  23.8 us (12%)
  waiting for transfers between devices  20 us (10%)
  starting transfers between devices  10.6 us (5%)
    sub x16, matrix products, softmax_bf16(): exponent = jnp.exp(masked - highest)  20 us
    dot_general x16, matrix products, one_step(): jnp.einsum('sha,uha->hsu', query_step, key_step, preferred_element_type=j...  18.4 us
    squeeze x16, local copies, waits for them, and re-layouts, local(): context_graph = lax.map(one_step, (stepwise_q, stepwise_kv))  15.5 us
    dot_general x16, matrix products, one_step(): jnp.einsum('hsu,uha->sha', weights_step, val_step, preferred_element_type...  14.9 us
    all_to_all x1, waiting for transfers between devices, local(): lax.all_to_all(temporal_output, 'tm', split_axis=1, concat_axis=0, tiled=...  14.8 us
    reshape x1, local copies, waits for them, and re-layouts, local(): key_val[..., :model_width].reshape(sensors_here, time_len, H, head_size)  7.7 us
    while x1, local copies, waits for them, and re-layouts, local(): context_graph = lax.map(one_step, (stepwise_q, stepwise_kv))  6.32 us
    all_to_all x1, starting transfers between devices, local(): lax.all_to_all(outgoing, 'sensor', split_axis=0, concat_axis=0, tiled=True)  6.04 us
  transfers between devices with their start and end apart: 2, of which 2 were waited for; matrix products, arithmetic and copies ran while one was open for 9% of the time, Pallas kernels for 0%

commit v1 on v0

v1 whole, which is shorter than its diff:
```python
import functools
import math

import jax
import jax.numpy as jnp
from jax import lax
from jax.experimental import pallas as pl
from jax.experimental.pallas import tpu as pltpu
from jax.sharding import PartitionSpec as P

H = 8
HEAD = 32
REMOTE_SENSORS = 4
EPSILON = 1e-06
NEG = -1e30
SCALE = math.log2(math.e) / math.sqrt(HEAD)
F32 = jnp.float32
BF16 = jnp.bfloat16
VMEM_LIMIT = 48 * 1024 * 1024


def dot(a, b):
    return jnp.dot(a, b, preferred_element_type=F32)


def dot_nt(a, b):
    return lax.dot_general(a, b, (((1,), (1,)), ((), ())), preferred_element_type=F32)


def dot_tn(a, b):
    return lax.dot_general(a, b, (((0,), (0,)), ((), ())), preferred_element_type=F32)


def rms(x, gain):
    inverse = lax.rsqrt(jnp.mean(x * x, axis=-1, keepdims=True) + EPSILON)
    return (x * inverse * gain).astype(BF16)


def swap16():
    row = lax.broadcasted_iota(jnp.int32, (256, 256), 0)
    col = lax.broadcasted_iota(jnp.int32, (256, 256), 1)
    return (col == ((row & 15) << 4) + (row >> 4)).astype(BF16)


def head_rows(rows, lanes, head_of_row, first_head):
    row = lax.broadcasted_iota(jnp.int32, (rows, lanes), 0)
    lane = lax.broadcasted_iota(jnp.int32, (rows, lanes), 1)
    return (lane // HEAD + first_head == row // head_of_row).astype(BF16)


def time_kernel(split, my_ref, x_ref, gain_ref, wq_ref, wkv_ref, wo_ref, *refs):
    if split:
        keep_ref, send_ref, q_s, k_s, v_s, c_s, after_s = refs
    else:
        out_ref, q_s, k_s, v_s, c_s = refs
    sensors, steps, width = x_ref.shape
    rows = sensors * steps
    x = x_ref[...].reshape(rows, width).astype(F32)
    normed = rms(x, gain_ref[...])
    q_s[...] = dot(normed, wq_ref[...]).astype(BF16)
    kv = dot(normed, wkv_ref[...]).astype(BF16)
    k_s[...] = kv[:, :width]
    v_s[...] = kv[:, width:]
    lanes = H * steps
    mask = head_rows(lanes, width, steps, 0)
    key_t = lax.broadcasted_iota(jnp.int32, (steps, lanes), 0)
    query_t = lax.broadcasted_iota(jnp.int32, (steps, lanes), 1) & (steps - 1)
    causal = key_t <= query_t
    half_heads = 128 // HEAD
    lane_head = lax.broadcasted_iota(jnp.int32, (steps, 128), 1) // HEAD
    for s in range(sensors):
        here = slice(s * steps, (s + 1) * steps)
        spread = jnp.concatenate([q_s[here, :]] * H, axis=0) * mask
        scores = dot_nt(k_s[here, :], spread)
        scores = jnp.where(causal, scores, NEG)
        top = jnp.max(scores, axis=0, keepdims=True)
        e = jnp.exp2((scores - top) * SCALE)
        attn = (e * (1.0 / jnp.sum(e, axis=0, keepdims=True))).astype(BF16)
        for half in range(width // 128):
            cols = slice(half * 128, (half + 1) * 128)
            span = half_heads * steps
            wide = dot_tn(attn[:, half * span : (half + 1) * span], v_s[here, cols])
            ctx = wide[:steps]
            for h in range(1, half_heads):
                ctx = jnp.where(lane_head == h, wide[h * steps : (h + 1) * steps], ctx)
            c_s[here, cols] = ctx.astype(BF16)
    after = (x + dot(c_s[...], wo_ref[...])).astype(BF16)
    if not split:
        out_ref[...] = after.reshape(sensors, steps, width)
        return
    after_s[...] = after.reshape(sensors, steps, width)
    order = swap16()
    mine = my_ref[0]
    for ref, part in ((keep_ref, mine), (send_ref, 1 - mine)):
        rows16 = after_s[:, pl.ds(pl.multiple_of(part * 16, 16), 16), :]
        for b in range(sensors // 16):
            block = rows16[b * 16 : (b + 1) * 16].reshape(256, width)
            ref[:, b * 16 : (b + 1) * 16, :] = dot(order, block).astype(BF16).reshape(16, 16, width)


def time_block(tokens, my, gain, wq, wkv, wo, first, count, split):
    steps, width = tokens.shape[1:]
    sb = min(16, count)
    rows = sb * steps
    full = lambda a: pl.BlockSpec(a.shape, lambda i, *_: (0,) * a.ndim)
    if split:
        out_shape = [jax.ShapeDtypeStruct((16, count, width), BF16)] * 2
        out_specs = [pl.BlockSpec((16, sb, width), lambda i, *_: (0, i, 0))] * 2
        extra = [pltpu.VMEM((sb, steps, width), BF16)]
    else:
        out_shape = jax.ShapeDtypeStruct((count, steps, width), BF16)
        out_specs = pl.BlockSpec((sb, steps, width), lambda i, *_: (i, 0, 0))
        extra = []
    return pl.pallas_call(
        functools.partial(time_kernel, split),
        out_shape=out_shape,
        grid_spec=pltpu.PrefetchScalarGridSpec(
            num_scalar_prefetch=1,
            grid=(count // sb,),
            in_specs=[
                pl.BlockSpec((sb, steps, width), lambda i, *_: (first // sb + i, 0, 0)),
                full(gain),
                full(wq),
                full(wkv),
                full(wo),
            ],
            out_specs=out_specs,
            scratch_shapes=[pltpu.VMEM((rows, width), BF16)] * 4 + extra,
        ),
        compiler_params=pltpu.CompilerParams(vmem_limit_bytes=VMEM_LIMIT),
        cost_estimate=pl.CostEstimate(
            flops=count * steps * width * width * 12, bytes_accessed=count * steps * width * 4, transcendentals=0
        ),
        name="time_block",
    )(my, tokens, gain, wq, wkv, wo)


def pick_kernel(n, pick_ref, *refs):
    pieces, (out_ref, o_s) = refs[:n], refs[n:]
    steps = out_ref.shape[1]
    wanted = out_ref.shape[0]
    order = swap16()
    pick = pick_ref[...]
    for t in range(steps):
        rows = jnp.concatenate([p[t] for p in pieces], axis=0)
        o_s[t] = dot(pick, rows).astype(BF16)
    for b in range(wanted // 16):
        block = o_s[:, b * 16 : (b + 1) * 16, :].reshape(256, 256)
        out_ref[b * 16 : (b + 1) * 16] = dot(order, block).astype(BF16).reshape(16, 16, 256)


def pick_rows(pick, pieces):
    steps, _, width = pieces[0].shape
    wanted = pick.shape[0]
    return pl.pallas_call(
        functools.partial(pick_kernel, len(pieces)),
        out_shape=jax.ShapeDtypeStruct((wanted, steps, width), BF16),
        scratch_shapes=[pltpu.VMEM((steps, wanted, width), BF16)],
        compiler_params=pltpu.CompilerParams(vmem_limit_bytes=VMEM_LIMIT),
        name="pick_rows",
    )(pick, *pieces)


def local_kernel(n, *refs):
    pieces = refs[:n]
    gain_ref, wq_ref, wkv_ref, q_ref, ctx_ref, top_ref, sum_ref, wvt_ref = refs[n:]
    tb, block, width = q_ref.shape

    @pl.when(pl.program_id(0) == 0)
    def _():
        wvt_ref[...] = wkv_ref[:, width:].astype(F32).T.astype(BF16)

    x = jnp.concatenate([p[t] for t in range(tb) for p in pieces], axis=0).astype(F32)
    normed = rms(x, gain_ref[...])
    q = dot(normed, wq_ref[...]).astype(BF16)
    k = dot(normed, wkv_ref[:, :width]).astype(BF16)
    q_ref[...] = q.reshape(tb, block, width)
    masks = [head_rows(2 * block, 128, block, -2 * p) for p in range(2)]
    for t in range(tb):
        here = slice(t * block, (t + 1) * block)
        vt = dot_nt(wvt_ref[...], normed[here]).astype(BF16)
        for pair in range(H // 2):
            cols = slice(pair // 2 * 128, pair // 2 * 128 + 128)
            qh = q[here, cols]
            spread = jnp.concatenate([qh, qh], axis=0) * masks[pair % 2]
            scores = dot_nt(k[here, cols], spread)
            top = jnp.max(scores, axis=0, keepdims=True)
            e = jnp.exp2((scores - top) * SCALE)
            total = jnp.sum(e, axis=0, keepdims=True)
            lo = pair * 2 * HEAD
            both = dot(vt[lo : lo + 2 * HEAD], e.astype(BF16))
            for i in range(2):
                lanes = slice(i * block, (i + 1) * block)
                ctx_ref[t, lo + i * HEAD : lo + (i + 1) * HEAD, :] = both[i * HEAD : (i + 1) * HEAD, lanes]
                top_ref[t, 2 * pair + i : 2 * pair + i + 1, :] = top[:, lanes]
                sum_ref[t, 2 * pair + i : 2 * pair + i + 1, :] = total[:, lanes]


def local_part(pieces, gain, wq, wkv):
    steps, _, width = pieces[0].shape
    block = sum(p.shape[1] for p in pieces)
    tb = 2
    full = lambda a: pl.BlockSpec(a.shape, lambda i: (0,) * a.ndim)
    per_t = lambda *shape: pl.BlockSpec((tb,) + shape, lambda i: (i, 0, 0))
    return pl.pallas_call(
        functools.partial(local_kernel, len(pieces)),
        out_shape=[
            jax.ShapeDtypeStruct((steps, block, width), BF16),
            jax.ShapeDtypeStruct((steps, width, block), F32),
            jax.ShapeDtypeStruct((steps, H, block), F32),
            jax.ShapeDtypeStruct((steps, H, block), F32),
            jax.ShapeDtypeStruct((width, width), BF16),
        ],
        grid=(steps // tb,),
        in_specs=[per_t(p.shape[1], width) for p in pieces] + [full(gain), full(wq), full(wkv)],
        out_specs=[
            per_t(block, width),
            per_t(width, block),
            per_t(H, block),
            per_t(H, block),
            pl.BlockSpec((width, width), lambda i: (0, 0)),
        ],
        compiler_params=pltpu.CompilerParams(vmem_limit_bytes=VMEM_LIMIT),
        cost_estimate=pl.CostEstimate(
            flops=steps * block * width * width * 12, bytes_accessed=steps * block * width * 10, transcendentals=0
        ),
        name="local_keys",
    )(*pieces, gain, wq, wkv)


def gelu(x):
    inner = x * (0.7978845608028654 + 0.035677408136300125 * (x * x))
    half = 0.5 * x
    return half + half * jnp.tanh(inner)


def finish_kernel(n, split, own_ref, *refs):
    pieces = refs[:n]
    (in_ref, live_ref, q_ref, lctx_ref, ltop_ref, lsum_ref, gain_ref, wk_ref, wvt_ref, wo_ref, gain_ffn_ref,
     w_in_ref, w_out_ref, out_ref, rn_s, rk_s, ctx_s, y_s, pick_s) = refs[n:]
    tb, block, width = q_ref.shape
    steps, remote = rn_s.shape[:2]
    step = pl.program_id(0)

    @pl.when(step == 0)
    def _():
        if split:
            order = swap16()
            for j in range(remote // REMOTE_SENSORS):
                pick_s[j * REMOTE_SENSORS : (j + 1) * REMOTE_SENSORS] = in_ref[own_ref[j]]
            for b in range(remote // 16):
                rows = pick_s[b * 16 : (b + 1) * 16].reshape(256, width)
                rn_s[:, b * 16 : (b + 1) * 16, :] = dot(order, rows).astype(BF16).reshape(16, 16, width)
            raw = rn_s[...]
        else:
            raw = in_ref[...]
        normed = rms(raw.reshape(steps * remote, width).astype(F32), gain_ref[...])
        rn_s[...] = normed.reshape(steps, remote, width)
        rk_s[...] = dot(normed, wk_ref[...]).astype(BF16).reshape(steps, remote, width)

    live = live_ref[...] > 0
    masks = [head_rows(2 * block, 128, block, -2 * p) for p in range(2)]
    rows = []
    for t in range(tb):
        at = step * tb + t
        rk = rk_s[at]
        vt = dot_nt(wvt_ref[...], rn_s[at]).astype(BF16)
        for pair in range(H // 2):
            cols = slice(pair // 2 * 128, pair // 2 * 128 + 128)
            qh = q_ref[t, :, cols]
            spread = jnp.concatenate([qh, qh], axis=0) * masks[pair % 2]
            scores = jnp.where(live, dot_nt(rk[:, cols], spread), NEG)
            pick = lambda ref: jnp.concatenate(
                [ref[t, 2 * pair : 2 * pair + 1, :], ref[t, 2 * pair + 1 : 2 * pair + 2, :]], axis=1
            )
            ltop = pick(ltop_ref)
            top = jnp.maximum(jnp.max(scores, axis=0, keepdims=True), ltop)
            e = jnp.exp2((scores - top) * SCALE)
            keep = jnp.exp2((ltop - top) * SCALE)
            inverse = 1.0 / (jnp.sum(e, axis=0, keepdims=True) + pick(lsum_ref) * keep)
            keep = keep * inverse
            lo = pair * 2 * HEAD
            both = dot(vt[lo : lo + 2 * HEAD], (e * inverse).astype(BF16))
            for i in range(2):
                lanes = slice(i * block, (i + 1) * block)
                dims = slice(lo + i * HEAD, lo + (i + 1) * HEAD)
                merged = lctx_ref[t, dims, :] * keep[:, lanes] + both[i * HEAD : (i + 1) * HEAD, lanes]
                ctx_s[dims, t * block : (t + 1) * block] = merged.astype(BF16)
        rows += [p[t] for p in pieces]
    after = jnp.concatenate(rows, axis=0).astype(F32) + dot_tn(ctx_s[...], wo_ref[...])
    normed = rms(after, gain_ffn_ref[...])
    hidden = gelu(dot(normed, w_in_ref[...])).astype(BF16)
    y = (after + dot(hidden, w_out_ref[...])).astype(BF16).reshape(tb, block, width)
    if not split:
        out_ref[...] = y
        return
    y_s[pl.ds(step * tb, tb)] = y

    @pl.when(step == pl.num_programs(0) - 1)
    def _():
        order = swap16()
        mine = own_ref[own_ref.shape[0] - 1]
        half = block // 2
        for b in range(block // 16):
            first = b * 16
            owner = mine if first < half else 1 - mine
            rows = y_s[:, first : first + 16, :].reshape(256, width)
            at = owner * half + first % half
            out_ref[pl.ds(at, 16)] = dot(order, rows).astype(BF16).reshape(16, 16, width)


def finish(own, pieces, incoming, live, local, gain, wkv, wo, gain_ffn, w_in, w_out, split):
    q, lctx, ltop, lsum, wvt = local
    steps, block, width = q.shape
    remote = live.shape[0]
    tb = 2
    full = lambda a: pl.BlockSpec(a.shape, lambda i, *_: (0,) * a.ndim)
    per_t = lambda *shape: pl.BlockSpec((tb,) + shape, lambda i, *_: (i, 0, 0))
    if split:
        out_shape = jax.ShapeDtypeStruct((block, steps, width), BF16)
        out_specs = pl.BlockSpec((block, steps, width), lambda i, *_: (0, 0, 0))
    else:
        out_shape = jax.ShapeDtypeStruct((steps, block, width), BF16)
        out_specs = per_t(block, width)
    return pl.pallas_call(
        functools.partial(finish_kernel, len(pieces), split),
        out_shape=out_shape,
        grid_spec=pltpu.PrefetchScalarGridSpec(
            num_scalar_prefetch=1,
            grid=(steps // tb,),
            in_specs=[per_t(p.shape[1], width) for p in pieces]
            + [
                full(incoming),
                full(live),
                per_t(block, width),
                per_t(width, block),
                per_t(H, block),
                per_t(H, block),
                full(gain),
                pl.BlockSpec((width, width), lambda i, *_: (0, 0)),
                full(wvt),
                full(wo),
                full(gain_ffn),
                full(w_in),
                full(w_out),
            ],
            out_specs=out_specs,
            scratch_shapes=[
                pltpu.VMEM((steps, remote, width), BF16),
                pltpu.VMEM((steps, remote, width), BF16),
                pltpu.VMEM((width, tb * block), BF16),
                pltpu.VMEM((steps, block, width), BF16),
                pltpu.VMEM((remote, steps, width), BF16),
            ],
        ),
        compiler_params=pltpu.CompilerParams(vmem_limit_bytes=VMEM_LIMIT),
        cost_estimate=pl.CostEstimate(
            flops=steps * block * width * width * 18, bytes_accessed=steps * block * width * 12, transcendentals=0
        ),
        name="remote_keys_and_feed_forward",
    )(own, *pieces, incoming, live, q, lctx, ltop, lsum, gain, wkv, wvt, wo, gain_ffn, w_in, w_out)


def local(
    tm,
    tokens,
    gain_time,
    wq_time,
    wkv_time,
    wo_time,
    gain_graph,
    wq_graph,
    wkv_graph,
    wo_graph,
    gain_ffn,
    w_in,
    w_out,
    neighbour_blocks,
    slot_used_mask,
    neighbour_rows,
):
    sensors_here, steps, width = tokens.shape
    block = sensors_here * tm
    group = steps // tm
    block_count, slots = neighbour_blocks.shape
    split = tm == 2 and group == 16 and sensors_here % 32 == 0
    gain_time, gain_graph, gain_ffn = (g.reshape(1, width) for g in (gain_time, gain_graph, gain_ffn))
    mine = lax.axis_index("tm").astype(jnp.int32)
    block_index = lax.axis_index("sensor")
    time = functools.partial(time_block, tokens, mine.reshape(1), gain_time, wq_time, wkv_time, wo_time)
    if split:
        chunks = 2
        size = sensors_here // chunks
        kept, got = [], []
        for c in range(chunks):
            keep, send = time(c * size, size, True)
            kept.append(keep)
            got.append(lax.ppermute(send, "tm", [(0, 1), (1, 0)]))
        pieces = kept + got
    else:
        whole = lax.all_to_all(time(0, sensors_here, False), "tm", split_axis=1, concat_axis=0, tiled=True)
        pieces = [whole.transpose(1, 0, 2)]
    matches = (neighbour_blocks == block_index).astype(jnp.int32)
    wanted = jnp.sum(matches[:, :, None] * neighbour_rows, axis=1).reshape(-1)
    own = lax.dynamic_index_in_dim(neighbour_blocks, block_index, 0, keepdims=False)
    live = jnp.broadcast_to(jnp.repeat(slot_used_mask[0], REMOTE_SENSORS)[:, None], (slots * REMOTE_SENSORS, 2 * block))
    if split:
        place = (jnp.arange(block) + mine * sensors_here) % block
        pick = (wanted[:, None] == place[None, :]).astype(BF16)
        outgoing = pick_rows(pick, pieces)
    else:
        outgoing = jnp.take(whole, wanted, axis=0)
    outgoing = outgoing.reshape(block_count, REMOTE_SENSORS, group, width)
    incoming = lax.all_to_all(outgoing, "sensor", split_axis=0, concat_axis=0, tiled=True)
    if not split:
        incoming = jnp.take(incoming, own, axis=0).reshape(-1, group, width).transpose(1, 0, 2)
    near = local_part(pieces, gain_graph, wq_graph, wkv_graph)
    numbers = jnp.concatenate([own.astype(jnp.int32), mine.reshape(1)])
    out = finish(numbers, pieces, incoming, live, near, gain_graph, wkv_graph, wo_graph, gain_ffn, w_in, w_out, split)
    return out if split else out.transpose(1, 0, 2)


def solution(mesh):
    in_specs = (
        P(("sensor", "tm"), None, None),
        P(),
        P(),
        P(),
        P(),
        P(),
        P(),
        P(),
        P(),
        P(),
        P(),
        P(),
        P(),
        P("sensor", None),
        P(),
    )
    out_specs = P("sensor", "tm", None)
    body = functools.partial(local, mesh.shape["tm"])
    return jax.shard_map(body, mesh=mesh, in_specs=in_specs, out_specs=out_specs, check_vma=False)
```

time: 202 us -> 82.7 us (0.41); the launches traced: 198 us -> 82.3 us
  matrix products: 78 us -> 0 us
  Pallas kernels: 0 us -> 56.7 us
  local copies, waits for them, and re-layouts: 64.8 us -> 8.82 us
  other arithmetic: 23.8 us -> 0.18 us
  waiting for transfers between devices: 20 us -> 7.42 us
    dot_general x41 -> x0, matrix products: 58 us -> none  [the longest x16 18.4 us: one_step(): jnp.einsum('sha,uha->hsu', query_step, key_step, preferred_element_type=j...]
    pallas_call x0 -> x5, Pallas kernels: none -> 56.7 us  [the longest x1 22.4 us: finish(): pl.pallas_call(functools.partial(finish_kernel, len(pieces), split), out_...]
    sub x16 -> x0, matrix products: 20 us -> none  [softmax_bf16(): exponent = jnp.exp(masked - highest)]
    squeeze x16 -> x0, local copies, waits for them, and re-layouts: 15.5 us -> none  [local(): context_graph = lax.map(one_step, (stepwise_q, stepwise_kv))]
    all_to_all x1 -> x0, waiting for transfers between devices: 14.8 us -> none  [local(): lax.all_to_all(temporal_output, 'tm', split_axis=1, concat_axis=0, tiled=...]
    reshape x4 -> x0, local copies, waits for them, and re-layouts: 12.5 us -> none  [the longest x1 7.7 us: local(): key_val[..., :model_width].reshape(sensors_here, time_len, H, head_size)]
    convert_element_type x5 -> x0, local copies, waits for them, and re-layouts: 8.79 us -> none  [the longest x2 4.1 us: local(): moved.astype(jnp.float32)]
    convert_element_type x5 -> x1, other arithmetic: 8.44 us -> 0.07 us  [local(): pick = (wanted[:, None] == place[None, :]).astype(BF16)]
  transfers between devices with their start and end apart: 2 -> 3, of which waited for: 2 -> 1; matrix products, arithmetic and copies ran while one was open for 9% -> 1% of each run, Pallas kernels for 0% -> 27%
where the time goes in v1:
time: 82.7 us; the launch traced here: 82.3 us
  Pallas kernels  56.7 us (69%)
  starting transfers between devices  9.05 us (11%)
  local copies, waits for them, and re-layouts  8.82 us (11%)
  waiting for transfers between devices  7.42 us (9%)
    pallas_call x1, Pallas kernels, finish(): pl.pallas_call(functools.partial(finish_kernel, len(pieces), split), out_...  22.4 us
    pallas_call x2, Pallas kernels, time_block(): pl.pallas_call(functools.partial(time_kernel, split), out_shape=out_shape...  21.2 us
    pallas_call x1, Pallas kernels, local_part(): pl.pallas_call(functools.partial(local_kernel, len(pieces)), out_shape=[j...  11.8 us
    unnamed x38, local copies, waits for them, and re-layouts  8.25 us
    ppermute x2, waiting for transfers between devices, local(): got.append(lax.ppermute(send, 'tm', [(0, 1), (1, 0)]))  7.41 us
    all_to_all x1, starting transfers between devices, local(): lax.all_to_all(outgoing, 'sensor', split_axis=0, concat_axis=0, tiled=True)  5.94 us
    ppermute x2, starting transfers between devices, local(): got.append(lax.ppermute(send, 'tm', [(0, 1), (1, 0)]))  3.11 us
  transfers between devices with their start and end apart: 3, of which 1 were waited for; matrix products, arithmetic and copies ran while one was open for 1% of the time, Pallas kernels for 27%

profile of v1, /device:TPU:0, one launch (start us, length us, event | category | flops | bytes accessed | tf_op | source)
XLA Modules:
  0.0 82.3 jit_solution(10098391986081660186)
XLA Ops:
  0.0 1.2 %copy-done = bf16[64,32,256]{2,1,0:T(8,128)(2,1)S(1)} copy-done((bf16[64,32,256]{2,1,0:T(8,128)(2,1)S(1)}, bf16[64,32,256]{2,1,0:T(8,128)(2,1)}, u32[]{:S(2)}) %copy-start) | copy-done | bytes 1048600
  1.2 0.9 %copy-done.3 = bf16[256,512]{1,0:T(8,128)(2,1)S(1)} copy-done((bf16[256,512]{1,0:T(8,128)(2,1)S(1)}, bf16[256,512]{1,0:T(8,128)(2,1)}, u32[]{:S(2)}) %copy-start.3) | copy-done | bytes 262168
  2.2 0.9 %copy-done.5 = bf16[256,256]{1,0:T(8,128)(2,1)S(1)} copy-done((bf16[256,256]{1,0:T(8,128)(2,1)S(1)}, bf16[256,256]{1,0:T(8,128)(2,1)}, u32[]{:S(2)}) %copy-start.5) | copy-done | bytes 131096
  3.1 0.9 %copy-done.6 = bf16[256,256]{1,0:T(8,128)(2,1)S(1)} copy-done((bf16[256,256]{1,0:T(8,128)(2,1)S(1)}, bf16[256,256]{1,0:T(8,128)(2,1)}, u32[]{:S(2)}) %copy-start.6) | copy-done | bytes 131096
  4.0 0.7 copy-done.10
  4.7 10.6 %time_block.3 = (bf16[16,32,256]{2,1,0:T(8,128)(2,1)S(1)}, bf16[16,32,256]{2,1,0:T(8,128)(2,1)S(1)}) custom-call(s32[1]{0:T(128)} %bitcast.my_ref, bf16[64,32,256]{2,1,0:T(8,128)(2,1)S(1)} %copy-done, f32[1,256]{1,0:T(1,128)S(1)} %bitcast.6, bf16[256,256]{1,0:T(8,128)(2,1)S(1)} %copy-done.5, bf16[256,512]{1,0:T(8,128)(2,1)S(1)} %copy-done.3, ...), custom_call_target="tpu_custom_call" | custom-call | flops 805306368 | bytes 1048576 | tf_op jit(solution)/shard_map/time_block/pallas_call | solution.py:114
  15.3 0.0 copy-start.16
  15.3 0.0 copy-start.17
  15.3 3.0 %collective-permute-start.1 = (bf16[16,32,256]{2,1,0:T(8,128)(2,1)S(1)}, bf16[16,32,256]{2,1,0:T(8,128)(2,1)S(1)}, u32[]{:S(2)}, u32[]{:S(2)}) collective-permute-start(bf16[16,32,256]{2,1,0:T(8,128)(2,1)S(1)} %get-tuple-element.17), channel_id=1, source_target_pairs={{0,1},{1,0},{2,3},{3,2},{4,5},{5,4},{6,7},{7,6},{8,9},{9,8},{10,11... | collective-permute-start | bytes 786440 | tf_op jit(solution)/shard_map/ppermute | solution.py:398
  18.3 0.0 copy-done.7
  18.3 10.6 %time_block.2 = (bf16[16,32,256]{2,1,0:T(8,128)(2,1)S(1)}, bf16[16,32,256]{2,1,0:T(8,128)(2,1)S(1)}) custom-call(s32[1]{0:T(128)} %bitcast.my_ref, bf16[64,32,256]{2,1,0:T(8,128)(2,1)S(1)} %copy-done, f32[1,256]{1,0:T(1,128)S(1)} %bitcast.7, bf16[256,256]{1,0:T(8,128)(2,1)S(1)} %copy-done.5, bf16[256,512]{1,0:T(8,128)(2,1)S(1)} %copy-done.3, ...), custom_call_target="tpu_custom_call" | custom-call | flops 805306368 | bytes 1048576 | tf_op jit(solution)/shard_map/time_block/pallas_call | solution.py:114
  28.9 0.0 copy-start.18
  28.9 0.0 copy-start.4
  28.9 0.0 copy-start.8
  28.9 0.0 copy-start.11
  29.0 0.1 collective-permute-start
  29.1 0.0 copy-done.16
  29.1 0.0 copy-done.17
  29.1 0.1 copy.16
  29.2 0.1 eq.25
  29.3 0.1 compare_convert_fusion.pick_ref
  29.4 0.0 collective-permute-done.1.refs_3_
  29.4 7.4 %collective-permute-done.refs_2_ = bf16[16,32,256]{2,1,0:T(8,128)(2,1)S(1)} collective-permute-done((bf16[16,32,256]{2,1,0:T(8,128)(2,1)S(1)}, bf16[16,32,256]{2,1,0:T(8,128)(2,1)S(1)}, u32[]{:S(2)}, u32[]{:S(2)}) %collective-permute-start) | collective-permute-done | bytes 262176 | tf_op jit(solution)/shard_map/ppermute | solution.py:398
  36.8 1.4 %pick_rows.1 = bf16[64,16,256]{2,1,0:T(8,128)(2,1)} custom-call(bf16[64,128]{1,0:T(8,128)(2,1)S(1)} %compare_convert_fusion.pick_ref, bf16[16,32,256]{2,1,0:T(8,128)(2,1)S(1)} %get-tuple-element.14.refs_0_, bf16[16,32,256]{2,1,0:T(8,128)(2,1)S(1)} %get-tuple-element.15.refs_1_, bf16[16,32,256]{2,1,0:T(8,128)(2,1)S(1)} %collective-permute-done.refs_2_, ...), custom_call_target="tpu_custom_call" | custom-call | tf_op jit(solution)/shard_map/pick_rows/pallas_call | solution.py:155
  38.1 5.9 %all-to-all-start = ((bf16[16,4,16,256]{3,2,1,0:T(8,128)(2,1)}), bf16[16,4,16,256]{3,2,1,0:T(8,128)(2,1)S(1)}, u32[]{:S(2)}, u32[]{:S(2)}) async-start(bf16[16,4,16,256]{3,2,1,0:T(8,128)(2,1)} %bitcast.2), calls=%async_computation | async-start | bytes 1048576 | tf_op jit(solution)/shard_map/all_to_all | solution.py:414
  44.1 0.2 dynamic-slice_reduce_fusion
  44.3 0.0 copy-done.18
  44.3 0.1 broadcast_in_dim.12
  44.3 0.1 broadcast_in_dim.13
  44.4 0.1 pad_add_fusion.own_ref
  44.5 0.0 copy-done.4
  44.5 0.0 copy-done.8
  44.5 0.0 copy-done.11
  44.5 0.0 copy-start.1
  44.5 0.0 copy-start.2
  44.5 0.0 copy-start.9
  44.5 0.0 copy-start.12
  44.6 11.8 %local_keys.1 = (bf16[16,128,256]{2,1,0:T(8,128)(2,1)S(1)}, f32[16,256,128]{2,1,0:T(8,128)S(1)}, f32[16,8,128]{2,1,0:T(8,128)S(1)}, f32[16,8,128]{2,1,0:T(8,128)S(1)}, bf16[256,256]{1,0:T(8,128)(2,1)S(1)}) custom-call(bf16[16,32,256]{2,1,0:T(8,128)(2,1)S(1)} %get-tuple-element.14.refs_0_, bf16[16,32,256]{2,1,0:T(8,128)(2,1)S(1)} %get-tuple-element.15.refs_1_, ...), custom_call_target="tpu_custom_call" | custom-call | flops 1610612736 | bytes 5242880 | tf_op jit(solution)/shard_map/local_keys/pallas_call | solution.py:205
  56.3 0.0 copy-start.13
  56.4 1.3 %copy-done.13 = f32[16,256,128]{2,1,0:T(8,128)} copy-done((f32[16,256,128]{2,1,0:T(8,128)}, f32[16,256,128]{2,1,0:T(8,128)S(1)}, u32[]{:S(2)}) %copy-start.13) | copy-done | bytes 2097176
  57.7 1.0 %copy-done.14 = bf16[16,128,256]{2,1,0:T(8,128)(2,1)} copy-done((bf16[16,128,256]{2,1,0:T(8,128)(2,1)}, bf16[16,128,256]{2,1,0:T(8,128)(2,1)S(1)}, u32[]{:S(2)}) %copy-start.14) | copy-done | bytes 1048600
  58.7 0.0 all-to-all-done.refs_4_
  58.7 0.1 broadcast_in_dim.14.refs_5_
  58.7 0.0 copy-done.1
  58.7 0.0 copy-done.9
  58.8 0.0 copy-start.15
  58.8 1.2 %copy-done.15 = bf16[16,128,256]{2,1,0:T(8,128)(2,1)S(1)} copy-done((bf16[16,128,256]{2,1,0:T(8,128)(2,1)S(1)}, bf16[16,128,256]{2,1,0:T(8,128)(2,1)}, u32[]{:S(2)}) %copy-start.15) | copy-done | bytes 1048600
  60.0 22.4 %remote_keys_and_feed_forward.1 = bf16[128,16,256]{2,1,0:T(8,128)(2,1)} custom-call(s32[9]{0:T(128)S(1)} %pad_add_fusion.own_ref, bf16[16,32,256]{2,1,0:T(8,128)(2,1)S(1)} %get-tuple-element.14.refs_0_, bf16[16,32,256]{2,1,0:T(8,128)(2,1)S(1)} %get-tuple-element.15.refs_1_, bf16[16,32,256]{2,1,0:T(8,128)(2,1)S(1)} %collective-permute-done.refs_2_, ...), custom_call_target="tpu_custom_call" | custom-call | flops 2415919104 | bytes 6291456 | tf_op jit(solution)/shard_map/remote_keys_and_feed_forward/pallas_call | solution.py:325
  (12 shorter events, 0.1 us)
Async XLA Ops:
  0.0 1.2 %copy-start = (bf16[64,32,256]{2,1,0:T(8,128)(2,1)S(1)}, bf16[64,32,256]{2,1,0:T(8,128)(2,1)}, u32[]{:S(2)}) copy-start(bf16[64,32,256]{2,1,0:T(8,128)(2,1)} %x_ref.3) | copy-start | bytes 3145732
  1.2 0.9 %copy-start.3 = (bf16[256,512]{1,0:T(8,128)(2,1)S(1)}, bf16[256,512]{1,0:T(8,128)(2,1)}, u32[]{:S(2)}) copy-start(bf16[256,512]{1,0:T(8,128)(2,1)} %wkv_ref.3) | copy-start | bytes 786436
  2.2 0.9 %copy-start.5 = (bf16[256,256]{1,0:T(8,128)(2,1)S(1)}, bf16[256,256]{1,0:T(8,128)(2,1)}, u32[]{:S(2)}) copy-start(bf16[256,256]{1,0:T(8,128)(2,1)} %wq_ref.3) | copy-start | bytes 393220
  3.1 0.9 %copy-start.6 = (bf16[256,256]{1,0:T(8,128)(2,1)S(1)}, bf16[256,256]{1,0:T(8,128)(2,1)}, u32[]{:S(2)}) copy-start(bf16[256,256]{1,0:T(8,128)(2,1)} %wo_ref.3) | copy-start | bytes 393220
  4.0 0.7 copy-start.10
  4.7 13.6 %copy-start.7 = (bf16[256,256]{1,0:T(8,128)(2,1)S(1)}, bf16[256,256]{1,0:T(8,128)(2,1)}, u32[]{:S(2)}) copy-start(bf16[256,256]{1,0:T(8,128)(2,1)} %wo_ref.3) | copy-start | bytes 393220
  15.3 13.8 %copy-start.16 = (s32[16,8]{0,1:T(8,128)S(1)}, s32[16,8]{0,1:T(8,128)}, u32[]{:S(2)}) copy-start(s32[16,8]{0,1:T(8,128)} %param.27) | copy-start | bytes 1540
  15.3 13.8 %copy-start.17 = (s32[16,8,4]{0,2,1:T(4,128)S(1)}, s32[16,8,4]{0,2,1:T(4,128)}, u32[]{:S(2)}) copy-start(s32[16,8,4]{0,2,1:T(4,128)} %param.29) | copy-start | bytes 6148
  15.3 14.1 %collective-permute-start.1 = (bf16[16,32,256]{2,1,0:T(8,128)(2,1)S(1)}, bf16[16,32,256]{2,1,0:T(8,128)(2,1)S(1)}, u32[]{:S(2)}, u32[]{:S(2)}) collective-permute-start(bf16[16,32,256]{2,1,0:T(8,128)(2,1)S(1)} %get-tuple-element.17), channel_id=1, source_target_pairs={{0,1},{1,0},{2,3},{3,2},{4,5},{5,4},{6,7},{7,6},{8,9},{9,8},{10,11... | collective-permute-start | bytes 786440 | tf_op jit(solution)/shard_map/ppermute | solution.py:398
  28.9 15.4 %copy-start.18 = (s32[1,8]{1,0:T(1,128)S(1)}, s32[1,8]{1,0:T(1,128)}, u32[]{:S(2)}) copy-start(s32[1,8]{1,0:T(1,128)} %param.28) | copy-start | bytes 100
  28.9 15.6 %copy-start.4 = (bf16[256,512]{1,0:T(8,128)(2,1)S(1)}, bf16[256,512]{1,0:T(8,128)(2,1)}, u32[]{:S(2)}) copy-start(bf16[256,512]{1,0:T(8,128)(2,1)} %refs_11_.1) | copy-start | bytes 786436
  28.9 15.6 %copy-start.8 = (bf16[256,256]{1,0:T(8,128)(2,1)S(1)}, bf16[256,256]{1,0:T(8,128)(2,1)}, u32[]{:S(2)}) copy-start(bf16[256,256]{1,0:T(8,128)(2,1)} %refs_5_.1) | copy-start | bytes 393220
  28.9 15.6 %copy-start.11 = (f32[256]{0:T(256)S(1)}, f32[256]{0:T(256)}, u32[]{:S(2)}) copy-start(f32[256]{0:T(256)} %param.20) | copy-start | bytes 3076
  29.0 7.8 %collective-permute-start = (bf16[16,32,256]{2,1,0:T(8,128)(2,1)S(1)}, bf16[16,32,256]{2,1,0:T(8,128)(2,1)S(1)}, u32[]{:S(2)}, u32[]{:S(2)}) collective-permute-start(bf16[16,32,256]{2,1,0:T(8,128)(2,1)S(1)} %get-tuple-element.16), channel_id=1, source_target_pairs={{0,1},{1,0},{2,3},{3,2},{4,5},{5,4},{6,7},{7,6},{8,9},{9,8},{10,11... | collective-permute-start | bytes 786440 | tf_op jit(solution)/shard_map/ppermute | solution.py:398
  38.1 20.5 %all-to-all-start = ((bf16[16,4,16,256]{3,2,1,0:T(8,128)(2,1)}), bf16[16,4,16,256]{3,2,1,0:T(8,128)(2,1)S(1)}, u32[]{:S(2)}, u32[]{:S(2)}) async-start(bf16[16,4,16,256]{3,2,1,0:T(8,128)(2,1)} %bitcast.2), calls=%async_computation | async-start | bytes 1048576 | tf_op jit(solution)/shard_map/all_to_all | solution.py:414
  44.5 14.2 %copy-start.1 = (bf16[256,1024]{1,0:T(8,128)(2,1)S(1)}, bf16[256,1024]{1,0:T(8,128)(2,1)}, u32[]{:S(2)}) copy-start(bf16[256,1024]{1,0:T(8,128)(2,1)} %refs_15_.1) | copy-start | bytes 1572868
  44.5 14.2 %copy-start.2 = (bf16[1024,256]{1,0:T(8,128)(2,1)S(1)}, bf16[1024,256]{1,0:T(8,128)(2,1)}, u32[]{:S(2)}) copy-start(bf16[1024,256]{1,0:T(8,128)(2,1)} %refs_16_.1) | copy-start | bytes 1572868
  44.5 14.2 %copy-start.9 = (bf16[256,256]{1,0:T(8,128)(2,1)S(1)}, bf16[256,256]{1,0:T(8,128)(2,1)}, u32[]{:S(2)}) copy-start(bf16[256,256]{1,0:T(8,128)(2,1)} %refs_13_.1) | copy-start | bytes 393220
  44.5 14.2 %copy-start.12 = (f32[256]{0:T(256)S(1)}, f32[256]{0:T(256)}, u32[]{:S(2)}) copy-start(f32[256]{0:T(256)} %param.24) | copy-start | bytes 3076
  56.3 1.3 %copy-start.13 = (f32[16,256,128]{2,1,0:T(8,128)}, f32[16,256,128]{2,1,0:T(8,128)S(1)}, u32[]{:S(2)}) copy-start(f32[16,256,128]{2,1,0:T(8,128)S(1)} %get-tuple-element.19.refs_7_) | copy-start | bytes 6291460
  57.7 1.0 %copy-start.14 = (bf16[16,128,256]{2,1,0:T(8,128)(2,1)}, bf16[16,128,256]{2,1,0:T(8,128)(2,1)S(1)}, u32[]{:S(2)}) copy-start(bf16[16,128,256]{2,1,0:T(8,128)(2,1)S(1)} %get-tuple-element.18.refs_6_) | copy-start | bytes 3145732
  58.8 1.2 %copy-start.15 = (bf16[16,128,256]{2,1,0:T(8,128)(2,1)S(1)}, bf16[16,128,256]{2,1,0:T(8,128)(2,1)}, u32[]{:S(2)}) copy-start(bf16[16,128,256]{2,1,0:T(8,128)(2,1)} %copy-done.14) | copy-start | bytes 3145732

commit v2 on v1

--- a/solution.py
+++ b/solution.py
@@ -16,7 +16,7 @@
 SCALE = math.log2(math.e) / math.sqrt(HEAD)
 F32 = jnp.float32
 BF16 = jnp.bfloat16
-VMEM_LIMIT = 48 * 1024 * 1024
+VMEM_LIMIT = 60 * 1024 * 1024
 
 
 def dot(a, b):
@@ -50,9 +50,9 @@
 
 def time_kernel(split, my_ref, x_ref, gain_ref, wq_ref, wkv_ref, wo_ref, *refs):
     if split:
-        keep_ref, send_ref, q_s, k_s, v_s, c_s, after_s = refs
+        keep_ref, send_ref, q_s, k_s, v_s, a_s, c_s, after_s = refs
     else:
-        out_ref, q_s, k_s, v_s, c_s = refs
+        out_ref, q_s, k_s, v_s, a_s, c_s = refs
     sensors, steps, width = x_ref.shape
     rows = sensors * steps
     x = x_ref[...].reshape(rows, width).astype(F32)
@@ -62,28 +62,41 @@
     k_s[...] = kv[:, :width]
     v_s[...] = kv[:, width:]
     lanes = H * steps
-    mask = head_rows(lanes, width, steps, 0)
+    near = 128 // HEAD
+    span = near * steps
+    mask = head_rows(span, 128, steps, 0)
+    none = jnp.zeros((span, 128), BF16)
     key_t = lax.broadcasted_iota(jnp.int32, (steps, lanes), 0)
     query_t = lax.broadcasted_iota(jnp.int32, (steps, lanes), 1) & (steps - 1)
     causal = key_t <= query_t
-    half_heads = 128 // HEAD
-    lane_head = lax.broadcasted_iota(jnp.int32, (steps, 128), 1) // HEAD
     for s in range(sensors):
         here = slice(s * steps, (s + 1) * steps)
-        spread = jnp.concatenate([q_s[here, :]] * H, axis=0) * mask
-        scores = dot_nt(k_s[here, :], spread)
-        scores = jnp.where(causal, scores, NEG)
+        first, second = (jnp.concatenate([q_s[here, c : c + 128]] * near, axis=0) * mask for c in (0, 128))
+        spread = jnp.concatenate(
+            [jnp.concatenate([first, none], axis=1), jnp.concatenate([none, second], axis=1)], axis=0
+        )
+        scores = jnp.where(causal, dot_nt(k_s[here, :], spread), NEG)
         top = jnp.max(scores, axis=0, keepdims=True)
         e = jnp.exp2((scores - top) * SCALE)
-        attn = (e * (1.0 / jnp.sum(e, axis=0, keepdims=True))).astype(BF16)
-        for half in range(width // 128):
+        a_s[here, :] = (e * (1.0 / jnp.sum(e, axis=0, keepdims=True))).astype(BF16)
+    lane_head = lax.broadcasted_iota(jnp.int32, (steps, 128), 1) // HEAD
+    for g in range(rows // 128):
+        turned = a_s[g * 128 : (g + 1) * 128, :].T
+        for half in range(2):
             cols = slice(half * 128, (half + 1) * 128)
-            span = half_heads * steps
-            wide = dot_tn(attn[:, half * span : (half + 1) * span], v_s[here, cols])
-            ctx = wide[:steps]
-            for h in range(1, half_heads):
-                ctx = jnp.where(lane_head == h, wide[h * steps : (h + 1) * steps], ctx)
-            c_s[here, cols] = ctx.astype(BF16)
+            for s in range(0, 128 // steps, 2):
+                columns = []
+                for r in (s, s + 1):
+                    v = v_s[g * 128 + r * steps : g * 128 + (r + 1) * steps, cols]
+                    parts = [jnp.zeros((r * steps, 128), BF16), v, jnp.zeros((128 - (r + 1) * steps, 128), BF16)]
+                    columns.append(jnp.concatenate([p for p in parts if p.shape[0]], axis=0))
+                wide = dot(turned[half * span : (half + 1) * span], jnp.concatenate(columns, axis=1))
+                for i in range(2):
+                    ctx = wide[:steps, i * 128 : (i + 1) * 128]
+                    for h in range(1, near):
+                        ctx = jnp.where(lane_head == h, wide[h * steps : (h + 1) * steps, i * 128 : (i + 1) * 128], ctx)
+                    at = g * 128 + (s + i) * steps
+                    c_s[at : at + steps, cols] = ctx.astype(BF16)
     after = (x + dot(c_s[...], wo_ref[...])).astype(BF16)
     if not split:
         out_ref[...] = after.reshape(sensors, steps, width)
@@ -125,7 +138,7 @@
                 full(wo),
             ],
             out_specs=out_specs,
-            scratch_shapes=[pltpu.VMEM((rows, width), BF16)] * 4 + extra,
+            scratch_shapes=[pltpu.VMEM((rows, width), BF16)] * 5 + extra,
         ),
         compiler_params=pltpu.CompilerParams(vmem_limit_bytes=VMEM_LIMIT),
         cost_estimate=pl.CostEstimate(
@@ -161,6 +174,12 @@
     )(pick, *pieces)
 
 
+def pair_scores(q, k, masks, pair):
+    cols = slice(pair // 2 * 128, pair // 2 * 128 + 128)
+    spread = jnp.concatenate([q[:, cols]] * 2, axis=0) * masks[pair % 2]
+    return dot_nt(k[:, cols], spread)
+
+
 def local_kernel(n, *refs):
     pieces = refs[:n]
     gain_ref, wq_ref, wkv_ref, q_ref, ctx_ref, top_ref, sum_ref, wvt_ref = refs[n:]
@@ -179,27 +198,23 @@
     for t in range(tb):
         here = slice(t * block, (t + 1) * block)
         vt = dot_nt(wvt_ref[...], normed[here]).astype(BF16)
-        for pair in range(H // 2):
-            cols = slice(pair // 2 * 128, pair // 2 * 128 + 128)
-            qh = q[here, cols]
-            spread = jnp.concatenate([qh, qh], axis=0) * masks[pair % 2]
-            scores = dot_nt(k[here, cols], spread)
-            top = jnp.max(scores, axis=0, keepdims=True)
-            e = jnp.exp2((scores - top) * SCALE)
-            total = jnp.sum(e, axis=0, keepdims=True)
+        scores = [pair_scores(q[here], k[here], masks, pair) for pair in range(H // 2)]
+        tops = [jnp.max(x, axis=0, keepdims=True) for x in scores]
+        es = [jnp.exp2((x - top) * SCALE) for x, top in zip(scores, tops)]
+        top_ref[t] = jnp.concatenate(tops, axis=1)
+        sum_ref[t] = jnp.concatenate([jnp.sum(e, axis=0, keepdims=True) for e in es], axis=1)
+        for pair, e in enumerate(es):
             lo = pair * 2 * HEAD
             both = dot(vt[lo : lo + 2 * HEAD], e.astype(BF16))
             for i in range(2):
                 lanes = slice(i * block, (i + 1) * block)
                 ctx_ref[t, lo + i * HEAD : lo + (i + 1) * HEAD, :] = both[i * HEAD : (i + 1) * HEAD, lanes]
-                top_ref[t, 2 * pair + i : 2 * pair + i + 1, :] = top[:, lanes]
-                sum_ref[t, 2 * pair + i : 2 * pair + i + 1, :] = total[:, lanes]
 
 
 def local_part(pieces, gain, wq, wkv):
     steps, _, width = pieces[0].shape
     block = sum(p.shape[1] for p in pieces)
-    tb = 2
+    tb = 4
     full = lambda a: pl.BlockSpec(a.shape, lambda i: (0,) * a.ndim)
     per_t = lambda *shape: pl.BlockSpec((tb,) + shape, lambda i: (i, 0, 0))
     return pl.pallas_call(
@@ -207,8 +222,8 @@
         out_shape=[
             jax.ShapeDtypeStruct((steps, block, width), BF16),
             jax.ShapeDtypeStruct((steps, width, block), F32),
-            jax.ShapeDtypeStruct((steps, H, block), F32),
-            jax.ShapeDtypeStruct((steps, H, block), F32),
+            jax.ShapeDtypeStruct((steps, 1, H * block), F32),
+            jax.ShapeDtypeStruct((steps, 1, H * block), F32),
             jax.ShapeDtypeStruct((width, width), BF16),
         ],
         grid=(steps // tb,),
@@ -216,8 +231,8 @@
         out_specs=[
             per_t(block, width),
             per_t(width, block),
-            per_t(H, block),
-            per_t(H, block),
+            per_t(1, H * block),
+            per_t(1, H * block),
             pl.BlockSpec((width, width), lambda i: (0, 0)),
         ],
         compiler_params=pltpu.CompilerParams(vmem_limit_bytes=VMEM_LIMIT),
@@ -265,29 +280,28 @@
         at = step * tb + t
         rk = rk_s[at]
         vt = dot_nt(wvt_ref[...], rn_s[at]).astype(BF16)
+        q = q_ref[t]
+        scores = jnp.concatenate([pair_scores(q, rk, masks, pair) for pair in range(H // 2)], axis=1)
+        scores = jnp.where(live, scores, NEG)
+        ltop = ltop_ref[t]
+        top = jnp.maximum(jnp.max(scores, axis=0, keepdims=True), ltop)
+        e = jnp.exp2((scores - top) * SCALE)
+        keep = jnp.exp2((ltop - top) * SCALE)
+        inverse = 1.0 / (jnp.sum(e, axis=0, keepdims=True) + lsum_ref[t] * keep)
+        keep = keep * inverse
+        e = (e * inverse).astype(BF16)
         for pair in range(H // 2):
-            cols = slice(pair // 2 * 128, pair // 2 * 128 + 128)
-            qh = q_ref[t, :, cols]
-            spread = jnp.concatenate([qh, qh], axis=0) * masks[pair % 2]
-            scores = jnp.where(live, dot_nt(rk[:, cols], spread), NEG)
-            pick = lambda ref: jnp.concatenate(
-                [ref[t, 2 * pair : 2 * pair + 1, :], ref[t, 2 * pair + 1 : 2 * pair + 2, :]], axis=1
-            )
-            ltop = pick(ltop_ref)
-            top = jnp.maximum(jnp.max(scores, axis=0, keepdims=True), ltop)
-            e = jnp.exp2((scores - top) * SCALE)
-            keep = jnp.exp2((ltop - top) * SCALE)
-            inverse = 1.0 / (jnp.sum(e, axis=0, keepdims=True) + pick(lsum_ref) * keep)
-            keep = keep * inverse
             lo = pair * 2 * HEAD
-            both = dot(vt[lo : lo + 2 * HEAD], (e * inverse).astype(BF16))
+            both = dot(vt[lo : lo + 2 * HEAD], e[:, pair * 2 * block : (pair + 1) * 2 * block])
             for i in range(2):
                 lanes = slice(i * block, (i + 1) * block)
                 dims = slice(lo + i * HEAD, lo + (i + 1) * HEAD)
-                merged = lctx_ref[t, dims, :] * keep[:, lanes] + both[i * HEAD : (i + 1) * HEAD, lanes]
+                head = 2 * pair + i
+                far = both[i * HEAD : (i + 1) * HEAD, lanes]
+                merged = lctx_ref[t, dims, :] * keep[:, head * block : (head + 1) * block] + far
                 ctx_s[dims, t * block : (t + 1) * block] = merged.astype(BF16)
         rows += [p[t] for p in pieces]
-    after = jnp.concatenate(rows, axis=0).astype(F32) + dot_tn(ctx_s[...], wo_ref[...])
+    after = jnp.concatenate(rows, axis=0).astype(F32) + dot(ctx_s[...].T, wo_ref[...])
     normed = rms(after, gain_ffn_ref[...])
     hidden = gelu(dot(normed, w_in_ref[...])).astype(BF16)
     y = (after + dot(hidden, w_out_ref[...])).astype(BF16).reshape(tb, block, width)
@@ -313,7 +327,7 @@
     q, lctx, ltop, lsum, wvt = local
     steps, block, width = q.shape
     remote = live.shape[0]
-    tb = 2
+    tb = 4
     full = lambda a: pl.BlockSpec(a.shape, lambda i, *_: (0,) * a.ndim)
     per_t = lambda *shape: pl.BlockSpec((tb,) + shape, lambda i, *_: (i, 0, 0))
     if split:
@@ -334,8 +348,8 @@
                 full(live),
                 per_t(block, width),
                 per_t(width, block),
-                per_t(H, block),
-                per_t(H, block),
+                per_t(1, H * block),
+                per_t(1, H * block),
                 full(gain),
                 pl.BlockSpec((width, width), lambda i, *_: (0, 0)),
                 full(wvt),
@@ -403,7 +417,7 @@
     matches = (neighbour_blocks == block_index).astype(jnp.int32)
     wanted = jnp.sum(matches[:, :, None] * neighbour_rows, axis=1).reshape(-1)
     own = lax.dynamic_index_in_dim(neighbour_blocks, block_index, 0, keepdims=False)
-    live = jnp.broadcast_to(jnp.repeat(slot_used_mask[0], REMOTE_SENSORS)[:, None], (slots * REMOTE_SENSORS, 2 * block))
+    live = jnp.broadcast_to(jnp.repeat(slot_used_mask[0], REMOTE_SENSORS)[:, None], (slots * REMOTE_SENSORS, H * block))
     if split:
         place = (jnp.arange(block) + mine * sensors_here) % block
         pick = (wanted[:, None] == place[None, :]).astype(BF16)

time: 82.7 us -> 61.5 us (0.74)
  Pallas kernels: 56.7 us -> 37.2 us
  local copies, waits for them, and re-layouts: 8.82 us -> 2.05 us
  waiting for transfers between devices: 7.42 us -> 11.5 us
  other arithmetic: 0.18 us -> 1.34 us
    pallas_call x2, Pallas kernels: 21.2 us -> 10.6 us  [time_block(): pl.pallas_call(functools.partial(time_kernel, split), out_shape=out_shape...]
    unnamed x38 -> x12, local copies, waits for them, and re-layouts: 8.25 us -> 0.73 us
    pallas_call x1, Pallas kernels: 22.4 us -> 15.1 us  [finish(): pl.pallas_call(functools.partial(finish_kernel, len(pieces), split), out_...]
    all_to_all x1, waiting for transfers between devices: 0.01 us -> 4.47 us  [local(): lax.all_to_all(outgoing, 'sensor', split_axis=0, concat_axis=0, tiled=True)]
    pallas_call x1, Pallas kernels: 11.8 us -> 9.03 us  [local_part(): pl.pallas_call(functools.partial(local_kernel, len(pieces)), out_shape=[j...]
    pallas_call x1, Pallas kernels: 1.36 us -> 2.55 us  [pick_rows(): pl.pallas_call(functools.partial(pick_kernel, len(pieces)), out_shape=jax...]
  transfers between devices with their start and end apart: 3 -> 3, of which waited for: 1 -> 3; matrix products, arithmetic and copies ran while one was open for 1% -> 3% of each run, Pallas kernels for 27% -> 23%
where the time goes in v2:
time: 61.5 us; the launch traced here: 61.1 us
  Pallas kernels  37.2 us (60%)
  waiting for transfers between devices  11.5 us (19%)
  starting transfers between devices  9 us (15%)
  local copies, waits for them, and re-layouts  2.05 us (3%)
  other arithmetic  1.34 us (2%)
    pallas_call x1, Pallas kernels, finish(): pl.pallas_call(functools.partial(finish_kernel, len(pieces), split), out_...  15.1 us
    pallas_call x2, Pallas kernels, time_block(): pl.pallas_call(functools.partial(time_kernel, split), out_shape=out_shape...  10.6 us
    pallas_call x1, Pallas kernels, local_part(): pl.pallas_call(functools.partial(local_kernel, len(pieces)), out_shape=[j...  9.03 us
    ppermute x2, waiting for transfers between devices, local(): got.append(lax.ppermute(send, 'tm', [(0, 1), (1, 0)]))  7.02 us
    all_to_all x1, starting transfers between devices, local(): lax.all_to_all(outgoing, 'sensor', split_axis=0, concat_axis=0, tiled=True)  5.95 us
    all_to_all x1, waiting for transfers between devices, local(): lax.all_to_all(outgoing, 'sensor', split_axis=0, concat_axis=0, tiled=True)  4.47 us
    ppermute x2, starting transfers between devices, local(): got.append(lax.ppermute(send, 'tm', [(0, 1), (1, 0)]))  3.05 us
    pallas_call x1, Pallas kernels, pick_rows(): pl.pallas_call(functools.partial(pick_kernel, len(pieces)), out_shape=jax...  2.55 us
  transfers between devices with their start and end apart: 3, of which 3 were waited for; matrix products, arithmetic and copies ran while one was open for 3% of the time, Pallas kernels for 23%

profile of v2, /device:TPU:0, one launch (start us, length us, event | category | flops | bytes accessed | tf_op | source)
XLA Modules:
  0.0 61.1 jit_solution(12659548666998423294)
XLA Ops:
  0.0 5.3 %time_block.3 = (bf16[16,32,256]{2,1,0:T(8,128)(2,1)}, bf16[16,32,256]{2,1,0:T(8,128)(2,1)}) custom-call(s32[1]{0:T(128)} %bitcast.my_ref, bf16[64,32,256]{2,1,0:T(8,128)(2,1)} %x_ref.3, f32[1,256]{1,0:T(1,128)} %bitcast.8, bf16[256,256]{1,0:T(8,128)(2,1)} %wq_ref.3, bf16[256,512]{1,0:T(8,128)(2,1)} %wkv_ref.3, bf16[256,256]{1,0:T(8,128)(2,1)} %wo_ref.3), custom_call_target="tpu_custom_call" | custom-call | flops 805306368 | bytes 1048576 | tf_op jit(solution)/shard_map/time_block/pallas_call | solution.py:127
  5.3 0.0 copy-start.3
  5.3 0.0 copy-start.4
  5.3 3.0 %collective-permute-start.1 = (bf16[16,32,256]{2,1,0:T(8,128)(2,1)}, bf16[16,32,256]{2,1,0:T(8,128)(2,1)S(1)}, u32[]{:S(2)}, u32[]{:S(2)}) collective-permute-start(bf16[16,32,256]{2,1,0:T(8,128)(2,1)} %get-tuple-element.17), channel_id=1, source_target_pairs={{0,1},{1,0},{2,3},{3,2},{4,5},{5,4},{6,7},{7,6},{8,9},{9,8},{10,11... | collective-permute-start | bytes 786440 | tf_op jit(solution)/shard_map/ppermute | solution.py:412
  8.3 5.3 %time_block.2 = (bf16[16,32,256]{2,1,0:T(8,128)(2,1)}, bf16[16,32,256]{2,1,0:T(8,128)(2,1)}) custom-call(s32[1]{0:T(128)} %bitcast.my_ref, bf16[64,32,256]{2,1,0:T(8,128)(2,1)} %x_ref.3, f32[1,256]{1,0:T(1,128)} %bitcast.9, bf16[256,256]{1,0:T(8,128)(2,1)} %wq_ref.3, bf16[256,512]{1,0:T(8,128)(2,1)} %wkv_ref.3, bf16[256,256]{1,0:T(8,128)(2,1)} %wo_ref.3), custom_call_target="tpu_custom_call" | custom-call | flops 805306368 | bytes 1048576 | tf_op jit(solution)/shard_map/time_block/pallas_call | solution.py:127
  13.6 0.0 copy-start.5
  13.6 0.0 collective-permute-start
  13.6 0.0 copy-done.3
  13.6 0.0 copy-done.4
  13.7 0.1 copy.16
  13.8 0.1 eq.25
  13.9 0.7 %compare_convert_fusion.pick_ref = bf16[64,128]{1,0:T(8,128)(2,1)} fusion(s32[128]{0:T(128)S(1)} %and_select_fusion, s32[64]{0:T(128)S(1)} %eq.25), kind=kLoop, calls=%fused_computation | loop fusion | flops 16384 | bytes 17152 | tf_op jit(solution)/shard_map/convert_element_type | solution.py:423
  14.5 0.3 collective-permute-done.1.refs_3_
  14.8 0.0 copy-start.1
  14.8 6.7 %collective-permute-done.refs_2_ = bf16[16,32,256]{2,1,0:T(8,128)(2,1)S(1)} collective-permute-done((bf16[16,32,256]{2,1,0:T(8,128)(2,1)}, bf16[16,32,256]{2,1,0:T(8,128)(2,1)S(1)}, u32[]{:S(2)}, u32[]{:S(2)}) %collective-permute-start) | collective-permute-done | bytes 262176 | tf_op jit(solution)/shard_map/ppermute | solution.py:412
  21.6 0.0 copy-start.2
  21.6 0.0 copy-done.1
  21.6 0.7 %copy-done.2 = bf16[16,32,256]{2,1,0:T(8,128)(2,1)} copy-done((bf16[16,32,256]{2,1,0:T(8,128)(2,1)}, bf16[16,32,256]{2,1,0:T(8,128)(2,1)S(1)}, u32[]{:S(2)}) %copy-start.2) | copy-done | bytes 262168
  22.3 2.5 %pick_rows.1 = bf16[64,16,256]{2,1,0:T(8,128)(2,1)} custom-call(bf16[64,128]{1,0:T(8,128)(2,1)} %compare_convert_fusion.pick_ref, bf16[16,32,256]{2,1,0:T(8,128)(2,1)} %get-tuple-element.14.refs_0_, bf16[16,32,256]{2,1,0:T(8,128)(2,1)} %get-tuple-element.15.refs_1_, bf16[16,32,256]{2,1,0:T(8,128)(2,1)} %copy-done.2, bf16[16,32,256]{2,1,0:T(8,128)(2,1)} %copy-done.1), custom_call_target="tpu_custom_call" | custom-call | tf_op jit(solution)/shard_map/pick_rows/pallas_call | solution.py:168
  24.8 5.9 %all-to-all-start = ((bf16[16,4,16,256]{3,2,1,0:T(8,128)(2,1)}), bf16[16,4,16,256]{3,2,1,0:T(8,128)(2,1)S(1)}, u32[]{:S(2)}, u32[]{:S(2)}) async-start(bf16[16,4,16,256]{3,2,1,0:T(8,128)(2,1)} %bitcast.6), calls=%async_computation | async-start | bytes 1048576 | tf_op jit(solution)/shard_map/all_to_all | solution.py:428
  30.8 0.2 dynamic-slice_reduce_fusion
  31.0 0.0 copy-done.5
  31.0 0.1 broadcast_in_dim.12
  31.0 0.1 broadcast_in_dim.13
  31.1 0.6 %pad_add_fusion.own_ref = s32[9]{0:T(128)} fusion(s32[1]{0:T(128)} %bitcast.my_ref, s32[8]{0:T(128)S(1)} %dynamic-slice_reduce_fusion), kind=kLoop, calls=%fused_computation.8 | loop fusion | flops 9 | bytes 72 | tf_op jit(solution)/shard_map/concatenate | solution.py:432
  31.7 9.0 %local_keys.1 = (bf16[16,128,256]{2,1,0:T(8,128)(2,1)}, f32[16,256,128]{2,1,0:T(8,128)}, f32[16,1,1024]{2,1,0:T(1,128)}, f32[16,1,1024]{2,1,0:T(1,128)}, bf16[256,256]{1,0:T(8,128)(2,1)}) custom-call(bf16[16,32,256]{2,1,0:T(8,128)(2,1)} %get-tuple-element.14.refs_0_, bf16[16,32,256]{2,1,0:T(8,128)(2,1)} %get-tuple-element.15.refs_1_, ...), custom_call_target="tpu_custom_call" | custom-call | flops 1610612736 | bytes 5242880 | tf_op jit(solution)/shard_map/local_keys/pallas_call | solution.py:220
  40.8 4.5 %all-to-all-done.refs_4_ = bf16[16,4,16,256]{3,2,1,0:T(8,128)(2,1)S(1)} async-done(((bf16[16,4,16,256]{3,2,1,0:T(8,128)(2,1)}), bf16[16,4,16,256]{3,2,1,0:T(8,128)(2,1)S(1)}, u32[]{:S(2)}, u32[]{:S(2)}) %all-to-all-start) | async-done | bytes 524320 | tf_op jit(solution)/shard_map/all_to_all | solution.py:428
  45.2 0.0 copy-start
  45.2 0.8 %broadcast_in_dim.14.refs_5_ = s32[32,1024]{1,0:T(8,128)} broadcast(s32[32]{0:T(128)S(1)} %broadcast_in_dim.13), dimensions={0} | broadcast | bytes 131200 | tf_op jit(solution)/shard_map/broadcast_in_dim | solution.py:420
  46.0 0.0 copy-done
  46.1 15.1 %remote_keys_and_feed_forward.1 = bf16[128,16,256]{2,1,0:T(8,128)(2,1)} custom-call(s32[9]{0:T(128)} %pad_add_fusion.own_ref, bf16[16,32,256]{2,1,0:T(8,128)(2,1)} %get-tuple-element.14.refs_0_, bf16[16,32,256]{2,1,0:T(8,128)(2,1)} %get-tuple-element.15.refs_1_, bf16[16,32,256]{2,1,0:T(8,128)(2,1)} %copy-done.2, bf16[16,32,256]{2,1,0:T(8,128)(2,1)} %copy-done.1, ...), custom_call_target="tpu_custom_call" | custom-call | flops 2415919104 | bytes 6291456 | tf_op jit(solution)/shard_map/remote_keys_and_feed_forward/pallas_call | solution.py:339
  (3 shorter events, 0.0 us)
Async XLA Ops:
  5.3 8.3 %copy-start.3 = (s32[16,8]{0,1:T(8,128)S(1)}, s32[16,8]{0,1:T(8,128)}, u32[]{:S(2)}) copy-start(s32[16,8]{0,1:T(8,128)} %param.27) | copy-start | bytes 1540
  5.3 8.3 %copy-start.4 = (s32[16,8,4]{0,2,1:T(4,128)S(1)}, s32[16,8,4]{0,2,1:T(4,128)}, u32[]{:S(2)}) copy-start(s32[16,8,4]{0,2,1:T(4,128)} %param.29) | copy-start | bytes 6148
  5.3 9.5 %collective-permute-start.1 = (bf16[16,32,256]{2,1,0:T(8,128)(2,1)}, bf16[16,32,256]{2,1,0:T(8,128)(2,1)S(1)}, u32[]{:S(2)}, u32[]{:S(2)}) collective-permute-start(bf16[16,32,256]{2,1,0:T(8,128)(2,1)} %get-tuple-element.17), channel_id=1, source_target_pairs={{0,1},{1,0},{2,3},{3,2},{4,5},{5,4},{6,7},{7,6},{8,9},{9,8},{10,11... | collective-permute-start | bytes 786440 | tf_op jit(solution)/shard_map/ppermute | solution.py:412
  13.6 17.4 %copy-start.5 = (s32[1,8]{1,0:T(1,128)S(1)}, s32[1,8]{1,0:T(1,128)}, u32[]{:S(2)}) copy-start(s32[1,8]{1,0:T(1,128)} %param.28) | copy-start | bytes 100
  13.6 8.0 %collective-permute-start = (bf16[16,32,256]{2,1,0:T(8,128)(2,1)}, bf16[16,32,256]{2,1,0:T(8,128)(2,1)S(1)}, u32[]{:S(2)}, u32[]{:S(2)}) collective-permute-start(bf16[16,32,256]{2,1,0:T(8,128)(2,1)} %get-tuple-element.16), channel_id=1, source_target_pairs={{0,1},{1,0},{2,3},{3,2},{4,5},{5,4},{6,7},{7,6},{8,9},{9,8},{10,11... | collective-permute-start | bytes 786440 | tf_op jit(solution)/shard_map/ppermute | solution.py:412
  14.8 6.7 %copy-start.1 = (bf16[16,32,256]{2,1,0:T(8,128)(2,1)}, bf16[16,32,256]{2,1,0:T(8,128)(2,1)S(1)}, u32[]{:S(2)}) copy-start(bf16[16,32,256]{2,1,0:T(8,128)(2,1)S(1)} %collective-permute-done.1.refs_3_) | copy-start | bytes 786436
  21.6 0.7 %copy-start.2 = (bf16[16,32,256]{2,1,0:T(8,128)(2,1)}, bf16[16,32,256]{2,1,0:T(8,128)(2,1)S(1)}, u32[]{:S(2)}) copy-start(bf16[16,32,256]{2,1,0:T(8,128)(2,1)S(1)} %collective-permute-done.refs_2_) | copy-start | bytes 786436
  24.8 20.4 %all-to-all-start = ((bf16[16,4,16,256]{3,2,1,0:T(8,128)(2,1)}), bf16[16,4,16,256]{3,2,1,0:T(8,128)(2,1)S(1)}, u32[]{:S(2)}, u32[]{:S(2)}) async-start(bf16[16,4,16,256]{3,2,1,0:T(8,128)(2,1)} %bitcast.6), calls=%async_computation | async-start | bytes 1048576 | tf_op jit(solution)/shard_map/all_to_all | solution.py:428
  45.2 0.8 %copy-start = (bf16[16,4,16,256]{3,2,1,0:T(8,128)(2,1)}, bf16[16,4,16,256]{3,2,1,0:T(8,128)(2,1)S(1)}, u32[]{:S(2)}) copy-start(bf16[16,4,16,256]{3,2,1,0:T(8,128)(2,1)S(1)} %all-to-all-done.refs_4_) | copy-start | bytes 1572868

commit v3 on v2

--- a/solution.py
+++ b/solution.py
@@ -16,7 +16,8 @@
 SCALE = math.log2(math.e) / math.sqrt(HEAD)
 F32 = jnp.float32
 BF16 = jnp.bfloat16
-VMEM_LIMIT = 60 * 1024 * 1024
+VMEM_LARGE = 60 * 1024 * 1024
+VMEM_SMALL = 24 * 1024 * 1024
 
 
 def dot(a, b):
@@ -140,7 +141,7 @@
             out_specs=out_specs,
             scratch_shapes=[pltpu.VMEM((rows, width), BF16)] * 5 + extra,
         ),
-        compiler_params=pltpu.CompilerParams(vmem_limit_bytes=VMEM_LIMIT),
+        compiler_params=pltpu.CompilerParams(vmem_limit_bytes=VMEM_LARGE if first == 0 else VMEM_SMALL),
         cost_estimate=pl.CostEstimate(
             flops=count * steps * width * width * 12, bytes_accessed=count * steps * width * 4, transcendentals=0
         ),
@@ -169,7 +170,7 @@
         functools.partial(pick_kernel, len(pieces)),
         out_shape=jax.ShapeDtypeStruct((wanted, steps, width), BF16),
         scratch_shapes=[pltpu.VMEM((steps, wanted, width), BF16)],
-        compiler_params=pltpu.CompilerParams(vmem_limit_bytes=VMEM_LIMIT),
+        compiler_params=pltpu.CompilerParams(vmem_limit_bytes=VMEM_SMALL),
         name="pick_rows",
     )(pick, *pieces)
 
@@ -182,33 +183,36 @@
 
 def local_kernel(n, *refs):
     pieces = refs[:n]
-    gain_ref, wq_ref, wkv_ref, q_ref, ctx_ref, top_ref, sum_ref, wvt_ref = refs[n:]
-    tb, block, width = q_ref.shape
+    gain_ref, wq_ref, wkv_ref, qt_ref, ctx_ref, top_ref, sum_ref, wvt_ref, wqt_s = refs[n:]
+    tb, width, block = qt_ref.shape
 
     @pl.when(pl.program_id(0) == 0)
     def _():
-        wvt_ref[...] = wkv_ref[:, width:].astype(F32).T.astype(BF16)
+        wvt_ref[...] = wkv_ref[:, width:].T
+        wqt_s[...] = wq_ref[...].T
 
     x = jnp.concatenate([p[t] for t in range(tb) for p in pieces], axis=0).astype(F32)
     normed = rms(x, gain_ref[...])
     q = dot(normed, wq_ref[...]).astype(BF16)
     k = dot(normed, wkv_ref[:, :width]).astype(BF16)
-    q_ref[...] = q.reshape(tb, block, width)
     masks = [head_rows(2 * block, 128, block, -2 * p) for p in range(2)]
     for t in range(tb):
         here = slice(t * block, (t + 1) * block)
+        qt_ref[t] = dot_nt(wqt_s[...], normed[here]).astype(BF16)
         vt = dot_nt(wvt_ref[...], normed[here]).astype(BF16)
         scores = [pair_scores(q[here], k[here], masks, pair) for pair in range(H // 2)]
         tops = [jnp.max(x, axis=0, keepdims=True) for x in scores]
         es = [jnp.exp2((x - top) * SCALE) for x, top in zip(scores, tops)]
-        top_ref[t] = jnp.concatenate(tops, axis=1)
-        sum_ref[t] = jnp.concatenate([jnp.sum(e, axis=0, keepdims=True) for e in es], axis=1)
         for pair, e in enumerate(es):
             lo = pair * 2 * HEAD
             both = dot(vt[lo : lo + 2 * HEAD], e.astype(BF16))
+            total = jnp.sum(e, axis=0, keepdims=True)
             for i in range(2):
                 lanes = slice(i * block, (i + 1) * block)
-                ctx_ref[t, lo + i * HEAD : lo + (i + 1) * HEAD, :] = both[i * HEAD : (i + 1) * HEAD, lanes]
+                head = 2 * pair + i
+                ctx_ref[t, lo + i * HEAD : lo + (i + 1) * HEAD, :] = both[i * HEAD : (i + 1) * HEAD, lanes].astype(BF16)
+                top_ref[t, head : head + 1, :] = tops[pair][:, lanes]
+                sum_ref[t, head : head + 1, :] = total[:, lanes]
 
 
 def local_part(pieces, gain, wq, wkv):
@@ -220,22 +224,23 @@
     return pl.pallas_call(
         functools.partial(local_kernel, len(pieces)),
         out_shape=[
-            jax.ShapeDtypeStruct((steps, block, width), BF16),
-            jax.ShapeDtypeStruct((steps, width, block), F32),
-            jax.ShapeDtypeStruct((steps, 1, H * block), F32),
-            jax.ShapeDtypeStruct((steps, 1, H * block), F32),
+            jax.ShapeDtypeStruct((steps, width, block), BF16),
+            jax.ShapeDtypeStruct((steps, width, block), BF16),
+            jax.ShapeDtypeStruct((steps, H, block), F32),
+            jax.ShapeDtypeStruct((steps, H, block), F32),
             jax.ShapeDtypeStruct((width, width), BF16),
         ],
         grid=(steps // tb,),
         in_specs=[per_t(p.shape[1], width) for p in pieces] + [full(gain), full(wq), full(wkv)],
         out_specs=[
-            per_t(block, width),
             per_t(width, block),
-            per_t(1, H * block),
-            per_t(1, H * block),
+            per_t(width, block),
+            per_t(H, block),
+            per_t(H, block),
             pl.BlockSpec((width, width), lambda i: (0, 0)),
         ],
-        compiler_params=pltpu.CompilerParams(vmem_limit_bytes=VMEM_LIMIT),
+        scratch_shapes=[pltpu.VMEM((width, width), BF16)],
+        compiler_params=pltpu.CompilerParams(vmem_limit_bytes=VMEM_SMALL),
         cost_estimate=pl.CostEstimate(
             flops=steps * block * width * width * 12, bytes_accessed=steps * block * width * 10, transcendentals=0
         ),
@@ -249,130 +254,175 @@
     return half + half * jnp.tanh(inner)
 
 
-def finish_kernel(n, split, own_ref, *refs):
+def finish_kernel(n, split, tb, numbers_ref, *refs):
     pieces = refs[:n]
-    (in_ref, live_ref, q_ref, lctx_ref, ltop_ref, lsum_ref, gain_ref, wk_ref, wvt_ref, wo_ref, gain_ffn_ref,
-     w_in_ref, w_out_ref, out_ref, rn_s, rk_s, ctx_s, y_s, pick_s) = refs[n:]
-    tb, block, width = q_ref.shape
-    steps, remote = rn_s.shape[:2]
-    step = pl.program_id(0)
-
-    @pl.when(step == 0)
-    def _():
-        if split:
-            order = swap16()
-            for j in range(remote // REMOTE_SENSORS):
-                pick_s[j * REMOTE_SENSORS : (j + 1) * REMOTE_SENSORS] = in_ref[own_ref[j]]
-            for b in range(remote // 16):
-                rows = pick_s[b * 16 : (b + 1) * 16].reshape(256, width)
-                rn_s[:, b * 16 : (b + 1) * 16, :] = dot(order, rows).astype(BF16).reshape(16, 16, width)
-            raw = rn_s[...]
-        else:
-            raw = in_ref[...]
-        normed = rms(raw.reshape(steps * remote, width).astype(F32), gain_ref[...])
-        rn_s[...] = normed.reshape(steps, remote, width)
-        rk_s[...] = dot(normed, wk_ref[...]).astype(BF16).reshape(steps, remote, width)
-
-    live = live_ref[...] > 0
-    masks = [head_rows(2 * block, 128, block, -2 * p) for p in range(2)]
-    rows = []
-    for t in range(tb):
-        at = step * tb + t
-        rk = rk_s[at]
-        vt = dot_nt(wvt_ref[...], rn_s[at]).astype(BF16)
-        q = q_ref[t]
-        scores = jnp.concatenate([pair_scores(q, rk, masks, pair) for pair in range(H // 2)], axis=1)
-        scores = jnp.where(live, scores, NEG)
-        ltop = ltop_ref[t]
-        top = jnp.maximum(jnp.max(scores, axis=0, keepdims=True), ltop)
-        e = jnp.exp2((scores - top) * SCALE)
-        keep = jnp.exp2((ltop - top) * SCALE)
-        inverse = 1.0 / (jnp.sum(e, axis=0, keepdims=True) + lsum_ref[t] * keep)
-        keep = keep * inverse
-        e = (e * inverse).astype(BF16)
-        for pair in range(H // 2):
-            lo = pair * 2 * HEAD
-            both = dot(vt[lo : lo + 2 * HEAD], e[:, pair * 2 * block : (pair + 1) * 2 * block])
-            for i in range(2):
-                lanes = slice(i * block, (i + 1) * block)
-                dims = slice(lo + i * HEAD, lo + (i + 1) * HEAD)
-                head = 2 * pair + i
-                far = both[i * HEAD : (i + 1) * HEAD, lanes]
-                merged = lctx_ref[t, dims, :] * keep[:, head * block : (head + 1) * block] + far
-                ctx_s[dims, t * block : (t + 1) * block] = merged.astype(BF16)
-        rows += [p[t] for p in pieces]
-    after = jnp.concatenate(rows, axis=0).astype(F32) + dot(ctx_s[...].T, wo_ref[...])
-    normed = rms(after, gain_ffn_ref[...])
-    hidden = gelu(dot(normed, w_in_ref[...])).astype(BF16)
-    y = (after + dot(hidden, w_out_ref[...])).astype(BF16).reshape(tb, block, width)
+    in_hbm, gain_ref, gain_ffn_ref, ltop_ref, lsum_ref = refs[n : n + 5]
+    qt_hbm, lctx_hbm, wkv_hbm, wvt_hbm, wo_hbm, w_in_hbm, w_out_hbm, out_hbm = refs[n + 5 : n + 13]
+    x_s, raw_s, rn_s, rk_s, ctx_s, y_s, out_s, qt_s, lctx_s, wk_s, wvt_s, wo_s, w_in_s, w_out_s, sems, out_sems = refs[n + 13 :]
+    steps, width, block = qt_s.shape
+    remote = rn_s.shape[1]
+    slots = remote // REMOTE_SENSORS
+    chunks = steps // tb
+    count = [0]
+
+    def fetch(src, dst):
+        copy = pltpu.make_async_copy(src, dst, sems.at[count[0]])
+        count[0] += 1
+        copy.start()
+        return copy
+
+    if split:
+        raw_in = [
+            fetch(in_hbm.at[numbers_ref[1 + j]], raw_s.at[pl.ds(j * REMOTE_SENSORS, REMOTE_SENSORS)]) for j in range(slots)
+        ]
+    else:
+        raw_in = [fetch(in_hbm, raw_s)]
+    first_in = [fetch(wkv_hbm.at[:, pl.ds(0, width)], wk_s), fetch(wvt_hbm, wvt_s)]
+    chunk = [pl.ds(c * tb, tb) for c in range(chunks)]
+    qt_in = [fetch(qt_hbm.at[here], qt_s.at[here]) for here in chunk]
+
+    order = swap16() if split else None
+    lane_head = lax.broadcasted_iota(jnp.int32, (1, 128), 1) // HEAD
+    heads = [(lane_head == h).astype(BF16) for h in range(128 // HEAD)]
+    none = jnp.zeros((remote, 128), BF16)
+    own_block = (
+        lax.broadcasted_iota(jnp.int32, (width, H * remote), 0) // HEAD
+        == lax.broadcasted_iota(jnp.int32, (width, H * remote), 1) // remote
+    ).astype(BF16)
+    slot = lax.broadcasted_iota(jnp.int32, (remote, block), 0) // REMOTE_SENSORS
+    live = jnp.zeros((remote, block), jnp.int32)
+    for j in range(slots):
+        live = jnp.where(slot == j, numbers_ref[1 + slots + j], live)
+    live = live > 0
+
+    for copy in raw_in + first_in:
+        copy.wait()
+    lctx_in, x_in = [], []
+    for here in chunk:
+        lctx_in.append(fetch(lctx_hbm.at[here], lctx_s.at[here]))
+        place, x_c = 0, []
+        for p in pieces:
+            x_c.append(fetch(p.at[here], x_s.at[here, pl.ds(place, p.shape[1])]))
+            place += p.shape[1]
+        x_in.append(x_c)
+    wo_in = fetch(wo_hbm, wo_s)
+    ffn_in = [fetch(w_in_hbm, w_in_s), fetch(w_out_hbm, w_out_s)]
+    if split:
+        for b in range(remote // 16):
+            rows = raw_s[b * 16 : (b + 1) * 16].reshape(256, width)
+            rn_s[:, b * 16 : (b + 1) * 16, :] = dot(order, rows).astype(BF16).reshape(16, 16, width)
+        raw = rn_s[...]
+    else:
+        raw = raw_s[...]
+    normed = rms(raw.reshape(steps * remote, width).astype(F32), gain_ref[...])
+    rn_s[...] = normed.reshape(steps, remote, width)
+    rk_s[...] = dot(normed, wk_s[...]).astype(BF16).reshape(steps, remote, width)
+
+    for c in range(chunks):
+        ts = range(c * tb, (c + 1) * tb)
+        qt_in[c].wait()
+        keys = []
+        for t in ts:
+            rk = rk_s[t]
+            spread = []
+            for h in range(H):
+                half = h * HEAD // 128
+                part = rk[:, half * 128 : (half + 1) * 128] * heads[h % (128 // HEAD)]
+                spread.append(jnp.concatenate([part, none] if half == 0 else [none, part], axis=1))
+            keys.append(jnp.concatenate(spread, axis=0))
+        scores = [dot(k, qt_s[t]).reshape(H, remote, block) for k, t in zip(keys, ts)]
+        values = []
+        for t in ts:
+            tiled = jnp.concatenate([rn_s[t]] * H, axis=0)
+            values.append(dot_nt(wvt_s[...], tiled).astype(BF16) * own_block)
+        weights, keeps = [], []
+        for s, t in zip(scores, ts):
+            masked = jnp.where(live[None], s, NEG)
+            ltop = ltop_ref[t]
+            top = jnp.maximum(jnp.max(masked, axis=1), ltop)
+            e = jnp.exp2((masked - top[:, None, :]) * SCALE)
+            keep = jnp.exp2((ltop - top) * SCALE)
+            inverse = 1.0 / (jnp.sum(e, axis=1) + lsum_ref[t] * keep)
+            keeps.append(keep * inverse)
+            weights.append((e * inverse[:, None, :]).astype(BF16).reshape(H * remote, block))
+        far = [dot(v, w).reshape(H, HEAD, block) for v, w in zip(values, weights)]
+        lctx_in[c].wait()
+        for i, t in enumerate(ts):
+            merged = lctx_s[t].astype(F32).reshape(H, HEAD, block) * keeps[i][:, None, :] + far[i]
+            ctx_s[:, i * block : (i + 1) * block] = merged.reshape(width, block).astype(BF16)
+        if c == 0:
+            wo_in.wait()
+        for copy in x_in[c]:
+            copy.wait()
+        x = x_s[c * tb : (c + 1) * tb].reshape(tb * block, width)
+        after = x.astype(F32) + dot(ctx_s[...].T, wo_s[...])
+        normed = rms(after, gain_ffn_ref[...])
+        if c == 0:
+            for copy in ffn_in:
+                copy.wait()
+        hidden = gelu(dot(normed, w_in_s[...])).astype(BF16)
+        y_s[c * tb : (c + 1) * tb] = (after + dot(hidden, w_out_s[...])).astype(BF16).reshape(tb, block, width)
+
     if not split:
-        out_ref[...] = y
+        copy = pltpu.make_async_copy(y_s, out_hbm, out_sems.at[0])
+        copy.start()
+        copy.wait()
         return
-    y_s[pl.ds(step * tb, tb)] = y
-
-    @pl.when(step == pl.num_programs(0) - 1)
-    def _():
-        order = swap16()
-        mine = own_ref[own_ref.shape[0] - 1]
-        half = block // 2
-        for b in range(block // 16):
-            first = b * 16
-            owner = mine if first < half else 1 - mine
-            rows = y_s[:, first : first + 16, :].reshape(256, width)
-            at = owner * half + first % half
-            out_ref[pl.ds(at, 16)] = dot(order, rows).astype(BF16).reshape(16, 16, width)
-
-
-def finish(own, pieces, incoming, live, local, gain, wkv, wo, gain_ffn, w_in, w_out, split):
-    q, lctx, ltop, lsum, wvt = local
-    steps, block, width = q.shape
-    remote = live.shape[0]
-    tb = 4
-    full = lambda a: pl.BlockSpec(a.shape, lambda i, *_: (0,) * a.ndim)
-    per_t = lambda *shape: pl.BlockSpec((tb,) + shape, lambda i, *_: (i, 0, 0))
-    if split:
-        out_shape = jax.ShapeDtypeStruct((block, steps, width), BF16)
-        out_specs = pl.BlockSpec((block, steps, width), lambda i, *_: (0, 0, 0))
-    else:
-        out_shape = jax.ShapeDtypeStruct((steps, block, width), BF16)
-        out_specs = per_t(block, width)
+    mine = numbers_ref[0]
+    half = block // 2
+    copies = []
+    for b in range(block // 16):
+        first = b * 16
+        owner = mine if first < half else 1 - mine
+        rows = y_s[:, first : first + 16, :].reshape(256, width)
+        out_s[first : first + 16] = dot(order, rows).astype(BF16).reshape(16, 16, width)
+        place = out_hbm.at[pl.ds(owner * half + first % half, 16)]
+        copy = pltpu.make_async_copy(out_s.at[pl.ds(first, 16)], place, out_sems.at[b])
+        copy.start()
+        copies.append(copy)
+    for copy in copies:
+        copy.wait()
+
+
+def finish(numbers, pieces, incoming, local, gain, wkv, wo, gain_ffn, w_in, w_out, split):
+    qt, lctx, ltop, lsum, wvt = local
+    steps, width, block = qt.shape
+    remote = (numbers.shape[0] - 1) // 2 * REMOTE_SENSORS
+    tb = min(16, steps)
+    vmem = pl.BlockSpec(memory_space=pltpu.VMEM)
+    hbm = pl.BlockSpec(memory_space=pl.ANY)
+    chunks = steps // tb
+    n_copies = (remote // REMOTE_SENSORS if split else 1) + 5 + chunks * (2 + len(pieces))
+    buffer = lambda *shape: pltpu.VMEM(shape, BF16)
     return pl.pallas_call(
-        functools.partial(finish_kernel, len(pieces), split),
-        out_shape=out_shape,
-        grid_spec=pltpu.PrefetchScalarGridSpec(
-            num_scalar_prefetch=1,
-            grid=(steps // tb,),
-            in_specs=[per_t(p.shape[1], width) for p in pieces]
-            + [
-                full(incoming),
-                full(live),
-                per_t(block, width),
-                per_t(width, block),
-                per_t(1, H * block),
-                per_t(1, H * block),
-                full(gain),
-                pl.BlockSpec((width, width), lambda i, *_: (0, 0)),
-                full(wvt),
-                full(wo),
-                full(gain_ffn),
-                full(w_in),
-                full(w_out),
-            ],
-            out_specs=out_specs,
-            scratch_shapes=[
-                pltpu.VMEM((steps, remote, width), BF16),
-                pltpu.VMEM((steps, remote, width), BF16),
-                pltpu.VMEM((width, tb * block), BF16),
-                pltpu.VMEM((steps, block, width), BF16),
-                pltpu.VMEM((remote, steps, width), BF16),
-            ],
-        ),
-        compiler_params=pltpu.CompilerParams(vmem_limit_bytes=VMEM_LIMIT),
+        functools.partial(finish_kernel, len(pieces), split, tb),
+        out_shape=jax.ShapeDtypeStruct((block, steps, width) if split else (steps, block, width), BF16),
+        in_specs=[pl.BlockSpec(memory_space=pltpu.SMEM)] + [hbm] * (len(pieces) + 1) + [vmem] * 4 + [hbm] * 7,
+        out_specs=hbm,
+        scratch_shapes=[
+            buffer(steps, block, width),
+            buffer(remote, steps, width) if split else buffer(steps, remote, width),
+            buffer(steps, remote, width),
+            buffer(steps, remote, width),
+            buffer(width, tb * block),
+            buffer(steps, block, width),
+            buffer(block, steps, width) if split else buffer(8, 128),
+            buffer(steps, width, block),
+            buffer(steps, width, block),
+            buffer(width, width),
+            buffer(width, width),
+            buffer(*wo.shape),
+            buffer(*w_in.shape),
+            buffer(*w_out.shape),
+            pltpu.SemaphoreType.DMA((n_copies,)),
+            pltpu.SemaphoreType.DMA((max(block // 16, 1),)),
+        ],
+        compiler_params=pltpu.CompilerParams(vmem_limit_bytes=VMEM_LARGE),
         cost_estimate=pl.CostEstimate(
             flops=steps * block * width * width * 18, bytes_accessed=steps * block * width * 12, transcendentals=0
         ),
         name="remote_keys_and_feed_forward",
-    )(own, *pieces, incoming, live, q, lctx, ltop, lsum, gain, wkv, wvt, wo, gain_ffn, w_in, w_out)
+    )(numbers, *pieces, incoming, gain, gain_ffn, ltop, lsum, qt, lctx, wkv, wvt, wo, w_in, w_out)
 
 
 def local(
@@ -417,7 +467,7 @@
     matches = (neighbour_blocks == block_index).astype(jnp.int32)
     wanted = jnp.sum(matches[:, :, None] * neighbour_rows, axis=1).reshape(-1)
     own = lax.dynamic_index_in_dim(neighbour_blocks, block_index, 0, keepdims=False)
-    live = jnp.broadcast_to(jnp.repeat(slot_used_mask[0], REMOTE_SENSORS)[:, None], (slots * REMOTE_SENSORS, H * block))
+    numbers = jnp.concatenate([mine.reshape(1), own, slot_used_mask[0]])
     if split:
         place = (jnp.arange(block) + mine * sensors_here) % block
         pick = (wanted[:, None] == place[None, :]).astype(BF16)
@@ -429,8 +479,7 @@
     if not split:
         incoming = jnp.take(incoming, own, axis=0).reshape(-1, group, width).transpose(1, 0, 2)
     near = local_part(pieces, gain_graph, wq_graph, wkv_graph)
-    numbers = jnp.concatenate([own.astype(jnp.int32), mine.reshape(1)])
-    out = finish(numbers, pieces, incoming, live, near, gain_graph, wkv_graph, wo_graph, gain_ffn, w_in, w_out, split)
+    out = finish(numbers, pieces, incoming, near, gain_graph, wkv_graph, wo_graph, gain_ffn, w_in, w_out, split)
     return out if split else out.transpose(1, 0, 2)
 
 

time: 61.5 us -> 59.4 us (0.966)
  local copies, waits for them, and re-layouts: 2.05 us -> 12.7 us
  Pallas kernels: 37.2 us -> 28.6 us
  waiting for transfers between devices: 11.5 us -> 7.55 us
  other arithmetic: 1.34 us -> 0.72 us
    unnamed x12 -> x44, local copies, waits for them, and re-layouts: 0.73 us -> 12.3 us
    pallas_call x1, Pallas kernels: 15.1 us -> 10.6 us  [finish(): pl.pallas_call(functools.partial(finish_kernel, len(pieces), split, tb),...]
    all_to_all x1, waiting for transfers between devices: 4.47 us -> 0.55 us  [local(): lax.all_to_all(outgoing, 'sensor', split_axis=0, concat_axis=0, tiled=True)]
    pallas_call x2, Pallas kernels: 10.6 us -> 8.7 us  [time_block(): pl.pallas_call(functools.partial(time_kernel, split), out_shape=out_shape...]
    pallas_call x1, Pallas kernels: 2.55 us -> 1.35 us  [pick_rows(): pl.pallas_call(functools.partial(pick_kernel, len(pieces)), out_shape=jax...]
    pallas_call x1, Pallas kernels: 9.03 us -> 7.89 us  [local_part(): pl.pallas_call(functools.partial(local_kernel, len(pieces)), out_shape=[j...]
    broadcast_in_dim x3 -> x0, local copies, waits for them, and re-layouts: 0.95 us -> none  [the longest x2 0.88 us: local(): jnp.broadcast_to(jnp.repeat(slot_used_mask[0], REMOTE_SENSORS)[:, None],...]
  transfers between devices with their start and end apart: 3 -> 3, of which waited for: 3 -> 2; matrix products, arithmetic and copies ran while one was open for 3% -> 2% of each run, Pallas kernels for 23% -> 22%
where the time goes in v3:
time: 59.4 us; the launch traced here: 58.9 us
  Pallas kernels  28.6 us (48%)
  local copies, waits for them, and re-layouts  12.7 us (21%)
  starting transfers between devices  9.13 us (15%)
  waiting for transfers between devices  7.55 us (13%)
  other arithmetic  0.72 us (1%)
    unnamed x44, local copies, waits for them, and re-layouts  12.3 us
    pallas_call x1, Pallas kernels, finish(): pl.pallas_call(functools.partial(finish_kernel, len(pieces), split, tb),...  10.6 us
    pallas_call x2, Pallas kernels, time_block(): pl.pallas_call(functools.partial(time_kernel, split), out_shape=out_shape...  8.7 us
    pallas_call x1, Pallas kernels, local_part(): pl.pallas_call(functools.partial(local_kernel, len(pieces)), out_shape=[j...  7.89 us
    ppermute x2, waiting for transfers between devices, local(): got.append(lax.ppermute(send, 'tm', [(0, 1), (1, 0)]))  7 us
    all_to_all x1, starting transfers between devices, local(): lax.all_to_all(outgoing, 'sensor', split_axis=0, concat_axis=0, tiled=True)  6.08 us
    ppermute x2, starting transfers between devices, local(): got.append(lax.ppermute(send, 'tm', [(0, 1), (1, 0)]))  3.05 us
    pallas_call x1, Pallas kernels, pick_rows(): pl.pallas_call(functools.partial(pick_kernel, len(pieces)), out_shape=jax...  1.35 us
  transfers between devices with their start and end apart: 3, of which 2 were waited for; matrix products, arithmetic and copies ran while one was open for 2% of the time, Pallas kernels for 22%

profile of v3, /device:TPU:0, one launch (start us, length us, event | category | flops | bytes accessed | tf_op | source)
XLA Modules:
  0.0 58.9 jit_solution(879702667534535361)
XLA Ops:
  0.0 0.0 copy-start.11
  0.0 0.7 %copy-done.11 = f32[256]{0:T(256)S(1)} copy-done((f32[256]{0:T(256)S(1)}, f32[256]{0:T(256)}, u32[]{:S(2)}) %copy-start.11) | copy-done | bytes 1048
  0.7 0.0 copy-start.5
  0.7 1.2 %copy-done.5 = bf16[64,32,256]{2,1,0:T(8,128)(2,1)S(1)} copy-done((bf16[64,32,256]{2,1,0:T(8,128)(2,1)S(1)}, bf16[64,32,256]{2,1,0:T(8,128)(2,1)}, u32[]{:S(2)}) %copy-start.5) | copy-done | bytes 1048600
  1.9 0.0 copy-start.6
  1.9 0.9 %copy-done.6 = bf16[256,512]{1,0:T(8,128)(2,1)S(1)} copy-done((bf16[256,512]{1,0:T(8,128)(2,1)S(1)}, bf16[256,512]{1,0:T(8,128)(2,1)}, u32[]{:S(2)}) %copy-start.6) | copy-done | bytes 262168
  2.9 0.0 copy-start.8
  2.9 0.9 %copy-done.8 = bf16[256,256]{1,0:T(8,128)(2,1)S(1)} copy-done((bf16[256,256]{1,0:T(8,128)(2,1)S(1)}, bf16[256,256]{1,0:T(8,128)(2,1)}, u32[]{:S(2)}) %copy-start.8) | copy-done | bytes 131096
  3.8 0.0 copy-start.9
  3.8 0.9 %copy-done.9 = bf16[256,256]{1,0:T(8,128)(2,1)S(1)} copy-done((bf16[256,256]{1,0:T(8,128)(2,1)S(1)}, bf16[256,256]{1,0:T(8,128)(2,1)}, u32[]{:S(2)}) %copy-start.9) | copy-done | bytes 131096
  4.7 3.4 %time_block.3 = (bf16[16,32,256]{2,1,0:T(8,128)(2,1)S(1)}, bf16[16,32,256]{2,1,0:T(8,128)(2,1)S(1)}) custom-call(s32[1]{0:T(128)} %bitcast.my_ref, bf16[64,32,256]{2,1,0:T(8,128)(2,1)S(1)} %copy-done.5, f32[1,256]{1,0:T(1,128)S(1)} %bitcast.7, bf16[256,256]{1,0:T(8,128)(2,1)S(1)} %copy-done.8, bf16[256,512]{1,0:T(8,128)(2,1)S(1)} %copy-done.6, ...), custom_call_target="tpu_custom_call" | custom-call | flops 805306368 | bytes 1048576 | tf_op jit(solution)/shard_map/time_block/pallas_call | solution.py:128
  8.1 0.0 copy-start
  8.1 3.0 %collective-permute-start.1 = (bf16[16,32,256]{2,1,0:T(8,128)(2,1)S(1)}, bf16[16,32,256]{2,1,0:T(8,128)(2,1)S(1)}, u32[]{:S(2)}, u32[]{:S(2)}) collective-permute-start(bf16[16,32,256]{2,1,0:T(8,128)(2,1)S(1)} %get-tuple-element.17), channel_id=1, source_target_pairs={{0,1},{1,0},{2,3},{3,2},{4,5},{5,4},{6,7},{7,6},{8,9},{9,8},{10,11... | collective-permute-start | bytes 786440 | tf_op jit(solution)/shard_map/ppermute | solution.py:462
  11.1 0.0 copy-start.20
  11.1 5.3 %time_block.2 = (bf16[16,32,256]{2,1,0:T(8,128)(2,1)}, bf16[16,32,256]{2,1,0:T(8,128)(2,1)}) custom-call(s32[1]{0:T(128)} %bitcast.my_ref, bf16[64,32,256]{2,1,0:T(8,128)(2,1)} %x_ref.3, f32[1,256]{1,0:T(1,128)} %bitcast.6, bf16[256,256]{1,0:T(8,128)(2,1)} %wq_ref.3, bf16[256,512]{1,0:T(8,128)(2,1)} %wkv_ref.3, bf16[256,256]{1,0:T(8,128)(2,1)} %wo_ref.3), custom_call_target="tpu_custom_call" | custom-call | flops 805306368 | bytes 1048576 | tf_op jit(solution)/shard_map/time_block/pallas_call | solution.py:128
  16.4 0.0 copy-start.19
  16.4 0.0 collective-permute-start
  16.4 0.6 %copy-done.19 = s32[16,8]{0,1:T(8,128)S(1)} copy-done((s32[16,8]{0,1:T(8,128)S(1)}, s32[16,8]{0,1:T(8,128)}, u32[]{:S(2)}) %copy-start.19) | copy-done | bytes 536
  17.1 0.0 copy-done.20
  17.1 0.1 copy.16
  17.2 0.1 eq.25
  17.3 0.1 compare_convert_fusion.pick_ref
  17.4 0.0 collective-permute-done.1.refs_3_
  17.4 0.0 copy-start.1
  17.4 7.0 %collective-permute-done.refs_2_ = bf16[16,32,256]{2,1,0:T(8,128)(2,1)S(1)} collective-permute-done((bf16[16,32,256]{2,1,0:T(8,128)(2,1)}, bf16[16,32,256]{2,1,0:T(8,128)(2,1)S(1)}, u32[]{:S(2)}, u32[]{:S(2)}) %collective-permute-start) | collective-permute-done | bytes 262176 | tf_op jit(solution)/shard_map/ppermute | solution.py:462
  24.4 1.0 %copy-done.2 = bf16[16,32,256]{2,1,0:T(8,128)(2,1)S(1)} copy-done((bf16[16,32,256]{2,1,0:T(8,128)(2,1)S(1)}, bf16[16,32,256]{2,1,0:T(8,128)(2,1)}, u32[]{:S(2)}) %copy-start.2) | copy-done | bytes 262168
  25.4 1.4 %pick_rows.1 = bf16[64,16,256]{2,1,0:T(8,128)(2,1)} custom-call(bf16[64,128]{1,0:T(8,128)(2,1)S(1)} %compare_convert_fusion.pick_ref, bf16[16,32,256]{2,1,0:T(8,128)(2,1)S(1)} %copy-done.2, bf16[16,32,256]{2,1,0:T(8,128)(2,1)S(1)} %get-tuple-element.15.refs_1_, bf16[16,32,256]{2,1,0:T(8,128)(2,1)S(1)} %collective-permute-done.refs_2_, ...), custom_call_target="tpu_custom_call" | custom-call | tf_op jit(solution)/shard_map/pick_rows/pallas_call | solution.py:169
  26.8 6.1 %all-to-all-start = ((bf16[16,4,16,256]{3,2,1,0:T(8,128)(2,1)}), bf16[16,4,16,256]{3,2,1,0:T(8,128)(2,1)S(1)}, u32[]{:S(2)}, u32[]{:S(2)}) async-start(bf16[16,4,16,256]{3,2,1,0:T(8,128)(2,1)} %bitcast.3), calls=%async_computation | async-start | bytes 1048576 | tf_op jit(solution)/shard_map/all_to_all | solution.py:478
  32.9 0.2 dynamic-slice_reduce_fusion
  33.1 0.7 %copy-done.21 = s32[1,8]{1,0:T(1,128)S(1)} copy-done((s32[1,8]{1,0:T(1,128)S(1)}, s32[1,8]{1,0:T(1,128)}, u32[]{:S(2)}) %copy-start.21) | copy-done | bytes 56
  33.7 0.6 %pad_add_fusion.numbers_ref = s32[17]{0:T(128)} fusion(s32[8]{0:T(128)S(1)} %bitcast.10, s32[8]{0:T(128)S(1)} %dynamic-slice_reduce_fusion, s32[1]{0:T(128)} %bitcast.my_ref), kind=kLoop, calls=%fused_computation.8 | loop fusion | flops 34 | bytes 136 | tf_op jit(solution)/shard_map/concatenate | solution.py:470
  34.3 0.0 copy-done
  34.3 0.0 copy-done.1
  34.3 0.0 copy-done.4
  34.3 0.0 copy-done.3
  34.3 0.0 copy-done.7
  34.4 0.0 copy-done.10
  34.4 0.6 %copy-done.12 = f32[256]{0:T(256)S(1)} copy-done((f32[256]{0:T(256)S(1)}, f32[256]{0:T(256)}, u32[]{:S(2)}) %copy-start.12) | copy-done | bytes 1048
  35.0 7.9 %local_keys.1 = (bf16[16,256,128]{2,1,0:T(8,128)(2,1)S(1)}, bf16[16,256,128]{2,1,0:T(8,128)(2,1)S(1)}, f32[16,8,128]{2,1,0:T(8,128)S(1)}, f32[16,8,128]{2,1,0:T(8,128)S(1)}, bf16[256,256]{1,0:T(8,128)(2,1)S(1)}) custom-call(bf16[16,32,256]{2,1,0:T(8,128)(2,1)S(1)} %copy-done.3, bf16[16,32,256]{2,1,0:T(8,128)(2,1)S(1)} %get-tuple-element.15.refs_1_, ...), custom_call_target="tpu_custom_call" | custom-call | flops 1610612736 | bytes 5242880 | tf_op jit(solution)/shard_map/local_keys/pallas_call | solution.py:224
  42.9 0.0 copy-start.13
  42.9 1.0 %copy-done.13 = bf16[16,256,128]{2,1,0:T(8,128)(2,1)} copy-done((bf16[16,256,128]{2,1,0:T(8,128)(2,1)}, bf16[16,256,128]{2,1,0:T(8,128)(2,1)S(1)}, u32[]{:S(2)}) %copy-start.13) | copy-done | bytes 1048600
  43.9 1.0 %copy-done.14 = bf16[16,256,128]{2,1,0:T(8,128)(2,1)} copy-done((bf16[16,256,128]{2,1,0:T(8,128)(2,1)}, bf16[16,256,128]{2,1,0:T(8,128)(2,1)S(1)}, u32[]{:S(2)}) %copy-start.14) | copy-done | bytes 1048600
  44.9 0.7 %copy-done.15 = bf16[256,256]{1,0:T(8,128)(2,1)} copy-done((bf16[256,256]{1,0:T(8,128)(2,1)}, bf16[256,256]{1,0:T(8,128)(2,1)S(1)}, u32[]{:S(2)}) %copy-start.15) | copy-done | bytes 131096
  45.5 0.6 %copy-done.16 = f32[16,8,128]{2,1,0:T(8,128)} copy-done((f32[16,8,128]{2,1,0:T(8,128)}, f32[16,8,128]{2,1,0:T(8,128)S(1)}, u32[]{:S(2)}) %copy-start.16) | copy-done | bytes 65560
  46.2 0.6 %copy-done.17 = f32[16,8,128]{2,1,0:T(8,128)} copy-done((f32[16,8,128]{2,1,0:T(8,128)}, f32[16,8,128]{2,1,0:T(8,128)S(1)}, u32[]{:S(2)}) %copy-start.17) | copy-done | bytes 65560
  46.8 0.6 all-to-all-done.refs_4_
  47.3 0.8 %copy-done.18 = bf16[16,4,16,256]{3,2,1,0:T(8,128)(2,1)} copy-done((bf16[16,4,16,256]{3,2,1,0:T(8,128)(2,1)}, bf16[16,4,16,256]{3,2,1,0:T(8,128)(2,1)S(1)}, u32[]{:S(2)}) %copy-start.18) | copy-done | bytes 524312
  48.1 10.6 %remote_keys_and_feed_forward.1 = bf16[128,16,256]{2,1,0:T(8,128)(2,1)} custom-call(s32[17]{0:T(128)} %pad_add_fusion.numbers_ref, bf16[16,32,256]{2,1,0:T(8,128)(2,1)} %get-tuple-element.14.refs_0_, bf16[16,32,256]{2,1,0:T(8,128)(2,1)} %copy-done, bf16[16,32,256]{2,1,0:T(8,128)(2,1)} %copy-done.4, bf16[16,32,256]{2,1,0:T(8,128)(2,1)} %copy-done.1, ...), custom_call_target="tpu_custom_call" | custom-call | flops 2415919104 | bytes 6291456 | tf_op jit(solution)/shard_map/remote_keys_and_feed_forward/pallas_call | solution.py:397
  (15 shorter events, 0.1 us)
Async XLA Ops:
  0.0 0.7 %copy-start.11 = (f32[256]{0:T(256)S(1)}, f32[256]{0:T(256)}, u32[]{:S(2)}) copy-start(f32[256]{0:T(256)} %param.16) | copy-start | bytes 3076
  0.7 1.2 %copy-start.5 = (bf16[64,32,256]{2,1,0:T(8,128)(2,1)S(1)}, bf16[64,32,256]{2,1,0:T(8,128)(2,1)}, u32[]{:S(2)}) copy-start(bf16[64,32,256]{2,1,0:T(8,128)(2,1)} %x_ref.3) | copy-start | bytes 3145732
  1.9 0.9 %copy-start.6 = (bf16[256,512]{1,0:T(8,128)(2,1)S(1)}, bf16[256,512]{1,0:T(8,128)(2,1)}, u32[]{:S(2)}) copy-start(bf16[256,512]{1,0:T(8,128)(2,1)} %wkv_ref.3) | copy-start | bytes 786436
  2.9 0.9 %copy-start.8 = (bf16[256,256]{1,0:T(8,128)(2,1)S(1)}, bf16[256,256]{1,0:T(8,128)(2,1)}, u32[]{:S(2)}) copy-start(bf16[256,256]{1,0:T(8,128)(2,1)} %wq_ref.3) | copy-start | bytes 393220
  3.8 0.9 %copy-start.9 = (bf16[256,256]{1,0:T(8,128)(2,1)S(1)}, bf16[256,256]{1,0:T(8,128)(2,1)}, u32[]{:S(2)}) copy-start(bf16[256,256]{1,0:T(8,128)(2,1)} %wo_ref.3) | copy-start | bytes 393220
  8.1 26.2 %copy-start = (bf16[16,32,256]{2,1,0:T(8,128)(2,1)}, bf16[16,32,256]{2,1,0:T(8,128)(2,1)S(1)}, u32[]{:S(2)}) copy-start(bf16[16,32,256]{2,1,0:T(8,128)(2,1)S(1)} %get-tuple-element.15.refs_1_) | copy-start | bytes 786436
  8.1 9.3 %collective-permute-start.1 = (bf16[16,32,256]{2,1,0:T(8,128)(2,1)S(1)}, bf16[16,32,256]{2,1,0:T(8,128)(2,1)S(1)}, u32[]{:S(2)}, u32[]{:S(2)}) collective-permute-start(bf16[16,32,256]{2,1,0:T(8,128)(2,1)S(1)} %get-tuple-element.17), channel_id=1, source_target_pairs={{0,1},{1,0},{2,3},{3,2},{4,5},{5,4},{6,7},{7,6},{8,9},{9,8},{10,11... | collective-permute-start | bytes 786440 | tf_op jit(solution)/shard_map/ppermute | solution.py:462
  11.1 6.0 %copy-start.20 = (s32[16,8,4]{0,2,1:T(4,128)S(1)}, s32[16,8,4]{0,2,1:T(4,128)}, u32[]{:S(2)}) copy-start(s32[16,8,4]{0,2,1:T(4,128)} %param.29) | copy-start | bytes 6148
  16.4 0.7 %copy-start.19 = (s32[16,8]{0,1:T(8,128)S(1)}, s32[16,8]{0,1:T(8,128)}, u32[]{:S(2)}) copy-start(s32[16,8]{0,1:T(8,128)} %param.27) | copy-start | bytes 1540
  16.4 8.0 %collective-permute-start = (bf16[16,32,256]{2,1,0:T(8,128)(2,1)}, bf16[16,32,256]{2,1,0:T(8,128)(2,1)S(1)}, u32[]{:S(2)}, u32[]{:S(2)}) collective-permute-start(bf16[16,32,256]{2,1,0:T(8,128)(2,1)} %get-tuple-element.16), channel_id=1, source_target_pairs={{0,1},{1,0},{2,3},{3,2},{4,5},{5,4},{6,7},{7,6},{8,9},{9,8},{10,11... | collective-permute-start | bytes 786440 | tf_op jit(solution)/shard_map/ppermute | solution.py:462
  17.4 16.9 %copy-start.1 = (bf16[16,32,256]{2,1,0:T(8,128)(2,1)}, bf16[16,32,256]{2,1,0:T(8,128)(2,1)S(1)}, u32[]{:S(2)}) copy-start(bf16[16,32,256]{2,1,0:T(8,128)(2,1)S(1)} %collective-permute-done.1.refs_3_) | copy-start | bytes 786436
  24.4 10.0 %copy-start.4 = (bf16[16,32,256]{2,1,0:T(8,128)(2,1)}, bf16[16,32,256]{2,1,0:T(8,128)(2,1)S(1)}, u32[]{:S(2)}) copy-start(bf16[16,32,256]{2,1,0:T(8,128)(2,1)S(1)} %collective-permute-done.refs_2_) | copy-start | bytes 786436
  24.4 1.0 %copy-start.2 = (bf16[16,32,256]{2,1,0:T(8,128)(2,1)S(1)}, bf16[16,32,256]{2,1,0:T(8,128)(2,1)}, u32[]{:S(2)}) copy-start(bf16[16,32,256]{2,1,0:T(8,128)(2,1)} %get-tuple-element.14.refs_0_) | copy-start | bytes 786436
  26.8 7.6 %copy-start.3 = (bf16[16,32,256]{2,1,0:T(8,128)(2,1)S(1)}, bf16[16,32,256]{2,1,0:T(8,128)(2,1)}, u32[]{:S(2)}) copy-start(bf16[16,32,256]{2,1,0:T(8,128)(2,1)} %get-tuple-element.14.refs_0_) | copy-start | bytes 786436
  26.8 7.6 %copy-start.7 = (bf16[256,512]{1,0:T(8,128)(2,1)S(1)}, bf16[256,512]{1,0:T(8,128)(2,1)}, u32[]{:S(2)}) copy-start(bf16[256,512]{1,0:T(8,128)(2,1)} %refs_11_.1) | copy-start | bytes 786436
  26.8 7.6 %copy-start.10 = (bf16[256,256]{1,0:T(8,128)(2,1)S(1)}, bf16[256,256]{1,0:T(8,128)(2,1)}, u32[]{:S(2)}) copy-start(bf16[256,256]{1,0:T(8,128)(2,1)} %refs_5_.1) | copy-start | bytes 393220
  26.8 20.5 %all-to-all-start = ((bf16[16,4,16,256]{3,2,1,0:T(8,128)(2,1)}), bf16[16,4,16,256]{3,2,1,0:T(8,128)(2,1)S(1)}, u32[]{:S(2)}, u32[]{:S(2)}) async-start(bf16[16,4,16,256]{3,2,1,0:T(8,128)(2,1)} %bitcast.3), calls=%async_computation | async-start | bytes 1048576 | tf_op jit(solution)/shard_map/all_to_all | solution.py:478
  33.0 0.7 %copy-start.21 = (s32[1,8]{1,0:T(1,128)S(1)}, s32[1,8]{1,0:T(1,128)}, u32[]{:S(2)}) copy-start(s32[1,8]{1,0:T(1,128)} %param.28) | copy-start | bytes 100
  34.3 0.7 %copy-start.12 = (f32[256]{0:T(256)S(1)}, f32[256]{0:T(256)}, u32[]{:S(2)}) copy-start(f32[256]{0:T(256)} %param.20) | copy-start | bytes 3076
  42.9 1.0 %copy-start.13 = (bf16[16,256,128]{2,1,0:T(8,128)(2,1)}, bf16[16,256,128]{2,1,0:T(8,128)(2,1)S(1)}, u32[]{:S(2)}) copy-start(bf16[16,256,128]{2,1,0:T(8,128)(2,1)S(1)} %get-tuple-element.20.refs_9_) | copy-start | bytes 3145732
  43.9 1.0 %copy-start.14 = (bf16[16,256,128]{2,1,0:T(8,128)(2,1)}, bf16[16,256,128]{2,1,0:T(8,128)(2,1)S(1)}, u32[]{:S(2)}) copy-start(bf16[16,256,128]{2,1,0:T(8,128)(2,1)S(1)} %get-tuple-element.21.refs_10_) | copy-start | bytes 3145732
  44.9 0.7 %copy-start.15 = (bf16[256,256]{1,0:T(8,128)(2,1)}, bf16[256,256]{1,0:T(8,128)(2,1)S(1)}, u32[]{:S(2)}) copy-start(bf16[256,256]{1,0:T(8,128)(2,1)S(1)} %get-tuple-element.22.refs_12_) | copy-start | bytes 393220
  45.5 0.6 %copy-start.16 = (f32[16,8,128]{2,1,0:T(8,128)}, f32[16,8,128]{2,1,0:T(8,128)S(1)}, u32[]{:S(2)}) copy-start(f32[16,8,128]{2,1,0:T(8,128)S(1)} %get-tuple-element.18.refs_7_) | copy-start | bytes 196612
  46.2 0.6 %copy-start.17 = (f32[16,8,128]{2,1,0:T(8,128)}, f32[16,8,128]{2,1,0:T(8,128)S(1)}, u32[]{:S(2)}) copy-start(f32[16,8,128]{2,1,0:T(8,128)S(1)} %get-tuple-element.19.refs_8_) | copy-start | bytes 196612
  47.3 0.8 %copy-start.18 = (bf16[16,4,16,256]{3,2,1,0:T(8,128)(2,1)}, bf16[16,4,16,256]{3,2,1,0:T(8,128)(2,1)S(1)}, u32[]{:S(2)}) copy-start(bf16[16,4,16,256]{3,2,1,0:T(8,128)(2,1)S(1)} %all-to-all-done.refs_4_) | copy-start | bytes 1572868

commit v4 on v3

--- a/solution.py
+++ b/solution.py
@@ -14,10 +14,10 @@
 EPSILON = 1e-06
 NEG = -1e30
 SCALE = math.log2(math.e) / math.sqrt(HEAD)
+SHARES = (1, 1, 2)
 F32 = jnp.float32
 BF16 = jnp.bfloat16
-VMEM_LARGE = 60 * 1024 * 1024
-VMEM_SMALL = 24 * 1024 * 1024
+VMEM_LIMIT = 28 * 1024 * 1024
 
 
 def dot(a, b):
@@ -114,6 +114,8 @@
 
 def time_block(tokens, my, gain, wq, wkv, wo, first, count, split):
     steps, width = tokens.shape[1:]
+    if first == 0:
+        tokens, gain, wq, wkv, wo = (pltpu.with_memory_space_constraint(a, pltpu.HBM) for a in (tokens, gain, wq, wkv, wo))
     sb = min(16, count)
     rows = sb * steps
     full = lambda a: pl.BlockSpec(a.shape, lambda i, *_: (0,) * a.ndim)
@@ -141,7 +143,7 @@
             out_specs=out_specs,
             scratch_shapes=[pltpu.VMEM((rows, width), BF16)] * 5 + extra,
         ),
-        compiler_params=pltpu.CompilerParams(vmem_limit_bytes=VMEM_LARGE if first == 0 else VMEM_SMALL),
+        compiler_params=pltpu.CompilerParams(vmem_limit_bytes=VMEM_LIMIT),
         cost_estimate=pl.CostEstimate(
             flops=count * steps * width * width * 12, bytes_accessed=count * steps * width * 4, transcendentals=0
         ),
@@ -170,7 +172,7 @@
         functools.partial(pick_kernel, len(pieces)),
         out_shape=jax.ShapeDtypeStruct((wanted, steps, width), BF16),
         scratch_shapes=[pltpu.VMEM((steps, wanted, width), BF16)],
-        compiler_params=pltpu.CompilerParams(vmem_limit_bytes=VMEM_SMALL),
+        compiler_params=pltpu.CompilerParams(vmem_limit_bytes=VMEM_LIMIT),
         name="pick_rows",
     )(pick, *pieces)
 
@@ -224,11 +226,11 @@
     return pl.pallas_call(
         functools.partial(local_kernel, len(pieces)),
         out_shape=[
-            jax.ShapeDtypeStruct((steps, width, block), BF16),
-            jax.ShapeDtypeStruct((steps, width, block), BF16),
-            jax.ShapeDtypeStruct((steps, H, block), F32),
-            jax.ShapeDtypeStruct((steps, H, block), F32),
-            jax.ShapeDtypeStruct((width, width), BF16),
+            pltpu.HBM((steps, width, block), BF16),
+            pltpu.HBM((steps, width, block), BF16),
+            pltpu.HBM((steps, H, block), F32),
+            pltpu.HBM((steps, H, block), F32),
+            pltpu.HBM((width, width), BF16),
         ],
         grid=(steps // tb,),
         in_specs=[per_t(p.shape[1], width) for p in pieces] + [full(gain), full(wq), full(wkv)],
@@ -240,7 +242,7 @@
             pl.BlockSpec((width, width), lambda i: (0, 0)),
         ],
         scratch_shapes=[pltpu.VMEM((width, width), BF16)],
-        compiler_params=pltpu.CompilerParams(vmem_limit_bytes=VMEM_SMALL),
+        compiler_params=pltpu.CompilerParams(vmem_limit_bytes=VMEM_LIMIT),
         cost_estimate=pl.CostEstimate(
             flops=steps * block * width * width * 12, bytes_accessed=steps * block * width * 10, transcendentals=0
         ),
@@ -254,15 +256,15 @@
     return half + half * jnp.tanh(inner)
 
 
-def finish_kernel(n, split, tb, numbers_ref, *refs):
+def finish_kernel(n, split, sb, numbers_ref, *refs):
     pieces = refs[:n]
-    in_hbm, gain_ref, gain_ffn_ref, ltop_ref, lsum_ref = refs[n : n + 5]
+    in_ref, gain_hbm, gain_ffn_hbm, ltop_hbm, lsum_hbm = refs[n : n + 5]
     qt_hbm, lctx_hbm, wkv_hbm, wvt_hbm, wo_hbm, w_in_hbm, w_out_hbm, out_hbm = refs[n + 5 : n + 13]
-    x_s, raw_s, rn_s, rk_s, ctx_s, y_s, out_s, qt_s, lctx_s, wk_s, wvt_s, wo_s, w_in_s, w_out_s, sems, out_sems = refs[n + 13 :]
+    (x_s, raw_s, rn_s, rk_s, ctx_s, out_s, qt_s, lctx_s, wk_s, wvt_s, wo_s, w_in_s, w_out_s, gain_ref, gain_ffn_ref,
+     ltop_ref, lsum_ref, sems, out_sems) = refs[n + 13 :]
     steps, width, block = qt_s.shape
     remote = rn_s.shape[1]
     slots = remote // REMOTE_SENSORS
-    chunks = steps // tb
     count = [0]
 
     def fetch(src, dst):
@@ -271,15 +273,8 @@
         copy.start()
         return copy
 
-    if split:
-        raw_in = [
-            fetch(in_hbm.at[numbers_ref[1 + j]], raw_s.at[pl.ds(j * REMOTE_SENSORS, REMOTE_SENSORS)]) for j in range(slots)
-        ]
-    else:
-        raw_in = [fetch(in_hbm, raw_s)]
-    first_in = [fetch(wkv_hbm.at[:, pl.ds(0, width)], wk_s), fetch(wvt_hbm, wvt_s)]
-    chunk = [pl.ds(c * tb, tb) for c in range(chunks)]
-    qt_in = [fetch(qt_hbm.at[here], qt_s.at[here]) for here in chunk]
+    first_in = [fetch(gain_hbm, gain_ref), fetch(wkv_hbm.at[:, pl.ds(0, width)], wk_s), fetch(wvt_hbm, wvt_s)]
+    score_in = [fetch(qt_hbm, qt_s), fetch(ltop_hbm, ltop_ref), fetch(lsum_hbm, lsum_ref)]
 
     order = swap16() if split else None
     lane_head = lax.broadcasted_iota(jnp.int32, (1, 128), 1) // HEAD
@@ -295,91 +290,101 @@
         live = jnp.where(slot == j, numbers_ref[1 + slots + j], live)
     live = live > 0
 
-    for copy in raw_in + first_in:
+    for copy in first_in:
         copy.wait()
-    lctx_in, x_in = [], []
-    for here in chunk:
-        lctx_in.append(fetch(lctx_hbm.at[here], lctx_s.at[here]))
-        place, x_c = 0, []
-        for p in pieces:
-            x_c.append(fetch(p.at[here], x_s.at[here, pl.ds(place, p.shape[1])]))
-            place += p.shape[1]
-        x_in.append(x_c)
-    wo_in = fetch(wo_hbm, wo_s)
-    ffn_in = [fetch(w_in_hbm, w_in_s), fetch(w_out_hbm, w_out_s)]
+    merge_in = [fetch(lctx_hbm, lctx_s)]
+    x_in, place = [fetch(wo_hbm, wo_s)], 0
+    for p in pieces:
+        x_in.append(fetch(p, x_s.at[:, pl.ds(place, p.shape[1])]))
+        place += p.shape[1]
+    ffn_in = [fetch(gain_ffn_hbm, gain_ffn_ref), fetch(w_in_hbm, w_in_s), fetch(w_out_hbm, w_out_s)]
     if split:
+        for j in range(slots):
+            raw_s[j * REMOTE_SENSORS : (j + 1) * REMOTE_SENSORS] = in_ref[numbers_ref[1 + j]]
         for b in range(remote // 16):
             rows = raw_s[b * 16 : (b + 1) * 16].reshape(256, width)
             rn_s[:, b * 16 : (b + 1) * 16, :] = dot(order, rows).astype(BF16).reshape(16, 16, width)
         raw = rn_s[...]
     else:
-        raw = raw_s[...]
+        raw = in_ref[...]
     normed = rms(raw.reshape(steps * remote, width).astype(F32), gain_ref[...])
     rn_s[...] = normed.reshape(steps, remote, width)
     rk_s[...] = dot(normed, wk_s[...]).astype(BF16).reshape(steps, remote, width)
 
-    for c in range(chunks):
-        ts = range(c * tb, (c + 1) * tb)
-        qt_in[c].wait()
-        keys = []
-        for t in ts:
-            rk = rk_s[t]
-            spread = []
-            for h in range(H):
-                half = h * HEAD // 128
-                part = rk[:, half * 128 : (half + 1) * 128] * heads[h % (128 // HEAD)]
-                spread.append(jnp.concatenate([part, none] if half == 0 else [none, part], axis=1))
-            keys.append(jnp.concatenate(spread, axis=0))
-        scores = [dot(k, qt_s[t]).reshape(H, remote, block) for k, t in zip(keys, ts)]
-        values = []
-        for t in ts:
-            tiled = jnp.concatenate([rn_s[t]] * H, axis=0)
-            values.append(dot_nt(wvt_s[...], tiled).astype(BF16) * own_block)
-        weights, keeps = [], []
-        for s, t in zip(scores, ts):
-            masked = jnp.where(live[None], s, NEG)
-            ltop = ltop_ref[t]
-            top = jnp.maximum(jnp.max(masked, axis=1), ltop)
-            e = jnp.exp2((masked - top[:, None, :]) * SCALE)
-            keep = jnp.exp2((ltop - top) * SCALE)
-            inverse = 1.0 / (jnp.sum(e, axis=1) + lsum_ref[t] * keep)
-            keeps.append(keep * inverse)
-            weights.append((e * inverse[:, None, :]).astype(BF16).reshape(H * remote, block))
-        far = [dot(v, w).reshape(H, HEAD, block) for v, w in zip(values, weights)]
-        lctx_in[c].wait()
-        for i, t in enumerate(ts):
-            merged = lctx_s[t].astype(F32).reshape(H, HEAD, block) * keeps[i][:, None, :] + far[i]
-            ctx_s[:, i * block : (i + 1) * block] = merged.reshape(width, block).astype(BF16)
-        if c == 0:
-            wo_in.wait()
-        for copy in x_in[c]:
-            copy.wait()
-        x = x_s[c * tb : (c + 1) * tb].reshape(tb * block, width)
-        after = x.astype(F32) + dot(ctx_s[...].T, wo_s[...])
-        normed = rms(after, gain_ffn_ref[...])
-        if c == 0:
-            for copy in ffn_in:
-                copy.wait()
-        hidden = gelu(dot(normed, w_in_s[...])).astype(BF16)
-        y_s[c * tb : (c + 1) * tb] = (after + dot(hidden, w_out_s[...])).astype(BF16).reshape(tb, block, width)
-
+    for copy in score_in:
+        copy.wait()
+    keys = []
+    for t in range(steps):
+        rk = rk_s[t]
+        spread = []
+        for h in range(H):
+            half = h * HEAD // 128
+            part = rk[:, half * 128 : (half + 1) * 128] * heads[h % (128 // HEAD)]
+            spread.append(jnp.concatenate([part, none] if half == 0 else [none, part], axis=1))
+        keys.append(jnp.concatenate(spread, axis=0))
+    scores = [dot(keys[t], qt_s[t]).reshape(H, remote, block) for t in range(steps)]
+    values = []
+    for t in range(steps):
+        tiled = jnp.concatenate([rn_s[t]] * H, axis=0)
+        values.append(dot_nt(wvt_s[...], tiled).astype(BF16) * own_block)
+    weights, keeps = [], []
+    for t in range(steps):
+        masked = jnp.where(live[None], scores[t], NEG)
+        ltop = ltop_ref[t]
+        top = jnp.maximum(jnp.max(masked, axis=1), ltop)
+        e = jnp.exp2((masked - top[:, None, :]) * SCALE)
+        keep = jnp.exp2((ltop - top) * SCALE)
+        inverse = 1.0 / (jnp.sum(e, axis=1) + lsum_ref[t] * keep)
+        keeps.append(keep * inverse)
+        weights.append((e * inverse[:, None, :]).astype(BF16).reshape(H * remote, block))
+    far = [dot(values[t], weights[t]).reshape(H, HEAD, block) for t in range(steps)]
+    for copy in merge_in:
+        copy.wait()
+    for t in range(steps):
+        merged = lctx_s[t].astype(F32).reshape(H, HEAD, block) * keeps[t][:, None, :] + far[t]
+        ctx_s[t] = merged.reshape(width, block).astype(BF16).T
+
+    for copy in x_in + ffn_in:
+        copy.wait()
+    tile = width
+    tiles = w_in_s.shape[1] // tile
+    work = [(first, n) for first in range(0, block, sb) for n in range(tiles)]
+    ready, total, copies = {}, {}, []
+
+    def open_rows(first):
+        rows = lambda ref: ref[:, first : first + sb, :].reshape(steps * sb, width)
+        after = rows(x_s).astype(F32) + dot(rows(ctx_s), wo_s[...])
+        total[first] = after
+        ready[first] = rms(after, gain_ffn_ref[...])
+
+    def up(first, n):
+        return dot(ready[first], w_in_s[:, n * tile : (n + 1) * tile])
+
+    open_rows(0)
+    upper = up(*work[0])
+    for k, (first, n) in enumerate(work):
+        if n == 0 and first + sb < block:
+            open_rows(first + sb)
+        later = up(*work[k + 1]) if k + 1 < len(work) else None
+        total[first] = total[first] + dot(gelu(upper).astype(BF16), w_out_s[n * tile : (n + 1) * tile, :])
+        upper = later
+        if n < tiles - 1:
+            continue
+        y = total[first].astype(BF16).reshape(steps, sb, width)
+        if not split:
+            out_s[:, first : first + sb, :] = y
+            continue
+        for b in range(sb // 16):
+            turned = dot(order, y[:, b * 16 : (b + 1) * 16].reshape(256, width)).astype(BF16)
+            out_s[first + b * 16 : first + (b + 1) * 16] = turned.reshape(16, steps, width)
+        half = block // 2
+        owner = numbers_ref[0] if first < half else 1 - numbers_ref[0]
+        place = out_hbm.at[pl.ds(owner * half + first % half, sb)]
+        copies.append(pltpu.make_async_copy(out_s.at[pl.ds(first, sb)], place, out_sems.at[first // sb]))
+        copies[-1].start()
     if not split:
-        copy = pltpu.make_async_copy(y_s, out_hbm, out_sems.at[0])
-        copy.start()
-        copy.wait()
-        return
-    mine = numbers_ref[0]
-    half = block // 2
-    copies = []
-    for b in range(block // 16):
-        first = b * 16
-        owner = mine if first < half else 1 - mine
-        rows = y_s[:, first : first + 16, :].reshape(256, width)
-        out_s[first : first + 16] = dot(order, rows).astype(BF16).reshape(16, 16, width)
-        place = out_hbm.at[pl.ds(owner * half + first % half, 16)]
-        copy = pltpu.make_async_copy(out_s.at[pl.ds(first, 16)], place, out_sems.at[b])
-        copy.start()
-        copies.append(copy)
+        copies.append(pltpu.make_async_copy(out_s, out_hbm, out_sems.at[0]))
+        copies[-1].start()
     for copy in copies:
         copy.wait()
 
@@ -388,25 +393,24 @@
     qt, lctx, ltop, lsum, wvt = local
     steps, width, block = qt.shape
     remote = (numbers.shape[0] - 1) // 2 * REMOTE_SENSORS
-    tb = min(16, steps)
-    vmem = pl.BlockSpec(memory_space=pltpu.VMEM)
+    sb = 32
     hbm = pl.BlockSpec(memory_space=pl.ANY)
-    chunks = steps // tb
-    n_copies = (remote // REMOTE_SENSORS if split else 1) + 5 + chunks * (2 + len(pieces))
+    n_copies = 12 + len(pieces)
+    far = (*pieces, incoming, gain, gain_ffn, ltop, lsum, qt, lctx, wkv, wvt, wo, w_in, w_out)
+    far = [a if a is incoming else pltpu.with_memory_space_constraint(a, pltpu.HBM) for a in far]
     buffer = lambda *shape: pltpu.VMEM(shape, BF16)
     return pl.pallas_call(
-        functools.partial(finish_kernel, len(pieces), split, tb),
+        functools.partial(finish_kernel, len(pieces), split, sb),
         out_shape=jax.ShapeDtypeStruct((block, steps, width) if split else (steps, block, width), BF16),
-        in_specs=[pl.BlockSpec(memory_space=pltpu.SMEM)] + [hbm] * (len(pieces) + 1) + [vmem] * 4 + [hbm] * 7,
+        in_specs=[pl.BlockSpec(memory_space=pltpu.SMEM)] + [pl.BlockSpec(memory_space=pltpu.VMEM) if a is incoming else hbm for a in far],
         out_specs=hbm,
         scratch_shapes=[
             buffer(steps, block, width),
-            buffer(remote, steps, width) if split else buffer(steps, remote, width),
+            buffer(remote, steps, width),
             buffer(steps, remote, width),
             buffer(steps, remote, width),
-            buffer(width, tb * block),
             buffer(steps, block, width),
-            buffer(block, steps, width) if split else buffer(8, 128),
+            buffer(block, steps, width) if split else buffer(steps, block, width),
             buffer(steps, width, block),
             buffer(steps, width, block),
             buffer(width, width),
@@ -414,15 +418,19 @@
             buffer(*wo.shape),
             buffer(*w_in.shape),
             buffer(*w_out.shape),
+            pltpu.VMEM(gain.shape, F32),
+            pltpu.VMEM(gain_ffn.shape, F32),
+            pltpu.VMEM(ltop.shape, F32),
+            pltpu.VMEM(lsum.shape, F32),
             pltpu.SemaphoreType.DMA((n_copies,)),
-            pltpu.SemaphoreType.DMA((max(block // 16, 1),)),
+            pltpu.SemaphoreType.DMA((block // sb,)),
         ],
-        compiler_params=pltpu.CompilerParams(vmem_limit_bytes=VMEM_LARGE),
+        compiler_params=pltpu.CompilerParams(vmem_limit_bytes=VMEM_LIMIT),
         cost_estimate=pl.CostEstimate(
             flops=steps * block * width * width * 18, bytes_accessed=steps * block * width * 12, transcendentals=0
         ),
         name="remote_keys_and_feed_forward",
-    )(numbers, *pieces, incoming, gain, gain_ffn, ltop, lsum, qt, lctx, wkv, wvt, wo, w_in, w_out)
+    )(numbers, *far)
 
 
 def local(
@@ -451,18 +459,20 @@
     gain_time, gain_graph, gain_ffn = (g.reshape(1, width) for g in (gain_time, gain_graph, gain_ffn))
     mine = lax.axis_index("tm").astype(jnp.int32)
     block_index = lax.axis_index("sensor")
-    time = functools.partial(time_block, tokens, mine.reshape(1), gain_time, wq_time, wkv_time, wo_time)
+    time = lambda x, *where: time_block(x, mine.reshape(1), gain_time, wq_time, wkv_time, wo_time, *where)
     if split:
-        chunks = 2
-        size = sensors_here // chunks
         kept, got = [], []
-        for c in range(chunks):
-            keep, send = time(c * size, size, True)
+        first = 0
+        for share in SHARES:
+            size = sensors_here * share // sum(SHARES)
+            keep, send = time(tokens, first, size, True)
+            tokens, send = lax.optimization_barrier((tokens, send))
             kept.append(keep)
             got.append(lax.ppermute(send, "tm", [(0, 1), (1, 0)]))
+            first += size
         pieces = kept + got
     else:
-        whole = lax.all_to_all(time(0, sensors_here, False), "tm", split_axis=1, concat_axis=0, tiled=True)
+        whole = lax.all_to_all(time(tokens, 0, sensors_here, False), "tm", split_axis=1, concat_axis=0, tiled=True)
         pieces = [whole.transpose(1, 0, 2)]
     matches = (neighbour_blocks == block_index).astype(jnp.int32)
     wanted = jnp.sum(matches[:, :, None] * neighbour_rows, axis=1).reshape(-1)

time: 59.4 us -> 51.5 us (0.87)
  local copies, waits for them, and re-layouts: 12.7 us -> 1.69 us
  waiting for transfers between devices: 7.55 us -> 10.2 us
  starting transfers between devices: 9.13 us -> 11.3 us
  Pallas kernels: 28.6 us -> 27.5 us
    unnamed x44 -> x34, local copies, waits for them, and re-layouts: 12.3 us -> 1.33 us
    all_to_all x1, waiting for transfers between devices: 0.55 us -> 4.19 us  [local(): lax.all_to_all(outgoing, 'sensor', split_axis=0, concat_axis=0, tiled=True)]
    ppermute x2 -> x3, starting transfers between devices: 3.05 us -> 5.17 us  [local(): got.append(lax.ppermute(send, 'tm', [(0, 1), (1, 0)]))]
    ppermute x2 -> x3, waiting for transfers between devices: 7 us -> 5.99 us  [local(): got.append(lax.ppermute(send, 'tm', [(0, 1), (1, 0)]))]
    pallas_call x2 -> x3, Pallas kernels: 8.7 us -> 8.05 us  [time_block(): pl.pallas_call(functools.partial(time_kernel, split), out_shape=out_shape...]
  transfers between devices with their start and end apart: 3 -> 4, of which waited for: 2 -> 2; matrix products, arithmetic and copies ran while one was open for 2% -> 1% of each run, Pallas kernels for 22% -> 27%
where the time goes in v4:
time: 51.5 us; the launch traced here: 51.2 us
  Pallas kernels  27.5 us (53%)
  starting transfers between devices  11.3 us (22%)
  waiting for transfers between devices  10.2 us (20%)
  local copies, waits for them, and re-layouts  1.69 us (3%)
    pallas_call x1, Pallas kernels, finish(): pl.pallas_call(functools.partial(finish_kernel, len(pieces), split, sb),...  9.44 us
    pallas_call x1, Pallas kernels, local_part(): pl.pallas_call(functools.partial(local_kernel, len(pieces)), out_shape=[p...  8.66 us
    pallas_call x3, Pallas kernels, time_block(): pl.pallas_call(functools.partial(time_kernel, split), out_shape=out_shape...  8.05 us
    all_to_all x1, starting transfers between devices, local(): lax.all_to_all(outgoing, 'sensor', split_axis=0, concat_axis=0, tiled=True)  6.08 us
    ppermute x3, waiting for transfers between devices, local(): got.append(lax.ppermute(send, 'tm', [(0, 1), (1, 0)]))  5.99 us
    ppermute x3, starting transfers between devices, local(): got.append(lax.ppermute(send, 'tm', [(0, 1), (1, 0)]))  5.17 us
    all_to_all x1, waiting for transfers between devices, local(): lax.all_to_all(outgoing, 'sensor', split_axis=0, concat_axis=0, tiled=True)  4.19 us
    pallas_call x1, Pallas kernels, pick_rows(): pl.pallas_call(functools.partial(pick_kernel, len(pieces)), out_shape=jax...  1.35 us
  transfers between devices with their start and end apart: 4, of which 2 were waited for; matrix products, arithmetic and copies ran while one was open for 1% of the time, Pallas kernels for 27%

profile of v4, /device:TPU:0, one launch (start us, length us, event | category | flops | bytes accessed | tf_op | source)
XLA Modules:
  0.0 51.2 jit_solution(16799935089900457609)
XLA Ops:
  0.0 0.0 copy-start
  0.0 0.0 copy-start.1
  0.0 0.0 copy-start.2
  0.0 0.0 copy-start.3
  0.0 2.9 %time_block.3 = (bf16[16,16,256]{2,1,0:T(8,128)(2,1)S(1)}, bf16[16,16,256]{2,1,0:T(8,128)(2,1)S(1)}) custom-call(s32[1]{0:T(128)} %bitcast.my_ref, bf16[64,32,256]{2,1,0:T(8,128)(2,1)} %x_ref.3, f32[1,256]{1,0:T(1,128)} %bitcast.6, bf16[256,256]{1,0:T(8,128)(2,1)} %wq_ref.5, bf16[256,512]{1,0:T(8,128)(2,1)} %wkv_ref.5, bf16[256,256]{1,0:T(8,128)(2,1)} %wo_ref.5), custom_call_target="tpu_custom_call" | custom-call | flops 402653184 | bytes 524288 | tf_op jit(solution)/shard_map/time_block/pallas_call | solution.py:130
  2.9 0.0 copy-start.6
  2.9 0.0 copy-start.10
  3.0 3.0 %collective-permute-start = (bf16[16,16,256]{2,1,0:T(8,128)(2,1)S(1)}, bf16[16,16,256]{2,1,0:T(8,128)(2,1)S(1)}, u32[]{:S(2)}, u32[]{:S(2)}) collective-permute-start(bf16[16,16,256]{2,1,0:T(8,128)(2,1)S(1)} %get-tuple-element.28), channel_id=1, source_target_pairs={{0,1},{1,0},{2,3},{3,2},{4,5},{5,4},{6,7},{7,6},{8,9},{9,8},{10,11... | collective-permute-start | bytes 393224 | tf_op jit(solution)/shard_map/ppermute | solution.py:471
  6.0 0.0 copy-done
  6.0 0.0 copy-done.1
  6.0 0.0 copy-done.2
  6.0 0.0 copy-done.3
  6.0 0.0 copy-done.10
  6.0 1.7 %time_block.4 = (bf16[16,16,256]{2,1,0:T(8,128)(2,1)S(1)}, bf16[16,16,256]{2,1,0:T(8,128)(2,1)S(1)}) custom-call(s32[1]{0:T(128)} %bitcast.my_ref, bf16[64,32,256]{2,1,0:T(8,128)(2,1)S(1)} %copy-done, f32[1,256]{1,0:T(1,128)S(1)} %bitcast.7, bf16[256,256]{1,0:T(8,128)(2,1)S(1)} %copy-done.2, bf16[256,512]{1,0:T(8,128)(2,1)S(1)} %copy-done.1, ...), custom_call_target="tpu_custom_call" | custom-call | flops 402653184 | bytes 524288 | tf_op jit(solution)/shard_map/time_block/pallas_call | solution.py:130
  7.7 0.0 copy-start.8
  7.7 0.7 %collective-permute-start.1 = (bf16[16,16,256]{2,1,0:T(8,128)(2,1)S(1)}, bf16[16,16,256]{2,1,0:T(8,128)(2,1)S(1)}, u32[]{:S(2)}, u32[]{:S(2)}) collective-permute-start(bf16[16,16,256]{2,1,0:T(8,128)(2,1)S(1)} %get-tuple-element.29), channel_id=1, source_target_pairs={{0,1},{1,0},{2,3},{3,2},{4,5},{5,4},{6,7},{7,6},{8,9},{9,8},{10,11... | collective-permute-start | bytes 393224 | tf_op jit(solution)/shard_map/ppermute | solution.py:471
  8.4 0.0 copy-start.15
  8.4 3.4 %time_block.5 = (bf16[16,32,256]{2,1,0:T(8,128)(2,1)S(1)}, bf16[16,32,256]{2,1,0:T(8,128)(2,1)S(1)}) custom-call(s32[1]{0:T(128)} %bitcast.my_ref, bf16[64,32,256]{2,1,0:T(8,128)(2,1)S(1)} %copy-done, f32[1,256]{1,0:T(1,128)S(1)} %bitcast.8, bf16[256,256]{1,0:T(8,128)(2,1)S(1)} %copy-done.2, bf16[256,512]{1,0:T(8,128)(2,1)S(1)} %copy-done.1, ...), custom_call_target="tpu_custom_call" | custom-call | flops 805306368 | bytes 1048576 | tf_op jit(solution)/shard_map/time_block/pallas_call | solution.py:130
  11.8 0.0 copy-start.4
  11.8 0.0 copy-start.14
  11.8 1.5 %collective-permute-start.2 = (bf16[16,32,256]{2,1,0:T(8,128)(2,1)S(1)}, bf16[16,32,256]{2,1,0:T(8,128)(2,1)S(1)}, u32[]{:S(2)}, u32[]{:S(2)}) collective-permute-start(bf16[16,32,256]{2,1,0:T(8,128)(2,1)S(1)} %get-tuple-element.31), channel_id=1, source_target_pairs={{0,1},{1,0},{2,3},{3,2},{4,5},{5,4},{6,7},{7,6},{8,9},{9,8},{10,11... | collective-permute-start | bytes 786440 | tf_op jit(solution)/shard_map/ppermute | solution.py:471
  13.3 0.0 copy-done.14
  13.3 0.0 copy-done.15
  13.4 0.1 copy.16
  13.5 0.1 eq.25
  13.6 0.1 compare_convert_fusion.pick_ref
  13.6 0.0 collective-permute-done.refs_3_
  13.7 0.0 copy-start.7
  13.7 0.0 collective-permute-done.1.refs_4_
  13.7 0.0 copy-start.9
  13.7 6.0 %collective-permute-done.2.refs_5_ = bf16[16,32,256]{2,1,0:T(8,128)(2,1)S(1)} collective-permute-done((bf16[16,32,256]{2,1,0:T(8,128)(2,1)S(1)}, bf16[16,32,256]{2,1,0:T(8,128)(2,1)S(1)}, u32[]{:S(2)}, u32[]{:S(2)}) %collective-permute-start.2) | collective-permute-done | bytes 262176 | tf_op jit(solution)/shard_map/ppermute | solution.py:471
  19.7 1.3 %pick_rows.1 = bf16[64,16,256]{2,1,0:T(8,128)(2,1)} custom-call(bf16[64,128]{1,0:T(8,128)(2,1)S(1)} %compare_convert_fusion.pick_ref, bf16[16,16,256]{2,1,0:T(8,128)(2,1)S(1)} %get-tuple-element.21.refs_0_, bf16[16,16,256]{2,1,0:T(8,128)(2,1)S(1)} %get-tuple-element.24.refs_1_, bf16[16,32,256]{2,1,0:T(8,128)(2,1)S(1)} %get-tuple-element.27.refs_2_, ...), custom_call_target="tpu_custom_call" | custom-call | tf_op jit(solution)/shard_map/pick_rows/pallas_call | solution.py:171
  21.0 6.1 %all-to-all-start = ((bf16[16,4,16,256]{3,2,1,0:T(8,128)(2,1)}), bf16[16,4,16,256]{3,2,1,0:T(8,128)(2,1)S(1)}, u32[]{:S(2)}, u32[]{:S(2)}) async-start(bf16[16,4,16,256]{3,2,1,0:T(8,128)(2,1)} %bitcast.3), calls=%async_computation | async-start | bytes 1048576 | tf_op jit(solution)/shard_map/all_to_all | solution.py:488
  27.1 0.2 dynamic-slice_reduce_fusion
  27.3 0.7 %copy-done.16 = s32[1,8]{1,0:T(1,128)S(1)} copy-done((s32[1,8]{1,0:T(1,128)S(1)}, s32[1,8]{1,0:T(1,128)}, u32[]{:S(2)}) %copy-start.16) | copy-done | bytes 56
  28.0 0.1 pad_add_fusion.numbers_ref
  28.0 0.0 copy-done.6
  28.0 0.0 copy-done.8
  28.0 0.0 copy-done.4
  28.0 0.0 copy-done.7
  28.1 0.0 copy-done.9
  28.1 0.0 copy-done.5
  28.1 0.0 copy-done.11
  28.1 0.0 copy-done.12
  28.1 0.6 %copy-done.13 = f32[256]{0:T(256)S(1)} copy-done((f32[256]{0:T(256)S(1)}, f32[256]{0:T(256)}, u32[]{:S(2)}) %copy-start.13) | copy-done | bytes 1048
  28.7 8.7 %local_keys.1 = (bf16[16,256,128]{2,1,0:T(8,128)(2,1)}, bf16[16,256,128]{2,1,0:T(8,128)(2,1)}, f32[16,8,128]{2,1,0:T(8,128)}, f32[16,8,128]{2,1,0:T(8,128)}, bf16[256,256]{1,0:T(8,128)(2,1)}) custom-call(bf16[16,16,256]{2,1,0:T(8,128)(2,1)S(1)} %get-tuple-element.21.refs_0_, bf16[16,16,256]{2,1,0:T(8,128)(2,1)S(1)} %get-tuple-element.24.refs_1_, ...), custom_call_target="tpu_custom_call" | custom-call | flops 1610612736 | bytes 5242880 | tf_op jit(solution)/shard_map/local_keys/pallas_call | solution.py:226
  37.4 4.2 %all-to-all-done.refs_6_ = bf16[16,4,16,256]{3,2,1,0:T(8,128)(2,1)S(1)} async-done(((bf16[16,4,16,256]{3,2,1,0:T(8,128)(2,1)}), bf16[16,4,16,256]{3,2,1,0:T(8,128)(2,1)S(1)}, u32[]{:S(2)}, u32[]{:S(2)}) %all-to-all-start) | async-done | bytes 524320 | tf_op jit(solution)/shard_map/all_to_all | solution.py:488
  41.6 9.4 %remote_keys_and_feed_forward.1 = bf16[128,16,256]{2,1,0:T(8,128)(2,1)} custom-call(s32[17]{0:T(128)S(1)} %pad_add_fusion.numbers_ref, bf16[16,16,256]{2,1,0:T(8,128)(2,1)} %copy-done.6, bf16[16,16,256]{2,1,0:T(8,128)(2,1)} %copy-done.8, bf16[16,32,256]{2,1,0:T(8,128)(2,1)} %copy-done.4, bf16[16,16,256]{2,1,0:T(8,128)(2,1)} %copy-done.7, ...), custom_call_target="tpu_custom_call" | custom-call | flops 2415919104 | bytes 6291456 | tf_op jit(solution)/shard_map/remote_keys_and_feed_forward/pallas_call | solution.py:402
  (8 shorter events, 0.0 us)
Async XLA Ops:
  0.0 6.0 %copy-start = (bf16[64,32,256]{2,1,0:T(8,128)(2,1)S(1)}, bf16[64,32,256]{2,1,0:T(8,128)(2,1)}, u32[]{:S(2)}) copy-start(bf16[64,32,256]{2,1,0:T(8,128)(2,1)} %x_ref.3) | copy-start | bytes 3145732
  0.0 6.0 %copy-start.1 = (bf16[256,512]{1,0:T(8,128)(2,1)S(1)}, bf16[256,512]{1,0:T(8,128)(2,1)}, u32[]{:S(2)}) copy-start(bf16[256,512]{1,0:T(8,128)(2,1)} %wkv_ref.5) | copy-start | bytes 786436
  0.0 6.0 %copy-start.2 = (bf16[256,256]{1,0:T(8,128)(2,1)S(1)}, bf16[256,256]{1,0:T(8,128)(2,1)}, u32[]{:S(2)}) copy-start(bf16[256,256]{1,0:T(8,128)(2,1)} %wq_ref.5) | copy-start | bytes 393220
  0.0 6.0 %copy-start.3 = (bf16[256,256]{1,0:T(8,128)(2,1)S(1)}, bf16[256,256]{1,0:T(8,128)(2,1)}, u32[]{:S(2)}) copy-start(bf16[256,256]{1,0:T(8,128)(2,1)} %wo_ref.5) | copy-start | bytes 393220
  2.9 25.1 %copy-start.6 = (bf16[16,16,256]{2,1,0:T(8,128)(2,1)}, bf16[16,16,256]{2,1,0:T(8,128)(2,1)S(1)}, u32[]{:S(2)}) copy-start(bf16[16,16,256]{2,1,0:T(8,128)(2,1)S(1)} %get-tuple-element.21.refs_0_) | copy-start | bytes 393220
  2.9 3.0 %copy-start.10 = (f32[256]{0:T(256)S(1)}, f32[256]{0:T(256)}, u32[]{:S(2)}) copy-start(f32[256]{0:T(256)} %param.16) | copy-start | bytes 3076
  3.0 10.7 %collective-permute-start = (bf16[16,16,256]{2,1,0:T(8,128)(2,1)S(1)}, bf16[16,16,256]{2,1,0:T(8,128)(2,1)S(1)}, u32[]{:S(2)}, u32[]{:S(2)}) collective-permute-start(bf16[16,16,256]{2,1,0:T(8,128)(2,1)S(1)} %get-tuple-element.28), channel_id=1, source_target_pairs={{0,1},{1,0},{2,3},{3,2},{4,5},{5,4},{6,7},{7,6},{8,9},{9,8},{10,11... | collective-permute-start | bytes 393224 | tf_op jit(solution)/shard_map/ppermute | solution.py:471
  7.7 20.3 %copy-start.8 = (bf16[16,16,256]{2,1,0:T(8,128)(2,1)}, bf16[16,16,256]{2,1,0:T(8,128)(2,1)S(1)}, u32[]{:S(2)}) copy-start(bf16[16,16,256]{2,1,0:T(8,128)(2,1)S(1)} %get-tuple-element.24.refs_1_) | copy-start | bytes 393220
  7.7 5.9 %collective-permute-start.1 = (bf16[16,16,256]{2,1,0:T(8,128)(2,1)S(1)}, bf16[16,16,256]{2,1,0:T(8,128)(2,1)S(1)}, u32[]{:S(2)}, u32[]{:S(2)}) collective-permute-start(bf16[16,16,256]{2,1,0:T(8,128)(2,1)S(1)} %get-tuple-element.29), channel_id=1, source_target_pairs={{0,1},{1,0},{2,3},{3,2},{4,5},{5,4},{6,7},{7,6},{8,9},{9,8},{10,11... | collective-permute-start | bytes 393224 | tf_op jit(solution)/shard_map/ppermute | solution.py:471
  8.4 5.0 %copy-start.15 = (s32[16,8,4]{0,2,1:T(4,128)S(1)}, s32[16,8,4]{0,2,1:T(4,128)}, u32[]{:S(2)}) copy-start(s32[16,8,4]{0,2,1:T(4,128)} %param.29) | copy-start | bytes 6148
  11.8 16.2 %copy-start.4 = (bf16[16,32,256]{2,1,0:T(8,128)(2,1)}, bf16[16,32,256]{2,1,0:T(8,128)(2,1)S(1)}, u32[]{:S(2)}) copy-start(bf16[16,32,256]{2,1,0:T(8,128)(2,1)S(1)} %get-tuple-element.27.refs_2_) | copy-start | bytes 786436
  11.8 1.5 %copy-start.14 = (s32[16,8]{0,1:T(8,128)S(1)}, s32[16,8]{0,1:T(8,128)}, u32[]{:S(2)}) copy-start(s32[16,8]{0,1:T(8,128)} %param.27) | copy-start | bytes 1540
  11.8 7.8 %collective-permute-start.2 = (bf16[16,32,256]{2,1,0:T(8,128)(2,1)S(1)}, bf16[16,32,256]{2,1,0:T(8,128)(2,1)S(1)}, u32[]{:S(2)}, u32[]{:S(2)}) collective-permute-start(bf16[16,32,256]{2,1,0:T(8,128)(2,1)S(1)} %get-tuple-element.31), channel_id=1, source_target_pairs={{0,1},{1,0},{2,3},{3,2},{4,5},{5,4},{6,7},{7,6},{8,9},{9,8},{10,11... | collective-permute-start | bytes 786440 | tf_op jit(solution)/shard_map/ppermute | solution.py:471
  13.7 14.4 %copy-start.7 = (bf16[16,16,256]{2,1,0:T(8,128)(2,1)}, bf16[16,16,256]{2,1,0:T(8,128)(2,1)S(1)}, u32[]{:S(2)}) copy-start(bf16[16,16,256]{2,1,0:T(8,128)(2,1)S(1)} %collective-permute-done.refs_3_) | copy-start | bytes 393220
  13.7 14.4 %copy-start.9 = (bf16[16,16,256]{2,1,0:T(8,128)(2,1)}, bf16[16,16,256]{2,1,0:T(8,128)(2,1)S(1)}, u32[]{:S(2)}) copy-start(bf16[16,16,256]{2,1,0:T(8,128)(2,1)S(1)} %collective-permute-done.1.refs_4_) | copy-start | bytes 393220
  19.7 8.4 %copy-start.5 = (bf16[16,32,256]{2,1,0:T(8,128)(2,1)}, bf16[16,32,256]{2,1,0:T(8,128)(2,1)S(1)}, u32[]{:S(2)}) copy-start(bf16[16,32,256]{2,1,0:T(8,128)(2,1)S(1)} %collective-permute-done.2.refs_5_) | copy-start | bytes 786436
  21.0 7.1 %copy-start.11 = (bf16[256,512]{1,0:T(8,128)(2,1)S(1)}, bf16[256,512]{1,0:T(8,128)(2,1)}, u32[]{:S(2)}) copy-start(bf16[256,512]{1,0:T(8,128)(2,1)} %refs_13_.1) | copy-start | bytes 786436
  21.0 7.1 %copy-start.12 = (bf16[256,256]{1,0:T(8,128)(2,1)S(1)}, bf16[256,256]{1,0:T(8,128)(2,1)}, u32[]{:S(2)}) copy-start(bf16[256,256]{1,0:T(8,128)(2,1)} %refs_7_.1) | copy-start | bytes 393220
  21.0 20.5 %all-to-all-start = ((bf16[16,4,16,256]{3,2,1,0:T(8,128)(2,1)}), bf16[16,4,16,256]{3,2,1,0:T(8,128)(2,1)S(1)}, u32[]{:S(2)}, u32[]{:S(2)}) async-start(bf16[16,4,16,256]{3,2,1,0:T(8,128)(2,1)} %bitcast.3), calls=%async_computation | async-start | bytes 1048576 | tf_op jit(solution)/shard_map/all_to_all | solution.py:488
  27.3 0.7 %copy-start.16 = (s32[1,8]{1,0:T(1,128)S(1)}, s32[1,8]{1,0:T(1,128)}, u32[]{:S(2)}) copy-start(s32[1,8]{1,0:T(1,128)} %param.28) | copy-start | bytes 100
  28.0 0.7 %copy-start.13 = (f32[256]{0:T(256)S(1)}, f32[256]{0:T(256)}, u32[]{:S(2)}) copy-start(f32[256]{0:T(256)} %param.20) | copy-start | bytes 3076

commit v5 on v4

--- a/solution.py
+++ b/solution.py
@@ -14,7 +14,7 @@
 EPSILON = 1e-06
 NEG = -1e30
 SCALE = math.log2(math.e) / math.sqrt(HEAD)
-SHARES = (1, 1, 2)
+SHARES = (1, 1, 1, 1)
 F32 = jnp.float32
 BF16 = jnp.bfloat16
 VMEM_LIMIT = 28 * 1024 * 1024

time: 51.5 us -> 50.2 us (0.975)
  waiting for transfers between devices: 10.2 us -> 7.59 us
  local copies, waits for them, and re-layouts: 1.69 us -> 2.35 us
  starting transfers between devices: 11.3 us -> 11.9 us
    ppermute x3 -> x4, waiting for transfers between devices: 5.99 us -> 3.41 us  [local(): got.append(lax.ppermute(send, 'tm', [(0, 1), (1, 0)]))]
    unnamed x34 -> x38, local copies, waits for them, and re-layouts: 1.33 us -> 1.99 us
    ppermute x3 -> x4, starting transfers between devices: 5.17 us -> 5.83 us  [local(): got.append(lax.ppermute(send, 'tm', [(0, 1), (1, 0)]))]
    pallas_call x3 -> x4, Pallas kernels: 8.05 us -> 8.02 us  [time_block(): pl.pallas_call(functools.partial(time_kernel, split), out_shape=out_shape...]
  transfers between devices with their start and end apart: 4 -> 5, of which waited for: 2 -> 3; matrix products, arithmetic and copies ran while one was open for 1% -> 1% of each run, Pallas kernels for 27% -> 28%
where the time goes in v5:
time: 50.2 us; the launch traced here: 49.9 us
  Pallas kernels  27.5 us (55%)
  starting transfers between devices  11.9 us (24%)
  waiting for transfers between devices  7.59 us (15%)
  local copies, waits for them, and re-layouts  2.35 us (5%)
    pallas_call x1, Pallas kernels, finish(): pl.pallas_call(functools.partial(finish_kernel, len(pieces), split, sb),...  9.46 us
    pallas_call x1, Pallas kernels, local_part(): pl.pallas_call(functools.partial(local_kernel, len(pieces)), out_shape=[p...  8.67 us
    pallas_call x4, Pallas kernels, time_block(): pl.pallas_call(functools.partial(time_kernel, split), out_shape=out_shape...  8.02 us
    all_to_all x1, starting transfers between devices, local(): lax.all_to_all(outgoing, 'sensor', split_axis=0, concat_axis=0, tiled=True)  6.07 us
    ppermute x4, starting transfers between devices, local(): got.append(lax.ppermute(send, 'tm', [(0, 1), (1, 0)]))  5.83 us
    all_to_all x1, waiting for transfers between devices, local(): lax.all_to_all(outgoing, 'sensor', split_axis=0, concat_axis=0, tiled=True)  4.18 us
    ppermute x4, waiting for transfers between devices, local(): got.append(lax.ppermute(send, 'tm', [(0, 1), (1, 0)]))  3.41 us
    unnamed x38, local copies, waits for them, and re-layouts  1.99 us
  transfers between devices with their start and end apart: 5, of which 3 were waited for; matrix products, arithmetic and copies ran while one was open for 1% of the time, Pallas kernels for 28%

profile of v5, /device:TPU:0, one launch (start us, length us, event | category | flops | bytes accessed | tf_op | source)
XLA Modules:
  0.0 49.9 jit_solution(16516920156155186805)
XLA Ops:
  0.0 2.9 %time_block.4 = (bf16[16,16,256]{2,1,0:T(8,128)(2,1)S(1)}, bf16[16,16,256]{2,1,0:T(8,128)(2,1)S(1)}) custom-call(s32[1]{0:T(128)} %bitcast.my_ref, bf16[64,32,256]{2,1,0:T(8,128)(2,1)} %x_ref.4, f32[1,256]{1,0:T(1,128)} %bitcast.6, bf16[256,256]{1,0:T(8,128)(2,1)} %wq_ref.7, bf16[256,512]{1,0:T(8,128)(2,1)} %wkv_ref.7, bf16[256,256]{1,0:T(8,128)(2,1)} %wo_ref.7), custom_call_target="tpu_custom_call" | custom-call | flops 402653184 | bytes 524288 | tf_op jit(solution)/shard_map/time_block/pallas_call | solution.py:130
  2.9 0.0 copy-start.4
  2.9 0.0 copy-start.12
  3.0 3.0 %collective-permute-start = (bf16[16,16,256]{2,1,0:T(8,128)(2,1)S(1)}, bf16[16,16,256]{2,1,0:T(8,128)(2,1)S(1)}, u32[]{:S(2)}, u32[]{:S(2)}) collective-permute-start(bf16[16,16,256]{2,1,0:T(8,128)(2,1)S(1)} %get-tuple-element.35), channel_id=1, source_target_pairs={{0,1},{1,0},{2,3},{3,2},{4,5},{5,4},{6,7},{7,6},{8,9},{9,8},{10,11... | collective-permute-start | bytes 393224 | tf_op jit(solution)/shard_map/ppermute | solution.py:471
  6.0 0.0 copy-done
  6.0 0.0 copy-done.1
  6.0 0.0 copy-done.2
  6.0 0.0 copy-done.3
  6.0 0.0 copy-done.12
  6.0 1.7 %time_block.5 = (bf16[16,16,256]{2,1,0:T(8,128)(2,1)S(1)}, bf16[16,16,256]{2,1,0:T(8,128)(2,1)S(1)}) custom-call(s32[1]{0:T(128)} %bitcast.my_ref, bf16[64,32,256]{2,1,0:T(8,128)(2,1)S(1)} %copy-done, f32[1,256]{1,0:T(1,128)S(1)} %bitcast.7, bf16[256,256]{1,0:T(8,128)(2,1)S(1)} %copy-done.2, bf16[256,512]{1,0:T(8,128)(2,1)S(1)} %copy-done.1, ...), custom_call_target="tpu_custom_call" | custom-call | flops 402653184 | bytes 524288 | tf_op jit(solution)/shard_map/time_block/pallas_call | solution.py:130
  7.7 0.0 copy-start.6
  7.7 0.7 %collective-permute-start.1 = (bf16[16,16,256]{2,1,0:T(8,128)(2,1)S(1)}, bf16[16,16,256]{2,1,0:T(8,128)(2,1)S(1)}, u32[]{:S(2)}, u32[]{:S(2)}) collective-permute-start(bf16[16,16,256]{2,1,0:T(8,128)(2,1)S(1)} %get-tuple-element.36), channel_id=1, source_target_pairs={{0,1},{1,0},{2,3},{3,2},{4,5},{5,4},{6,7},{7,6},{8,9},{9,8},{10,11... | collective-permute-start | bytes 393224 | tf_op jit(solution)/shard_map/ppermute | solution.py:471
  8.4 1.7 %time_block.6 = (bf16[16,16,256]{2,1,0:T(8,128)(2,1)S(1)}, bf16[16,16,256]{2,1,0:T(8,128)(2,1)S(1)}) custom-call(s32[1]{0:T(128)} %bitcast.my_ref, bf16[64,32,256]{2,1,0:T(8,128)(2,1)S(1)} %copy-done, f32[1,256]{1,0:T(1,128)S(1)} %bitcast.8, bf16[256,256]{1,0:T(8,128)(2,1)S(1)} %copy-done.2, bf16[256,512]{1,0:T(8,128)(2,1)S(1)} %copy-done.1, ...), custom_call_target="tpu_custom_call" | custom-call | flops 402653184 | bytes 524288 | tf_op jit(solution)/shard_map/time_block/pallas_call | solution.py:130
  10.1 0.0 copy-start.8
  10.1 1.5 %collective-permute-start.2 = (bf16[16,16,256]{2,1,0:T(8,128)(2,1)S(1)}, bf16[16,16,256]{2,1,0:T(8,128)(2,1)S(1)}, u32[]{:S(2)}, u32[]{:S(2)}) collective-permute-start(bf16[16,16,256]{2,1,0:T(8,128)(2,1)S(1)} %get-tuple-element.37), channel_id=1, source_target_pairs={{0,1},{1,0},{2,3},{3,2},{4,5},{5,4},{6,7},{7,6},{8,9},{9,8},{10,11... | collective-permute-start | bytes 393224 | tf_op jit(solution)/shard_map/ppermute | solution.py:471
  11.6 1.7 %time_block.7 = (bf16[16,16,256]{2,1,0:T(8,128)(2,1)S(1)}, bf16[16,16,256]{2,1,0:T(8,128)(2,1)S(1)}) custom-call(s32[1]{0:T(128)} %bitcast.my_ref, bf16[64,32,256]{2,1,0:T(8,128)(2,1)S(1)} %copy-done, f32[1,256]{1,0:T(1,128)S(1)} %bitcast.9, bf16[256,256]{1,0:T(8,128)(2,1)S(1)} %copy-done.2, bf16[256,512]{1,0:T(8,128)(2,1)S(1)} %copy-done.1, ...), custom_call_target="tpu_custom_call" | custom-call | flops 402653184 | bytes 524288 | tf_op jit(solution)/shard_map/time_block/pallas_call | solution.py:130
  13.3 0.0 copy-start.10
  13.3 0.7 %collective-permute-start.3 = (bf16[16,16,256]{2,1,0:T(8,128)(2,1)S(1)}, bf16[16,16,256]{2,1,0:T(8,128)(2,1)S(1)}, u32[]{:S(2)}, u32[]{:S(2)}) collective-permute-start(bf16[16,16,256]{2,1,0:T(8,128)(2,1)S(1)} %get-tuple-element.39), channel_id=1, source_target_pairs={{0,1},{1,0},{2,3},{3,2},{4,5},{5,4},{6,7},{7,6},{8,9},{9,8},{10,11... | collective-permute-start | bytes 393224 | tf_op jit(solution)/shard_map/ppermute | solution.py:471
  14.0 0.7 %copy-done.16 = s32[16,8]{0,1:T(8,128)S(1)} copy-done((s32[16,8]{0,1:T(8,128)S(1)}, s32[16,8]{0,1:T(8,128)}, u32[]{:S(2)}) %copy-start.16) | copy-done | bytes 536
  14.7 0.0 copy-done.17
  14.7 0.1 copy.16
  14.8 0.1 eq.25
  14.8 0.1 compare_convert_fusion.pick_ref
  14.9 0.0 collective-permute-done.refs_4_
  14.9 0.0 copy-start.5
  14.9 0.0 collective-permute-done.1.refs_5_
  15.0 0.0 copy-start.7
  15.0 1.2 %collective-permute-done.2.refs_6_ = bf16[16,16,256]{2,1,0:T(8,128)(2,1)S(1)} collective-permute-done((bf16[16,16,256]{2,1,0:T(8,128)(2,1)S(1)}, bf16[16,16,256]{2,1,0:T(8,128)(2,1)S(1)}, u32[]{:S(2)}, u32[]{:S(2)}) %collective-permute-start.2) | collective-permute-done | bytes 131104 | tf_op jit(solution)/shard_map/ppermute | solution.py:471
  16.1 2.2 %collective-permute-done.3.refs_7_ = bf16[16,16,256]{2,1,0:T(8,128)(2,1)S(1)} collective-permute-done((bf16[16,16,256]{2,1,0:T(8,128)(2,1)S(1)}, bf16[16,16,256]{2,1,0:T(8,128)(2,1)S(1)}, u32[]{:S(2)}, u32[]{:S(2)}) %collective-permute-start.3) | collective-permute-done | bytes 131104 | tf_op jit(solution)/shard_map/ppermute | solution.py:471
  18.4 1.3 %pick_rows.1 = bf16[64,16,256]{2,1,0:T(8,128)(2,1)} custom-call(bf16[64,128]{1,0:T(8,128)(2,1)S(1)} %compare_convert_fusion.pick_ref, bf16[16,16,256]{2,1,0:T(8,128)(2,1)S(1)} %get-tuple-element.25.refs_0_, bf16[16,16,256]{2,1,0:T(8,128)(2,1)S(1)} %get-tuple-element.28.refs_1_, bf16[16,16,256]{2,1,0:T(8,128)(2,1)S(1)} %get-tuple-element.31.refs_2_, ...), custom_call_target="tpu_custom_call" | custom-call | tf_op jit(solution)/shard_map/pick_rows/pallas_call | solution.py:171
  19.7 6.1 %all-to-all-start = ((bf16[16,4,16,256]{3,2,1,0:T(8,128)(2,1)}), bf16[16,4,16,256]{3,2,1,0:T(8,128)(2,1)S(1)}, u32[]{:S(2)}, u32[]{:S(2)}) async-start(bf16[16,4,16,256]{3,2,1,0:T(8,128)(2,1)} %bitcast.3), calls=%async_computation | async-start | bytes 1048576 | tf_op jit(solution)/shard_map/all_to_all | solution.py:488
  25.8 0.2 dynamic-slice_reduce_fusion
  26.0 0.7 %copy-done.18 = s32[1,8]{1,0:T(1,128)S(1)} copy-done((s32[1,8]{1,0:T(1,128)S(1)}, s32[1,8]{1,0:T(1,128)}, u32[]{:S(2)}) %copy-start.18) | copy-done | bytes 56
  26.7 0.1 pad_add_fusion.numbers_ref
  26.7 0.0 copy-done.4
  26.7 0.0 copy-done.6
  26.7 0.0 copy-done.8
  26.7 0.0 copy-done.10
  26.8 0.0 copy-done.5
  26.8 0.0 copy-done.7
  26.8 0.0 copy-done.9
  26.8 0.0 copy-done.11
  26.8 0.0 copy-done.13
  26.8 0.0 copy-done.14
  26.8 0.6 %copy-done.15 = f32[256]{0:T(256)S(1)} copy-done((f32[256]{0:T(256)S(1)}, f32[256]{0:T(256)}, u32[]{:S(2)}) %copy-start.15) | copy-done | bytes 1048
  27.4 8.7 %local_keys.1 = (bf16[16,256,128]{2,1,0:T(8,128)(2,1)}, bf16[16,256,128]{2,1,0:T(8,128)(2,1)}, f32[16,8,128]{2,1,0:T(8,128)}, f32[16,8,128]{2,1,0:T(8,128)}, bf16[256,256]{1,0:T(8,128)(2,1)}) custom-call(bf16[16,16,256]{2,1,0:T(8,128)(2,1)S(1)} %get-tuple-element.25.refs_0_, bf16[16,16,256]{2,1,0:T(8,128)(2,1)S(1)} %get-tuple-element.28.refs_1_, ...), custom_call_target="tpu_custom_call" | custom-call | flops 1610612736 | bytes 5242880 | tf_op jit(solution)/shard_map/local_keys/pallas_call | solution.py:226
  36.1 4.2 %all-to-all-done.refs_8_ = bf16[16,4,16,256]{3,2,1,0:T(8,128)(2,1)S(1)} async-done(((bf16[16,4,16,256]{3,2,1,0:T(8,128)(2,1)}), bf16[16,4,16,256]{3,2,1,0:T(8,128)(2,1)S(1)}, u32[]{:S(2)}, u32[]{:S(2)}) %all-to-all-start) | async-done | bytes 524320 | tf_op jit(solution)/shard_map/all_to_all | solution.py:488
  40.3 9.5 %remote_keys_and_feed_forward.1 = bf16[128,16,256]{2,1,0:T(8,128)(2,1)} custom-call(s32[17]{0:T(128)S(1)} %pad_add_fusion.numbers_ref, bf16[16,16,256]{2,1,0:T(8,128)(2,1)} %copy-done.4, bf16[16,16,256]{2,1,0:T(8,128)(2,1)} %copy-done.6, bf16[16,16,256]{2,1,0:T(8,128)(2,1)} %copy-done.8, bf16[16,16,256]{2,1,0:T(8,128)(2,1)} %copy-done.10, ...), custom_call_target="tpu_custom_call" | custom-call | flops 2415919104 | bytes 6291456 | tf_op jit(solution)/shard_map/remote_keys_and_feed_forward/pallas_call | solution.py:402
  (15 shorter events, 0.1 us)
Async XLA Ops:
  0.0 6.0 %copy-start = (bf16[64,32,256]{2,1,0:T(8,128)(2,1)S(1)}, bf16[64,32,256]{2,1,0:T(8,128)(2,1)}, u32[]{:S(2)}) copy-start(bf16[64,32,256]{2,1,0:T(8,128)(2,1)} %x_ref.4) | copy-start | bytes 3145732
  0.0 6.0 %copy-start.1 = (bf16[256,512]{1,0:T(8,128)(2,1)S(1)}, bf16[256,512]{1,0:T(8,128)(2,1)}, u32[]{:S(2)}) copy-start(bf16[256,512]{1,0:T(8,128)(2,1)} %wkv_ref.7) | copy-start | bytes 786436
  0.0 6.0 %copy-start.2 = (bf16[256,256]{1,0:T(8,128)(2,1)S(1)}, bf16[256,256]{1,0:T(8,128)(2,1)}, u32[]{:S(2)}) copy-start(bf16[256,256]{1,0:T(8,128)(2,1)} %wq_ref.7) | copy-start | bytes 393220
  0.0 6.0 %copy-start.3 = (bf16[256,256]{1,0:T(8,128)(2,1)S(1)}, bf16[256,256]{1,0:T(8,128)(2,1)}, u32[]{:S(2)}) copy-start(bf16[256,256]{1,0:T(8,128)(2,1)} %wo_ref.7) | copy-start | bytes 393220
  2.9 23.8 %copy-start.4 = (bf16[16,16,256]{2,1,0:T(8,128)(2,1)}, bf16[16,16,256]{2,1,0:T(8,128)(2,1)S(1)}, u32[]{:S(2)}) copy-start(bf16[16,16,256]{2,1,0:T(8,128)(2,1)S(1)} %get-tuple-element.25.refs_0_) | copy-start | bytes 393220
  2.9 3.0 %copy-start.12 = (f32[256]{0:T(256)S(1)}, f32[256]{0:T(256)}, u32[]{:S(2)}) copy-start(f32[256]{0:T(256)} %param.16) | copy-start | bytes 3076
  3.0 12.0 %collective-permute-start = (bf16[16,16,256]{2,1,0:T(8,128)(2,1)S(1)}, bf16[16,16,256]{2,1,0:T(8,128)(2,1)S(1)}, u32[]{:S(2)}, u32[]{:S(2)}) collective-permute-start(bf16[16,16,256]{2,1,0:T(8,128)(2,1)S(1)} %get-tuple-element.35), channel_id=1, source_target_pairs={{0,1},{1,0},{2,3},{3,2},{4,5},{5,4},{6,7},{7,6},{8,9},{9,8},{10,11... | collective-permute-start | bytes 393224 | tf_op jit(solution)/shard_map/ppermute | solution.py:471
  7.7 19.0 %copy-start.6 = (bf16[16,16,256]{2,1,0:T(8,128)(2,1)}, bf16[16,16,256]{2,1,0:T(8,128)(2,1)S(1)}, u32[]{:S(2)}) copy-start(bf16[16,16,256]{2,1,0:T(8,128)(2,1)S(1)} %get-tuple-element.28.refs_1_) | copy-start | bytes 393220
  7.7 7.2 %collective-permute-start.1 = (bf16[16,16,256]{2,1,0:T(8,128)(2,1)S(1)}, bf16[16,16,256]{2,1,0:T(8,128)(2,1)S(1)}, u32[]{:S(2)}, u32[]{:S(2)}) collective-permute-start(bf16[16,16,256]{2,1,0:T(8,128)(2,1)S(1)} %get-tuple-element.36), channel_id=1, source_target_pairs={{0,1},{1,0},{2,3},{3,2},{4,5},{5,4},{6,7},{7,6},{8,9},{9,8},{10,11... | collective-permute-start | bytes 393224 | tf_op jit(solution)/shard_map/ppermute | solution.py:471
  10.1 16.7 %copy-start.8 = (bf16[16,16,256]{2,1,0:T(8,128)(2,1)}, bf16[16,16,256]{2,1,0:T(8,128)(2,1)S(1)}, u32[]{:S(2)}) copy-start(bf16[16,16,256]{2,1,0:T(8,128)(2,1)S(1)} %get-tuple-element.31.refs_2_) | copy-start | bytes 393220
  10.1 6.0 %collective-permute-start.2 = (bf16[16,16,256]{2,1,0:T(8,128)(2,1)S(1)}, bf16[16,16,256]{2,1,0:T(8,128)(2,1)S(1)}, u32[]{:S(2)}, u32[]{:S(2)}) collective-permute-start(bf16[16,16,256]{2,1,0:T(8,128)(2,1)S(1)} %get-tuple-element.37), channel_id=1, source_target_pairs={{0,1},{1,0},{2,3},{3,2},{4,5},{5,4},{6,7},{7,6},{8,9},{9,8},{10,11... | collective-permute-start | bytes 393224 | tf_op jit(solution)/shard_map/ppermute | solution.py:471
  11.6 3.1 %copy-start.17 = (s32[16,8,4]{0,2,1:T(4,128)S(1)}, s32[16,8,4]{0,2,1:T(4,128)}, u32[]{:S(2)}) copy-start(s32[16,8,4]{0,2,1:T(4,128)} %param.29) | copy-start | bytes 6148
  13.3 13.5 %copy-start.10 = (bf16[16,16,256]{2,1,0:T(8,128)(2,1)}, bf16[16,16,256]{2,1,0:T(8,128)(2,1)S(1)}, u32[]{:S(2)}) copy-start(bf16[16,16,256]{2,1,0:T(8,128)(2,1)S(1)} %get-tuple-element.34.refs_3_) | copy-start | bytes 393220
  13.3 5.1 %collective-permute-start.3 = (bf16[16,16,256]{2,1,0:T(8,128)(2,1)S(1)}, bf16[16,16,256]{2,1,0:T(8,128)(2,1)S(1)}, u32[]{:S(2)}, u32[]{:S(2)}) collective-permute-start(bf16[16,16,256]{2,1,0:T(8,128)(2,1)S(1)} %get-tuple-element.39), channel_id=1, source_target_pairs={{0,1},{1,0},{2,3},{3,2},{4,5},{5,4},{6,7},{7,6},{8,9},{9,8},{10,11... | collective-permute-start | bytes 393224 | tf_op jit(solution)/shard_map/ppermute | solution.py:471
  14.0 0.7 %copy-start.16 = (s32[16,8]{0,1:T(8,128)S(1)}, s32[16,8]{0,1:T(8,128)}, u32[]{:S(2)}) copy-start(s32[16,8]{0,1:T(8,128)} %param.27) | copy-start | bytes 1540
  14.9 11.8 %copy-start.5 = (bf16[16,16,256]{2,1,0:T(8,128)(2,1)}, bf16[16,16,256]{2,1,0:T(8,128)(2,1)S(1)}, u32[]{:S(2)}) copy-start(bf16[16,16,256]{2,1,0:T(8,128)(2,1)S(1)} %collective-permute-done.refs_4_) | copy-start | bytes 393220
  15.0 11.8 %copy-start.7 = (bf16[16,16,256]{2,1,0:T(8,128)(2,1)}, bf16[16,16,256]{2,1,0:T(8,128)(2,1)S(1)}, u32[]{:S(2)}) copy-start(bf16[16,16,256]{2,1,0:T(8,128)(2,1)S(1)} %collective-permute-done.1.refs_5_) | copy-start | bytes 393220
  16.1 10.6 %copy-start.9 = (bf16[16,16,256]{2,1,0:T(8,128)(2,1)}, bf16[16,16,256]{2,1,0:T(8,128)(2,1)S(1)}, u32[]{:S(2)}) copy-start(bf16[16,16,256]{2,1,0:T(8,128)(2,1)S(1)} %collective-permute-done.2.refs_6_) | copy-start | bytes 393220
  18.4 8.4 %copy-start.11 = (bf16[16,16,256]{2,1,0:T(8,128)(2,1)}, bf16[16,16,256]{2,1,0:T(8,128)(2,1)S(1)}, u32[]{:S(2)}) copy-start(bf16[16,16,256]{2,1,0:T(8,128)(2,1)S(1)} %collective-permute-done.3.refs_7_) | copy-start | bytes 393220
  19.7 7.1 %copy-start.13 = (bf16[256,512]{1,0:T(8,128)(2,1)S(1)}, bf16[256,512]{1,0:T(8,128)(2,1)}, u32[]{:S(2)}) copy-start(bf16[256,512]{1,0:T(8,128)(2,1)} %refs_15_.1) | copy-start | bytes 786436
  19.7 7.1 %copy-start.14 = (bf16[256,256]{1,0:T(8,128)(2,1)S(1)}, bf16[256,256]{1,0:T(8,128)(2,1)}, u32[]{:S(2)}) copy-start(bf16[256,256]{1,0:T(8,128)(2,1)} %refs_9_.1) | copy-start | bytes 393220
  19.7 20.5 %all-to-all-start = ((bf16[16,4,16,256]{3,2,1,0:T(8,128)(2,1)}), bf16[16,4,16,256]{3,2,1,0:T(8,128)(2,1)S(1)}, u32[]{:S(2)}, u32[]{:S(2)}) async-start(bf16[16,4,16,256]{3,2,1,0:T(8,128)(2,1)} %bitcast.3), calls=%async_computation | async-start | bytes 1048576 | tf_op jit(solution)/shard_map/all_to_all | solution.py:488
  26.0 0.7 %copy-start.18 = (s32[1,8]{1,0:T(1,128)S(1)}, s32[1,8]{1,0:T(1,128)}, u32[]{:S(2)}) copy-start(s32[1,8]{1,0:T(1,128)} %param.28) | copy-start | bytes 100
  26.7 0.7 %copy-start.15 = (f32[256]{0:T(256)S(1)}, f32[256]{0:T(256)}, u32[]{:S(2)}) copy-start(f32[256]{0:T(256)} %param.20) | copy-start | bytes 3076

commit v6 on v5

--- a/solution.py
+++ b/solution.py
@@ -185,12 +185,12 @@
 
 def local_kernel(n, *refs):
     pieces = refs[:n]
-    gain_ref, wq_ref, wkv_ref, qt_ref, ctx_ref, top_ref, sum_ref, wvt_ref, wqt_s = refs[n:]
+    gain_ref, wq_ref, wkv_ref, qt_ref, ctx_ref, stat_ref, wqt_s, wvt_s = refs[n:]
     tb, width, block = qt_ref.shape
 
     @pl.when(pl.program_id(0) == 0)
     def _():
-        wvt_ref[...] = wkv_ref[:, width:].T
+        wvt_s[...] = wkv_ref[:, width:].T
         wqt_s[...] = wq_ref[...].T
 
     x = jnp.concatenate([p[t] for t in range(tb) for p in pieces], axis=0).astype(F32)
@@ -201,10 +201,11 @@
     for t in range(tb):
         here = slice(t * block, (t + 1) * block)
         qt_ref[t] = dot_nt(wqt_s[...], normed[here]).astype(BF16)
-        vt = dot_nt(wvt_ref[...], normed[here]).astype(BF16)
+        vt = dot_nt(wvt_s[...], normed[here]).astype(BF16)
         scores = [pair_scores(q[here], k[here], masks, pair) for pair in range(H // 2)]
         tops = [jnp.max(x, axis=0, keepdims=True) for x in scores]
         es = [jnp.exp2((x - top) * SCALE) for x, top in zip(scores, tops)]
+        context = []
         for pair, e in enumerate(es):
             lo = pair * 2 * HEAD
             both = dot(vt[lo : lo + 2 * HEAD], e.astype(BF16))
@@ -212,9 +213,10 @@
             for i in range(2):
                 lanes = slice(i * block, (i + 1) * block)
                 head = 2 * pair + i
-                ctx_ref[t, lo + i * HEAD : lo + (i + 1) * HEAD, :] = both[i * HEAD : (i + 1) * HEAD, lanes].astype(BF16)
-                top_ref[t, head : head + 1, :] = tops[pair][:, lanes]
-                sum_ref[t, head : head + 1, :] = total[:, lanes]
+                context.append(both[i * HEAD : (i + 1) * HEAD, lanes].astype(BF16))
+                stat_ref[t, head : head + 1, :] = tops[pair][:, lanes]
+                stat_ref[t, H + head : H + head + 1, :] = total[:, lanes]
+        ctx_ref[t] = jnp.concatenate(context, axis=0).T
 
 
 def local_part(pieces, gain, wq, wkv):
@@ -227,21 +229,17 @@
         functools.partial(local_kernel, len(pieces)),
         out_shape=[
             pltpu.HBM((steps, width, block), BF16),
-            pltpu.HBM((steps, width, block), BF16),
-            pltpu.HBM((steps, H, block), F32),
-            pltpu.HBM((steps, H, block), F32),
-            pltpu.HBM((width, width), BF16),
+            pltpu.HBM((steps, block, width), BF16),
+            jax.ShapeDtypeStruct((steps, 2 * H, block), F32),
         ],
         grid=(steps // tb,),
         in_specs=[per_t(p.shape[1], width) for p in pieces] + [full(gain), full(wq), full(wkv)],
         out_specs=[
             per_t(width, block),
-            per_t(width, block),
-            per_t(H, block),
-            per_t(H, block),
-            pl.BlockSpec((width, width), lambda i: (0, 0)),
+            per_t(block, width),
+            per_t(2 * H, block),
         ],
-        scratch_shapes=[pltpu.VMEM((width, width), BF16)],
+        scratch_shapes=[pltpu.VMEM((width, width), BF16)] * 2,
         compiler_params=pltpu.CompilerParams(vmem_limit_bytes=VMEM_LIMIT),
         cost_estimate=pl.CostEstimate(
             flops=steps * block * width * width * 12, bytes_accessed=steps * block * width * 10, transcendentals=0
@@ -256,12 +254,21 @@
     return half + half * jnp.tanh(inner)
 
 
+def rows_of(pieces, first, count):
+    parts, start = [], 0
+    for p in pieces:
+        low, high = max(first, start), min(first + count, start + p.shape[1])
+        if low < high:
+            parts.append(p[:, low - start : high - start, :])
+        start += p.shape[1]
+    return jnp.concatenate(parts, axis=1)
+
+
 def finish_kernel(n, split, sb, numbers_ref, *refs):
     pieces = refs[:n]
-    in_ref, gain_hbm, gain_ffn_hbm, ltop_hbm, lsum_hbm = refs[n : n + 5]
-    qt_hbm, lctx_hbm, wkv_hbm, wvt_hbm, wo_hbm, w_in_hbm, w_out_hbm, out_hbm = refs[n + 5 : n + 13]
-    (x_s, raw_s, rn_s, rk_s, ctx_s, out_s, qt_s, lctx_s, wk_s, wvt_s, wo_s, w_in_s, w_out_s, gain_ref, gain_ffn_ref,
-     ltop_ref, lsum_ref, sems, out_sems) = refs[n + 13 :]
+    in_ref, gain_ref, wkv_ref, stat_ref, wo_s, w_in_s, w_out_s = refs[n : n + 7]
+    gain_ffn_hbm, qt_hbm, lctx_hbm, out_hbm = refs[n + 7 : n + 11]
+    raw_s, rn_s, rk_s, rv_s, ctx_s, out_s, qt_s, lctx_s, gain_ffn_ref, sems, out_sems = refs[n + 11 :]
     steps, width, block = qt_s.shape
     remote = rn_s.shape[1]
     slots = remote // REMOTE_SENSORS
@@ -273,16 +280,17 @@
         copy.start()
         return copy
 
-    first_in = [fetch(gain_hbm, gain_ref), fetch(wkv_hbm.at[:, pl.ds(0, width)], wk_s), fetch(wvt_hbm, wvt_s)]
-    score_in = [fetch(qt_hbm, qt_s), fetch(ltop_hbm, ltop_ref), fetch(lsum_hbm, lsum_ref)]
+    score_in = [fetch(qt_hbm, qt_s)]
+    merge_in = [fetch(lctx_hbm, lctx_s)]
+    ffn_in = [fetch(gain_ffn_hbm, gain_ffn_ref)]
 
     order = swap16() if split else None
     lane_head = lax.broadcasted_iota(jnp.int32, (1, 128), 1) // HEAD
     heads = [(lane_head == h).astype(BF16) for h in range(128 // HEAD)]
     none = jnp.zeros((remote, 128), BF16)
-    own_block = (
-        lax.broadcasted_iota(jnp.int32, (width, H * remote), 0) // HEAD
-        == lax.broadcasted_iota(jnp.int32, (width, H * remote), 1) // remote
+    to_lanes = (
+        lax.broadcasted_iota(jnp.int32, (2 * H, width), 1) // HEAD
+        == lax.broadcasted_iota(jnp.int32, (2 * H, width), 0) % H
     ).astype(BF16)
     slot = lax.broadcasted_iota(jnp.int32, (remote, block), 0) // REMOTE_SENSORS
     live = jnp.zeros((remote, block), jnp.int32)
@@ -290,14 +298,6 @@
         live = jnp.where(slot == j, numbers_ref[1 + slots + j], live)
     live = live > 0
 
-    for copy in first_in:
-        copy.wait()
-    merge_in = [fetch(lctx_hbm, lctx_s)]
-    x_in, place = [fetch(wo_hbm, wo_s)], 0
-    for p in pieces:
-        x_in.append(fetch(p, x_s.at[:, pl.ds(place, p.shape[1])]))
-        place += p.shape[1]
-    ffn_in = [fetch(gain_ffn_hbm, gain_ffn_ref), fetch(w_in_hbm, w_in_s), fetch(w_out_hbm, w_out_s)]
     if split:
         for j in range(slots):
             raw_s[j * REMOTE_SENSORS : (j + 1) * REMOTE_SENSORS] = in_ref[numbers_ref[1 + j]]
@@ -308,43 +308,51 @@
     else:
         raw = in_ref[...]
     normed = rms(raw.reshape(steps * remote, width).astype(F32), gain_ref[...])
-    rn_s[...] = normed.reshape(steps, remote, width)
-    rk_s[...] = dot(normed, wk_s[...]).astype(BF16).reshape(steps, remote, width)
-
-    for copy in score_in:
-        copy.wait()
-    keys = []
-    for t in range(steps):
-        rk = rk_s[t]
+    kv = dot(normed, wkv_ref[...]).astype(BF16)
+    rk_s[...] = kv[:, :width].reshape(steps, remote, width)
+    rv_s[...] = kv[:, width:].reshape(steps, remote, width)
+
+    def by_head(rows):
         spread = []
         for h in range(H):
             half = h * HEAD // 128
-            part = rk[:, half * 128 : (half + 1) * 128] * heads[h % (128 // HEAD)]
+            part = rows[:, half * 128 : (half + 1) * 128] * heads[h % (128 // HEAD)]
             spread.append(jnp.concatenate([part, none] if half == 0 else [none, part], axis=1))
-        keys.append(jnp.concatenate(spread, axis=0))
-    scores = [dot(keys[t], qt_s[t]).reshape(H, remote, block) for t in range(steps)]
-    values = []
-    for t in range(steps):
-        tiled = jnp.concatenate([rn_s[t]] * H, axis=0)
-        values.append(dot_nt(wvt_s[...], tiled).astype(BF16) * own_block)
-    weights, keeps = [], []
-    for t in range(steps):
-        masked = jnp.where(live[None], scores[t], NEG)
-        ltop = ltop_ref[t]
+        return jnp.concatenate(spread, axis=0)
+
+    for copy in score_in:
+        copy.wait()
+    def score(t):
+        return dot(by_head(rk_s[t]), qt_s[t]).reshape(H, remote, block)
+
+    def weigh(t, scores):
+        masked = jnp.where(live[None], scores, NEG)
+        ltop = stat_ref[t, :H]
         top = jnp.maximum(jnp.max(masked, axis=1), ltop)
         e = jnp.exp2((masked - top[:, None, :]) * SCALE)
         keep = jnp.exp2((ltop - top) * SCALE)
-        inverse = 1.0 / (jnp.sum(e, axis=1) + lsum_ref[t] * keep)
-        keeps.append(keep * inverse)
-        weights.append((e * inverse[:, None, :]).astype(BF16).reshape(H * remote, block))
-    far = [dot(values[t], weights[t]).reshape(H, HEAD, block) for t in range(steps)]
+        inverse = 1.0 / (jnp.sum(e, axis=1) + stat_ref[t, H:] * keep)
+        keep = keep * inverse
+        high = keep.astype(BF16).astype(F32)
+        factors = jnp.concatenate([high, keep - high], axis=0).astype(BF16).T
+        return factors, (e * inverse[:, None, :]).astype(BF16).reshape(H * remote, block).T
+
+    def merge(t, factors, weights):
+        far = dot(weights, by_head(rv_s[t]))
+        ctx_s[t] = (lctx_s[t].astype(F32) * dot(factors, to_lanes) + far).astype(BF16)
+
     for copy in merge_in:
         copy.wait()
+    upcoming, waiting = score(0), None
     for t in range(steps):
-        merged = lctx_s[t].astype(F32).reshape(H, HEAD, block) * keeps[t][:, None, :] + far[t]
-        ctx_s[t] = merged.reshape(width, block).astype(BF16).T
-
-    for copy in x_in + ffn_in:
+        scores, upcoming = upcoming, score(t + 1) if t + 1 < steps else None
+        weighed = (t, *weigh(t, scores))
+        if waiting:
+            merge(*waiting)
+        waiting = weighed
+    merge(*waiting)
+
+    for copy in ffn_in:
         copy.wait()
     tile = width
     tiles = w_in_s.shape[1] // tile
@@ -352,8 +360,9 @@
     ready, total, copies = {}, {}, []
 
     def open_rows(first):
-        rows = lambda ref: ref[:, first : first + sb, :].reshape(steps * sb, width)
-        after = rows(x_s).astype(F32) + dot(rows(ctx_s), wo_s[...])
+        x = rows_of(pieces, first, sb).reshape(steps * sb, width)
+        context = ctx_s[:, first : first + sb, :].reshape(steps * sb, width)
+        after = x.astype(F32) + dot(context, wo_s[...])
         total[first] = after
         ready[first] = rms(after, gain_ffn_ref[...])
 
@@ -390,39 +399,31 @@
 
 
 def finish(numbers, pieces, incoming, local, gain, wkv, wo, gain_ffn, w_in, w_out, split):
-    qt, lctx, ltop, lsum, wvt = local
+    qt, lctx, stat = local
     steps, width, block = qt.shape
     remote = (numbers.shape[0] - 1) // 2 * REMOTE_SENSORS
     sb = 32
     hbm = pl.BlockSpec(memory_space=pl.ANY)
-    n_copies = 12 + len(pieces)
-    far = (*pieces, incoming, gain, gain_ffn, ltop, lsum, qt, lctx, wkv, wvt, wo, w_in, w_out)
-    far = [a if a is incoming else pltpu.with_memory_space_constraint(a, pltpu.HBM) for a in far]
+    near = [*pieces, incoming, gain, wkv, stat, wo, w_in, w_out]
+    pin = lambda arrays: [pltpu.with_memory_space_constraint(a, pltpu.HBM) for a in arrays]
+    vmem = pl.BlockSpec(memory_space=pltpu.VMEM)
     buffer = lambda *shape: pltpu.VMEM(shape, BF16)
     return pl.pallas_call(
         functools.partial(finish_kernel, len(pieces), split, sb),
         out_shape=jax.ShapeDtypeStruct((block, steps, width) if split else (steps, block, width), BF16),
-        in_specs=[pl.BlockSpec(memory_space=pltpu.SMEM)] + [pl.BlockSpec(memory_space=pltpu.VMEM) if a is incoming else hbm for a in far],
+        in_specs=[pl.BlockSpec(memory_space=pltpu.SMEM)] + [vmem] * len(near) + [hbm] * 3,
         out_specs=hbm,
         scratch_shapes=[
-            buffer(steps, block, width),
             buffer(remote, steps, width),
+            buffer(steps, remote, width),
             buffer(steps, remote, width),
             buffer(steps, remote, width),
             buffer(steps, block, width),
             buffer(block, steps, width) if split else buffer(steps, block, width),
             buffer(steps, width, block),
-            buffer(steps, width, block),
-            buffer(width, width),
-            buffer(width, width),
-            buffer(*wo.shape),
-            buffer(*w_in.shape),
-            buffer(*w_out.shape),
-            pltpu.VMEM(gain.shape, F32),
+            buffer(steps, block, width),
             pltpu.VMEM(gain_ffn.shape, F32),
-            pltpu.VMEM(ltop.shape, F32),
-            pltpu.VMEM(lsum.shape, F32),
-            pltpu.SemaphoreType.DMA((n_copies,)),
+            pltpu.SemaphoreType.DMA((3,)),
             pltpu.SemaphoreType.DMA((block // sb,)),
         ],
         compiler_params=pltpu.CompilerParams(vmem_limit_bytes=VMEM_LIMIT),
@@ -430,7 +431,7 @@
             flops=steps * block * width * width * 18, bytes_accessed=steps * block * width * 12, transcendentals=0
         ),
         name="remote_keys_and_feed_forward",
-    )(numbers, *far)
+    )(numbers, *near, *pin([gain_ffn, qt, lctx]))
 
 
 def local(

time: 50.2 us -> 49.8 us (level)
    unnamed x38 -> x28, local copies, waits for them, and re-layouts: 1.99 us -> 2.05 us
where the time goes in v6:
time: 49.8 us; the launch traced here: 49.5 us
  Pallas kernels  27.4 us (55%)
  starting transfers between devices  11.9 us (24%)
  waiting for transfers between devices  7.37 us (15%)
  local copies, waits for them, and re-layouts  2.41 us (5%)
    pallas_call x1, Pallas kernels, finish(): pl.pallas_call(functools.partial(finish_kernel, len(pieces), split, sb),...  9.1 us
    pallas_call x1, Pallas kernels, local_part(): pl.pallas_call(functools.partial(local_kernel, len(pieces)), out_shape=[p...  8.94 us
    pallas_call x4, Pallas kernels, time_block(): pl.pallas_call(functools.partial(time_kernel, split), out_shape=out_shape...  8.01 us
    all_to_all x1, starting transfers between devices, local(): lax.all_to_all(outgoing, 'sensor', split_axis=0, concat_axis=0, tiled=True)  6.07 us
    ppermute x4, starting transfers between devices, local(): got.append(lax.ppermute(send, 'tm', [(0, 1), (1, 0)]))  5.82 us
    all_to_all x1, waiting for transfers between devices, local(): lax.all_to_all(outgoing, 'sensor', split_axis=0, concat_axis=0, tiled=True)  3.91 us
    ppermute x4, waiting for transfers between devices, local(): got.append(lax.ppermute(send, 'tm', [(0, 1), (1, 0)]))  3.46 us
    unnamed x28, local copies, waits for them, and re-layouts  2.05 us
  transfers between devices with their start and end apart: 5, of which 3 were waited for; matrix products, arithmetic and copies ran while one was open for 1% of the time, Pallas kernels for 28%

profile of v6, /device:TPU:0, one launch (start us, length us, event | category | flops | bytes accessed | tf_op | source)
XLA Modules:
  0.0 49.5 jit_solution(7841550084615150479)
XLA Ops:
  0.0 0.0 copy-start
  0.0 0.0 copy-start.2
  0.0 0.0 copy-start.3
  0.0 2.9 %time_block.4 = (bf16[16,16,256]{2,1,0:T(8,128)(2,1)S(1)}, bf16[16,16,256]{2,1,0:T(8,128)(2,1)S(1)}) custom-call(s32[1]{0:T(128)} %bitcast.my_ref, bf16[64,32,256]{2,1,0:T(8,128)(2,1)} %x_ref.4, f32[1,256]{1,0:T(1,128)} %bitcast.6, bf16[256,256]{1,0:T(8,128)(2,1)} %wq_ref.7, bf16[256,512]{1,0:T(8,128)(2,1)} %wkv_ref.7, bf16[256,256]{1,0:T(8,128)(2,1)} %wo_ref.7), custom_call_target="tpu_custom_call" | custom-call | flops 402653184 | bytes 524288 | tf_op jit(solution)/shard_map/time_block/pallas_call | solution.py:130
  2.9 0.0 copy-start.4
  2.9 3.0 %collective-permute-start = (bf16[16,16,256]{2,1,0:T(8,128)(2,1)S(1)}, bf16[16,16,256]{2,1,0:T(8,128)(2,1)S(1)}, u32[]{:S(2)}, u32[]{:S(2)}) collective-permute-start(bf16[16,16,256]{2,1,0:T(8,128)(2,1)S(1)} %get-tuple-element.33), channel_id=1, source_target_pairs={{0,1},{1,0},{2,3},{3,2},{4,5},{5,4},{6,7},{7,6},{8,9},{9,8},{10,11... | collective-permute-start | bytes 393224 | tf_op jit(solution)/shard_map/ppermute | solution.py:472
  6.0 0.0 copy-done
  6.0 0.0 copy-done.1
  6.0 0.0 copy-done.2
  6.0 0.0 copy-done.3
  6.0 0.0 copy-done.4
  6.0 1.7 %time_block.5 = (bf16[16,16,256]{2,1,0:T(8,128)(2,1)S(1)}, bf16[16,16,256]{2,1,0:T(8,128)(2,1)S(1)}) custom-call(s32[1]{0:T(128)} %bitcast.my_ref, bf16[64,32,256]{2,1,0:T(8,128)(2,1)S(1)} %copy-done, f32[1,256]{1,0:T(1,128)S(1)} %bitcast.7, bf16[256,256]{1,0:T(8,128)(2,1)S(1)} %copy-done.2, bf16[256,512]{1,0:T(8,128)(2,1)S(1)} %copy-done.1, ...), custom_call_target="tpu_custom_call" | custom-call | flops 402653184 | bytes 524288 | tf_op jit(solution)/shard_map/time_block/pallas_call | solution.py:130
  7.7 0.6 %collective-permute-start.1 = (bf16[16,16,256]{2,1,0:T(8,128)(2,1)S(1)}, bf16[16,16,256]{2,1,0:T(8,128)(2,1)S(1)}, u32[]{:S(2)}, u32[]{:S(2)}) collective-permute-start(bf16[16,16,256]{2,1,0:T(8,128)(2,1)S(1)} %get-tuple-element.34), channel_id=1, source_target_pairs={{0,1},{1,0},{2,3},{3,2},{4,5},{5,4},{6,7},{7,6},{8,9},{9,8},{10,11... | collective-permute-start | bytes 393224 | tf_op jit(solution)/shard_map/ppermute | solution.py:472
  8.3 1.7 %time_block.6 = (bf16[16,16,256]{2,1,0:T(8,128)(2,1)S(1)}, bf16[16,16,256]{2,1,0:T(8,128)(2,1)S(1)}) custom-call(s32[1]{0:T(128)} %bitcast.my_ref, bf16[64,32,256]{2,1,0:T(8,128)(2,1)S(1)} %copy-done, f32[1,256]{1,0:T(1,128)S(1)} %bitcast.8, bf16[256,256]{1,0:T(8,128)(2,1)S(1)} %copy-done.2, bf16[256,512]{1,0:T(8,128)(2,1)S(1)} %copy-done.1, ...), custom_call_target="tpu_custom_call" | custom-call | flops 402653184 | bytes 524288 | tf_op jit(solution)/shard_map/time_block/pallas_call | solution.py:130
  10.0 1.5 %collective-permute-start.2 = (bf16[16,16,256]{2,1,0:T(8,128)(2,1)S(1)}, bf16[16,16,256]{2,1,0:T(8,128)(2,1)S(1)}, u32[]{:S(2)}, u32[]{:S(2)}) collective-permute-start(bf16[16,16,256]{2,1,0:T(8,128)(2,1)S(1)} %get-tuple-element.35), channel_id=1, source_target_pairs={{0,1},{1,0},{2,3},{3,2},{4,5},{5,4},{6,7},{7,6},{8,9},{9,8},{10,11... | collective-permute-start | bytes 393224 | tf_op jit(solution)/shard_map/ppermute | solution.py:472
  11.6 0.0 copy-start.12
  11.6 1.7 %time_block.7 = (bf16[16,16,256]{2,1,0:T(8,128)(2,1)S(1)}, bf16[16,16,256]{2,1,0:T(8,128)(2,1)S(1)}) custom-call(s32[1]{0:T(128)} %bitcast.my_ref, bf16[64,32,256]{2,1,0:T(8,128)(2,1)S(1)} %copy-done, f32[1,256]{1,0:T(1,128)S(1)} %bitcast.9, bf16[256,256]{1,0:T(8,128)(2,1)S(1)} %copy-done.2, bf16[256,512]{1,0:T(8,128)(2,1)S(1)} %copy-done.1, ...), custom_call_target="tpu_custom_call" | custom-call | flops 402653184 | bytes 524288 | tf_op jit(solution)/shard_map/time_block/pallas_call | solution.py:130
  13.3 0.6 %collective-permute-start.3 = (bf16[16,16,256]{2,1,0:T(8,128)(2,1)S(1)}, bf16[16,16,256]{2,1,0:T(8,128)(2,1)S(1)}, u32[]{:S(2)}, u32[]{:S(2)}) collective-permute-start(bf16[16,16,256]{2,1,0:T(8,128)(2,1)S(1)} %get-tuple-element.37), channel_id=1, source_target_pairs={{0,1},{1,0},{2,3},{3,2},{4,5},{5,4},{6,7},{7,6},{8,9},{9,8},{10,11... | collective-permute-start | bytes 393224 | tf_op jit(solution)/shard_map/ppermute | solution.py:472
  13.9 0.0 copy-start.11
  13.9 0.7 %copy-done.11 = s32[16,8]{0,1:T(8,128)S(1)} copy-done((s32[16,8]{0,1:T(8,128)S(1)}, s32[16,8]{0,1:T(8,128)}, u32[]{:S(2)}) %copy-start.11) | copy-done | bytes 536
  14.6 0.0 copy-done.12
  14.6 0.1 copy.16
  14.7 0.1 eq.25
  14.8 0.1 compare_convert_fusion.pick_ref
  14.9 0.0 collective-permute-done.refs_4_
  14.9 0.0 collective-permute-done.1.refs_5_
  14.9 1.2 %collective-permute-done.2.refs_6_ = bf16[16,16,256]{2,1,0:T(8,128)(2,1)S(1)} collective-permute-done((bf16[16,16,256]{2,1,0:T(8,128)(2,1)S(1)}, bf16[16,16,256]{2,1,0:T(8,128)(2,1)S(1)}, u32[]{:S(2)}, u32[]{:S(2)}) %collective-permute-start.2) | collective-permute-done | bytes 131104 | tf_op jit(solution)/shard_map/ppermute | solution.py:472
  16.1 2.2 %collective-permute-done.3.refs_7_ = bf16[16,16,256]{2,1,0:T(8,128)(2,1)S(1)} collective-permute-done((bf16[16,16,256]{2,1,0:T(8,128)(2,1)S(1)}, bf16[16,16,256]{2,1,0:T(8,128)(2,1)S(1)}, u32[]{:S(2)}, u32[]{:S(2)}) %collective-permute-start.3) | collective-permute-done | bytes 131104 | tf_op jit(solution)/shard_map/ppermute | solution.py:472
  18.3 1.3 %pick_rows.1 = bf16[64,16,256]{2,1,0:T(8,128)(2,1)} custom-call(bf16[64,128]{1,0:T(8,128)(2,1)S(1)} %compare_convert_fusion.pick_ref, bf16[16,16,256]{2,1,0:T(8,128)(2,1)S(1)} %get-tuple-element.23.refs_0_, bf16[16,16,256]{2,1,0:T(8,128)(2,1)S(1)} %get-tuple-element.26.refs_1_, bf16[16,16,256]{2,1,0:T(8,128)(2,1)S(1)} %get-tuple-element.29.refs_2_, ...), custom_call_target="tpu_custom_call" | custom-call | tf_op jit(solution)/shard_map/pick_rows/pallas_call | solution.py:171
  19.7 0.0 copy-start.7
  19.7 0.0 copy-start.8
  19.7 6.1 %all-to-all-start = ((bf16[16,4,16,256]{3,2,1,0:T(8,128)(2,1)}), bf16[16,4,16,256]{3,2,1,0:T(8,128)(2,1)S(1)}, u32[]{:S(2)}, u32[]{:S(2)}) async-start(bf16[16,4,16,256]{3,2,1,0:T(8,128)(2,1)} %bitcast.3), calls=%async_computation | async-start | bytes 1048576 | tf_op jit(solution)/shard_map/all_to_all | solution.py:489
  25.8 0.2 dynamic-slice_reduce_fusion
  26.0 0.0 copy-start.13
  26.0 0.7 %copy-done.13 = s32[1,8]{1,0:T(1,128)S(1)} copy-done((s32[1,8]{1,0:T(1,128)S(1)}, s32[1,8]{1,0:T(1,128)}, u32[]{:S(2)}) %copy-start.13) | copy-done | bytes 56
  26.6 0.1 pad_add_fusion.numbers_ref
  26.7 0.0 copy-start.10
  26.7 0.0 copy-done.7
  26.7 0.0 copy-done.8
  26.7 0.7 %copy-done.10 = f32[256]{0:T(256)S(1)} copy-done((f32[256]{0:T(256)S(1)}, f32[256]{0:T(256)}, u32[]{:S(2)}) %copy-start.10) | copy-done | bytes 1048
  27.4 0.0 copy-start.5
  27.4 0.0 copy-start.6
  27.4 8.9 %local_keys.1 = (bf16[16,256,128]{2,1,0:T(8,128)(2,1)}, bf16[16,128,256]{2,1,0:T(8,128)(2,1)}, f32[16,16,128]{2,1,0:T(8,128)S(1)}) custom-call(bf16[16,16,256]{2,1,0:T(8,128)(2,1)S(1)} %get-tuple-element.23.refs_0_, bf16[16,16,256]{2,1,0:T(8,128)(2,1)S(1)} %get-tuple-element.26.refs_1_, bf16[16,16,256]{2,1,0:T(8,128)(2,1)S(1)} %get-tuple-element.29.refs_2_, ...), custom_call_target="tpu_custom_call" | custom-call | flops 1610612736 | bytes 5242880 | tf_op jit(solution)/shard_map/local_keys/pallas_call | solution.py:228
  36.3 3.9 %all-to-all-done.refs_8_ = bf16[16,4,16,256]{3,2,1,0:T(8,128)(2,1)S(1)} async-done(((bf16[16,4,16,256]{3,2,1,0:T(8,128)(2,1)}), bf16[16,4,16,256]{3,2,1,0:T(8,128)(2,1)S(1)}, u32[]{:S(2)}, u32[]{:S(2)}) %all-to-all-start) | async-done | bytes 524320 | tf_op jit(solution)/shard_map/all_to_all | solution.py:489
  40.2 0.0 copy-done.5
  40.2 0.0 copy-done.6
  40.2 0.0 copy-done.9
  40.3 9.1 %remote_keys_and_feed_forward.1 = bf16[128,16,256]{2,1,0:T(8,128)(2,1)} custom-call(s32[17]{0:T(128)S(1)} %pad_add_fusion.numbers_ref, bf16[16,16,256]{2,1,0:T(8,128)(2,1)S(1)} %get-tuple-element.23.refs_0_, bf16[16,16,256]{2,1,0:T(8,128)(2,1)S(1)} %get-tuple-element.26.refs_1_, bf16[16,16,256]{2,1,0:T(8,128)(2,1)S(1)} %get-tuple-element.29.refs_2_, ...), custom_call_target="tpu_custom_call" | custom-call | flops 2415919104 | bytes 6291456 | tf_op jit(solution)/shard_map/remote_keys_and_feed_forward/pallas_call | solution.py:411
  (5 shorter events, 0.0 us)
Async XLA Ops:
  0.0 6.0 %copy-start = (bf16[64,32,256]{2,1,0:T(8,128)(2,1)S(1)}, bf16[64,32,256]{2,1,0:T(8,128)(2,1)}, u32[]{:S(2)}) copy-start(bf16[64,32,256]{2,1,0:T(8,128)(2,1)} %x_ref.4) | copy-start | bytes 3145732
  0.0 6.0 %copy-start.1 = (bf16[256,512]{1,0:T(8,128)(2,1)S(1)}, bf16[256,512]{1,0:T(8,128)(2,1)}, u32[]{:S(2)}) copy-start(bf16[256,512]{1,0:T(8,128)(2,1)} %wkv_ref.7) | copy-start | bytes 786436
  0.0 6.0 %copy-start.2 = (bf16[256,256]{1,0:T(8,128)(2,1)S(1)}, bf16[256,256]{1,0:T(8,128)(2,1)}, u32[]{:S(2)}) copy-start(bf16[256,256]{1,0:T(8,128)(2,1)} %wq_ref.7) | copy-start | bytes 393220
  0.0 6.0 %copy-start.3 = (bf16[256,256]{1,0:T(8,128)(2,1)S(1)}, bf16[256,256]{1,0:T(8,128)(2,1)}, u32[]{:S(2)}) copy-start(bf16[256,256]{1,0:T(8,128)(2,1)} %wo_ref.7) | copy-start | bytes 393220
  2.9 3.0 %copy-start.4 = (f32[256]{0:T(256)S(1)}, f32[256]{0:T(256)}, u32[]{:S(2)}) copy-start(f32[256]{0:T(256)} %param.16) | copy-start | bytes 3076
  2.9 11.9 %collective-permute-start = (bf16[16,16,256]{2,1,0:T(8,128)(2,1)S(1)}, bf16[16,16,256]{2,1,0:T(8,128)(2,1)S(1)}, u32[]{:S(2)}, u32[]{:S(2)}) collective-permute-start(bf16[16,16,256]{2,1,0:T(8,128)(2,1)S(1)} %get-tuple-element.33), channel_id=1, source_target_pairs={{0,1},{1,0},{2,3},{3,2},{4,5},{5,4},{6,7},{7,6},{8,9},{9,8},{10,11... | collective-permute-start | bytes 393224 | tf_op jit(solution)/shard_map/ppermute | solution.py:472
  7.7 7.2 %collective-permute-start.1 = (bf16[16,16,256]{2,1,0:T(8,128)(2,1)S(1)}, bf16[16,16,256]{2,1,0:T(8,128)(2,1)S(1)}, u32[]{:S(2)}, u32[]{:S(2)}) collective-permute-start(bf16[16,16,256]{2,1,0:T(8,128)(2,1)S(1)} %get-tuple-element.34), channel_id=1, source_target_pairs={{0,1},{1,0},{2,3},{3,2},{4,5},{5,4},{6,7},{7,6},{8,9},{9,8},{10,11... | collective-permute-start | bytes 393224 | tf_op jit(solution)/shard_map/ppermute | solution.py:472
  10.0 6.1 %collective-permute-start.2 = (bf16[16,16,256]{2,1,0:T(8,128)(2,1)S(1)}, bf16[16,16,256]{2,1,0:T(8,128)(2,1)S(1)}, u32[]{:S(2)}, u32[]{:S(2)}) collective-permute-start(bf16[16,16,256]{2,1,0:T(8,128)(2,1)S(1)} %get-tuple-element.35), channel_id=1, source_target_pairs={{0,1},{1,0},{2,3},{3,2},{4,5},{5,4},{6,7},{7,6},{8,9},{9,8},{10,11... | collective-permute-start | bytes 393224 | tf_op jit(solution)/shard_map/ppermute | solution.py:472
  11.6 3.0 %copy-start.12 = (s32[16,8,4]{0,2,1:T(4,128)S(1)}, s32[16,8,4]{0,2,1:T(4,128)}, u32[]{:S(2)}) copy-start(s32[16,8,4]{0,2,1:T(4,128)} %param.29) | copy-start | bytes 6148
  13.3 5.1 %collective-permute-start.3 = (bf16[16,16,256]{2,1,0:T(8,128)(2,1)S(1)}, bf16[16,16,256]{2,1,0:T(8,128)(2,1)S(1)}, u32[]{:S(2)}, u32[]{:S(2)}) collective-permute-start(bf16[16,16,256]{2,1,0:T(8,128)(2,1)S(1)} %get-tuple-element.37), channel_id=1, source_target_pairs={{0,1},{1,0},{2,3},{3,2},{4,5},{5,4},{6,7},{7,6},{8,9},{9,8},{10,11... | collective-permute-start | bytes 393224 | tf_op jit(solution)/shard_map/ppermute | solution.py:472
  13.9 0.7 %copy-start.11 = (s32[16,8]{0,1:T(8,128)S(1)}, s32[16,8]{0,1:T(8,128)}, u32[]{:S(2)}) copy-start(s32[16,8]{0,1:T(8,128)} %param.27) | copy-start | bytes 1540
  19.7 7.0 %copy-start.7 = (bf16[256,512]{1,0:T(8,128)(2,1)S(1)}, bf16[256,512]{1,0:T(8,128)(2,1)}, u32[]{:S(2)}) copy-start(bf16[256,512]{1,0:T(8,128)(2,1)} %refs_10_.3) | copy-start | bytes 786436
  19.7 7.0 %copy-start.8 = (bf16[256,256]{1,0:T(8,128)(2,1)S(1)}, bf16[256,256]{1,0:T(8,128)(2,1)}, u32[]{:S(2)}) copy-start(bf16[256,256]{1,0:T(8,128)(2,1)} %refs_9_.1) | copy-start | bytes 393220
  19.7 20.5 %all-to-all-start = ((bf16[16,4,16,256]{3,2,1,0:T(8,128)(2,1)}), bf16[16,4,16,256]{3,2,1,0:T(8,128)(2,1)S(1)}, u32[]{:S(2)}, u32[]{:S(2)}) async-start(bf16[16,4,16,256]{3,2,1,0:T(8,128)(2,1)} %bitcast.3), calls=%async_computation | async-start | bytes 1048576 | tf_op jit(solution)/shard_map/all_to_all | solution.py:489
  26.0 0.7 %copy-start.13 = (s32[1,8]{1,0:T(1,128)S(1)}, s32[1,8]{1,0:T(1,128)}, u32[]{:S(2)}) copy-start(s32[1,8]{1,0:T(1,128)} %param.28) | copy-start | bytes 100
  26.7 0.7 %copy-start.10 = (f32[256]{0:T(256)S(1)}, f32[256]{0:T(256)}, u32[]{:S(2)}) copy-start(f32[256]{0:T(256)} %param.20) | copy-start | bytes 3076
  27.4 12.9 %copy-start.5 = (bf16[256,1024]{1,0:T(8,128)(2,1)S(1)}, bf16[256,1024]{1,0:T(8,128)(2,1)}, u32[]{:S(2)}) copy-start(bf16[256,1024]{1,0:T(8,128)(2,1)} %refs_13_.1) | copy-start | bytes 1572868
  27.4 12.9 %copy-start.6 = (bf16[1024,256]{1,0:T(8,128)(2,1)S(1)}, bf16[1024,256]{1,0:T(8,128)(2,1)}, u32[]{:S(2)}) copy-start(bf16[1024,256]{1,0:T(8,128)(2,1)} %refs_14_.1) | copy-start | bytes 1572868
  27.4 12.9 %copy-start.9 = (bf16[256,256]{1,0:T(8,128)(2,1)S(1)}, bf16[256,256]{1,0:T(8,128)(2,1)}, u32[]{:S(2)}) copy-start(bf16[256,256]{1,0:T(8,128)(2,1)} %refs_12_.1) | copy-start | bytes 393220

commit v7 on v6

--- a/solution.py
+++ b/solution.py
@@ -152,26 +152,38 @@
 
 
 def pick_kernel(n, pick_ref, *refs):
-    pieces, (out_ref, o_s) = refs[:n], refs[n:]
-    steps = out_ref.shape[1]
-    wanted = out_ref.shape[0]
+    pieces, (out_hbm, o_s, out_s, sems) = refs[:n], refs[n:]
+    steps, wanted, width = o_s.shape
     order = swap16()
     pick = pick_ref[...]
     for t in range(steps):
         rows = jnp.concatenate([p[t] for p in pieces], axis=0)
         o_s[t] = dot(pick, rows).astype(BF16)
+    copies = []
     for b in range(wanted // 16):
-        block = o_s[:, b * 16 : (b + 1) * 16, :].reshape(256, 256)
-        out_ref[b * 16 : (b + 1) * 16] = dot(order, block).astype(BF16).reshape(16, 16, 256)
+        here = pl.ds(b * 16, 16)
+        block = o_s[:, b * 16 : (b + 1) * 16, :].reshape(256, width)
+        out_s[b * 16 : (b + 1) * 16] = dot(order, block).astype(BF16).reshape(16, 16, width)
+        copies.append(pltpu.make_async_copy(out_s.at[here], out_hbm.at[here], sems.at[b]))
+        copies[-1].start()
+    for copy in copies:
+        copy.wait()
 
 
 def pick_rows(pick, pieces):
     steps, _, width = pieces[0].shape
     wanted = pick.shape[0]
+    vmem = pl.BlockSpec(memory_space=pltpu.VMEM)
     return pl.pallas_call(
         functools.partial(pick_kernel, len(pieces)),
-        out_shape=jax.ShapeDtypeStruct((wanted, steps, width), BF16),
-        scratch_shapes=[pltpu.VMEM((steps, wanted, width), BF16)],
+        out_shape=pltpu.HBM((wanted, steps, width), BF16),
+        in_specs=[vmem] * (1 + len(pieces)),
+        out_specs=pl.BlockSpec(memory_space=pl.ANY),
+        scratch_shapes=[
+            pltpu.VMEM((steps, wanted, width), BF16),
+            pltpu.VMEM((wanted, steps, width), BF16),
+            pltpu.SemaphoreType.DMA((wanted // 16,)),
+        ],
         compiler_params=pltpu.CompilerParams(vmem_limit_bytes=VMEM_LIMIT),
         name="pick_rows",
     )(pick, *pieces)
@@ -248,10 +260,9 @@
     )(*pieces, gain, wq, wkv)
 
 
-def gelu(x):
-    inner = x * (0.7978845608028654 + 0.035677408136300125 * (x * x))
-    half = 0.5 * x
-    return half + half * jnp.tanh(inner)
+def gelu_of_half(x):
+    inner = x * (1.5957691216057308 + 0.28541926509040096 * (x * x))
+    return x + x * jnp.tanh(inner)
 
 
 def rows_of(pieces, first, count):
@@ -338,11 +349,12 @@
         return factors, (e * inverse[:, None, :]).astype(BF16).reshape(H * remote, block).T
 
     def merge(t, factors, weights):
+        if t == 0:
+            for copy in merge_in:
+                copy.wait()
         far = dot(weights, by_head(rv_s[t]))
         ctx_s[t] = (lctx_s[t].astype(F32) * dot(factors, to_lanes) + far).astype(BF16)
 
-    for copy in merge_in:
-        copy.wait()
     upcoming, waiting = score(0), None
     for t in range(steps):
         scores, upcoming = upcoming, score(t + 1) if t + 1 < steps else None
@@ -364,7 +376,7 @@
         context = ctx_s[:, first : first + sb, :].reshape(steps * sb, width)
         after = x.astype(F32) + dot(context, wo_s[...])
         total[first] = after
-        ready[first] = rms(after, gain_ffn_ref[...])
+        ready[first] = rms(after, 0.5 * gain_ffn_ref[...])
 
     def up(first, n):
         return dot(ready[first], w_in_s[:, n * tile : (n + 1) * tile])
@@ -375,7 +387,7 @@
         if n == 0 and first + sb < block:
             open_rows(first + sb)
         later = up(*work[k + 1]) if k + 1 < len(work) else None
-        total[first] = total[first] + dot(gelu(upper).astype(BF16), w_out_s[n * tile : (n + 1) * tile, :])
+        total[first] = total[first] + dot(gelu_of_half(upper).astype(BF16), w_out_s[n * tile : (n + 1) * tile, :])
         upper = later
         if n < tiles - 1:
             continue

time: 49.8 us -> 49.6 us (level)
  no operation moved by 1% of the time
where the time goes in v7:
time: 49.6 us; the launch traced here: 49.2 us
  Pallas kernels  27.1 us (55%)
  starting transfers between devices  11.9 us (24%)
  waiting for transfers between devices  7.39 us (15%)
  local copies, waits for them, and re-layouts  2.41 us (5%)
    pallas_call x1, Pallas kernels, local_part(): pl.pallas_call(functools.partial(local_kernel, len(pieces)), out_shape=[p...  8.94 us
    pallas_call x1, Pallas kernels, finish(): pl.pallas_call(functools.partial(finish_kernel, len(pieces), split, sb),...  8.85 us
    pallas_call x4, Pallas kernels, time_block(): pl.pallas_call(functools.partial(time_kernel, split), out_shape=out_shape...  8 us
    all_to_all x1, starting transfers between devices, local(): lax.all_to_all(outgoing, 'sensor', split_axis=0, concat_axis=0, tiled=True)  6.08 us
    ppermute x4, starting transfers between devices, local(): got.append(lax.ppermute(send, 'tm', [(0, 1), (1, 0)]))  5.81 us
    all_to_all x1, waiting for transfers between devices, local(): lax.all_to_all(outgoing, 'sensor', split_axis=0, concat_axis=0, tiled=True)  3.91 us
    ppermute x4, waiting for transfers between devices, local(): got.append(lax.ppermute(send, 'tm', [(0, 1), (1, 0)]))  3.48 us
    unnamed x28, local copies, waits for them, and re-layouts  2.05 us
  transfers between devices with their start and end apart: 5, of which 3 were waited for; matrix products, arithmetic and copies ran while one was open for 1% of the time, Pallas kernels for 28%

profile of v7, /device:TPU:0, one launch (start us, length us, event | category | flops | bytes accessed | tf_op | source)
XLA Modules:
  0.0 49.2 jit_solution(14082231408657770376)
XLA Ops:
  0.0 0.0 copy-start
  0.0 0.0 copy-start.1
  0.0 0.0 copy-start.2
  0.0 0.0 copy-start.3
  0.0 2.9 %time_block.4 = (bf16[16,16,256]{2,1,0:T(8,128)(2,1)S(1)}, bf16[16,16,256]{2,1,0:T(8,128)(2,1)S(1)}) custom-call(s32[1]{0:T(128)} %bitcast.my_ref, bf16[64,32,256]{2,1,0:T(8,128)(2,1)} %x_ref.4, f32[1,256]{1,0:T(1,128)} %bitcast.6, bf16[256,256]{1,0:T(8,128)(2,1)} %wq_ref.7, bf16[256,512]{1,0:T(8,128)(2,1)} %wkv_ref.7, bf16[256,256]{1,0:T(8,128)(2,1)} %wo_ref.7), custom_call_target="tpu_custom_call" | custom-call | flops 402653184 | bytes 524288 | tf_op jit(solution)/shard_map/time_block/pallas_call | solution.py:130
  2.9 0.0 copy-start.4
  2.9 3.0 %collective-permute-start = (bf16[16,16,256]{2,1,0:T(8,128)(2,1)S(1)}, bf16[16,16,256]{2,1,0:T(8,128)(2,1)S(1)}, u32[]{:S(2)}, u32[]{:S(2)}) collective-permute-start(bf16[16,16,256]{2,1,0:T(8,128)(2,1)S(1)} %get-tuple-element.33), channel_id=1, source_target_pairs={{0,1},{1,0},{2,3},{3,2},{4,5},{5,4},{6,7},{7,6},{8,9},{9,8},{10,11... | collective-permute-start | bytes 393224 | tf_op jit(solution)/shard_map/ppermute | solution.py:484
  6.0 0.0 copy-done
  6.0 0.0 copy-done.1
  6.0 0.0 copy-done.2
  6.0 0.0 copy-done.3
  6.0 0.0 copy-done.4
  6.0 1.7 %time_block.5 = (bf16[16,16,256]{2,1,0:T(8,128)(2,1)S(1)}, bf16[16,16,256]{2,1,0:T(8,128)(2,1)S(1)}) custom-call(s32[1]{0:T(128)} %bitcast.my_ref, bf16[64,32,256]{2,1,0:T(8,128)(2,1)S(1)} %copy-done, f32[1,256]{1,0:T(1,128)S(1)} %bitcast.7, bf16[256,256]{1,0:T(8,128)(2,1)S(1)} %copy-done.2, bf16[256,512]{1,0:T(8,128)(2,1)S(1)} %copy-done.1, ...), custom_call_target="tpu_custom_call" | custom-call | flops 402653184 | bytes 524288 | tf_op jit(solution)/shard_map/time_block/pallas_call | solution.py:130
  7.7 0.6 %collective-permute-start.1 = (bf16[16,16,256]{2,1,0:T(8,128)(2,1)S(1)}, bf16[16,16,256]{2,1,0:T(8,128)(2,1)S(1)}, u32[]{:S(2)}, u32[]{:S(2)}) collective-permute-start(bf16[16,16,256]{2,1,0:T(8,128)(2,1)S(1)} %get-tuple-element.34), channel_id=1, source_target_pairs={{0,1},{1,0},{2,3},{3,2},{4,5},{5,4},{6,7},{7,6},{8,9},{9,8},{10,11... | collective-permute-start | bytes 393224 | tf_op jit(solution)/shard_map/ppermute | solution.py:484
  8.3 1.7 %time_block.6 = (bf16[16,16,256]{2,1,0:T(8,128)(2,1)S(1)}, bf16[16,16,256]{2,1,0:T(8,128)(2,1)S(1)}) custom-call(s32[1]{0:T(128)} %bitcast.my_ref, bf16[64,32,256]{2,1,0:T(8,128)(2,1)S(1)} %copy-done, f32[1,256]{1,0:T(1,128)S(1)} %bitcast.8, bf16[256,256]{1,0:T(8,128)(2,1)S(1)} %copy-done.2, bf16[256,512]{1,0:T(8,128)(2,1)S(1)} %copy-done.1, ...), custom_call_target="tpu_custom_call" | custom-call | flops 402653184 | bytes 524288 | tf_op jit(solution)/shard_map/time_block/pallas_call | solution.py:130
  10.0 1.5 %collective-permute-start.2 = (bf16[16,16,256]{2,1,0:T(8,128)(2,1)S(1)}, bf16[16,16,256]{2,1,0:T(8,128)(2,1)S(1)}, u32[]{:S(2)}, u32[]{:S(2)}) collective-permute-start(bf16[16,16,256]{2,1,0:T(8,128)(2,1)S(1)} %get-tuple-element.35), channel_id=1, source_target_pairs={{0,1},{1,0},{2,3},{3,2},{4,5},{5,4},{6,7},{7,6},{8,9},{9,8},{10,11... | collective-permute-start | bytes 393224 | tf_op jit(solution)/shard_map/ppermute | solution.py:484
  11.5 0.0 copy-start.12
  11.5 1.7 %time_block.7 = (bf16[16,16,256]{2,1,0:T(8,128)(2,1)S(1)}, bf16[16,16,256]{2,1,0:T(8,128)(2,1)S(1)}) custom-call(s32[1]{0:T(128)} %bitcast.my_ref, bf16[64,32,256]{2,1,0:T(8,128)(2,1)S(1)} %copy-done, f32[1,256]{1,0:T(1,128)S(1)} %bitcast.9, bf16[256,256]{1,0:T(8,128)(2,1)S(1)} %copy-done.2, bf16[256,512]{1,0:T(8,128)(2,1)S(1)} %copy-done.1, ...), custom_call_target="tpu_custom_call" | custom-call | flops 402653184 | bytes 524288 | tf_op jit(solution)/shard_map/time_block/pallas_call | solution.py:130
  13.2 0.6 %collective-permute-start.3 = (bf16[16,16,256]{2,1,0:T(8,128)(2,1)S(1)}, bf16[16,16,256]{2,1,0:T(8,128)(2,1)S(1)}, u32[]{:S(2)}, u32[]{:S(2)}) collective-permute-start(bf16[16,16,256]{2,1,0:T(8,128)(2,1)S(1)} %get-tuple-element.37), channel_id=1, source_target_pairs={{0,1},{1,0},{2,3},{3,2},{4,5},{5,4},{6,7},{7,6},{8,9},{9,8},{10,11... | collective-permute-start | bytes 393224 | tf_op jit(solution)/shard_map/ppermute | solution.py:484
  13.9 0.0 copy-start.11
  13.9 0.7 %copy-done.11 = s32[16,8]{0,1:T(8,128)S(1)} copy-done((s32[16,8]{0,1:T(8,128)S(1)}, s32[16,8]{0,1:T(8,128)}, u32[]{:S(2)}) %copy-start.11) | copy-done | bytes 536
  14.6 0.0 copy-done.12
  14.6 0.1 copy.16
  14.7 0.1 eq.25
  14.8 0.1 compare_convert_fusion.pick_ref
  14.8 0.0 collective-permute-done.refs_4_
  14.9 0.0 collective-permute-done.1.refs_5_
  14.9 1.3 %collective-permute-done.2.refs_6_ = bf16[16,16,256]{2,1,0:T(8,128)(2,1)S(1)} collective-permute-done((bf16[16,16,256]{2,1,0:T(8,128)(2,1)S(1)}, bf16[16,16,256]{2,1,0:T(8,128)(2,1)S(1)}, u32[]{:S(2)}, u32[]{:S(2)}) %collective-permute-start.2) | collective-permute-done | bytes 131104 | tf_op jit(solution)/shard_map/ppermute | solution.py:484
  16.1 2.2 %collective-permute-done.3.refs_7_ = bf16[16,16,256]{2,1,0:T(8,128)(2,1)S(1)} collective-permute-done((bf16[16,16,256]{2,1,0:T(8,128)(2,1)S(1)}, bf16[16,16,256]{2,1,0:T(8,128)(2,1)S(1)}, u32[]{:S(2)}, u32[]{:S(2)}) %collective-permute-start.3) | collective-permute-done | bytes 131104 | tf_op jit(solution)/shard_map/ppermute | solution.py:484
  18.3 1.3 %pick_rows.1 = bf16[64,16,256]{2,1,0:T(8,128)(2,1)} custom-call(bf16[64,128]{1,0:T(8,128)(2,1)S(1)} %compare_convert_fusion.pick_ref, bf16[16,16,256]{2,1,0:T(8,128)(2,1)S(1)} %get-tuple-element.23.refs_0_, bf16[16,16,256]{2,1,0:T(8,128)(2,1)S(1)} %get-tuple-element.26.refs_1_, bf16[16,16,256]{2,1,0:T(8,128)(2,1)S(1)} %get-tuple-element.29.refs_2_, ...), custom_call_target="tpu_custom_call" | custom-call | tf_op jit(solution)/shard_map/pick_rows/pallas_call | solution.py:177
  19.6 0.0 copy-start.7
  19.7 0.0 copy-start.8
  19.7 6.1 %all-to-all-start = ((bf16[16,4,16,256]{3,2,1,0:T(8,128)(2,1)}), bf16[16,4,16,256]{3,2,1,0:T(8,128)(2,1)S(1)}, u32[]{:S(2)}, u32[]{:S(2)}) async-start(bf16[16,4,16,256]{3,2,1,0:T(8,128)(2,1)} %bitcast.12), calls=%async_computation | async-start | bytes 1048576 | tf_op jit(solution)/shard_map/all_to_all | solution.py:501
  25.8 0.2 dynamic-slice_reduce_fusion
  26.0 0.0 copy-start.13
  26.0 0.7 %copy-done.13 = s32[1,8]{1,0:T(1,128)S(1)} copy-done((s32[1,8]{1,0:T(1,128)S(1)}, s32[1,8]{1,0:T(1,128)}, u32[]{:S(2)}) %copy-start.13) | copy-done | bytes 56
  26.6 0.1 pad_add_fusion.numbers_ref
  26.7 0.0 copy-start.10
  26.7 0.0 copy-done.7
  26.7 0.0 copy-done.8
  26.7 0.7 %copy-done.10 = f32[256]{0:T(256)S(1)} copy-done((f32[256]{0:T(256)S(1)}, f32[256]{0:T(256)}, u32[]{:S(2)}) %copy-start.10) | copy-done | bytes 1048
  27.4 0.0 copy-start.5
  27.4 8.9 %local_keys.1 = (bf16[16,256,128]{2,1,0:T(8,128)(2,1)}, bf16[16,128,256]{2,1,0:T(8,128)(2,1)}, f32[16,16,128]{2,1,0:T(8,128)S(1)}) custom-call(bf16[16,16,256]{2,1,0:T(8,128)(2,1)S(1)} %get-tuple-element.23.refs_0_, bf16[16,16,256]{2,1,0:T(8,128)(2,1)S(1)} %get-tuple-element.26.refs_1_, bf16[16,16,256]{2,1,0:T(8,128)(2,1)S(1)} %get-tuple-element.29.refs_2_, ...), custom_call_target="tpu_custom_call" | custom-call | flops 1610612736 | bytes 5242880 | tf_op jit(solution)/shard_map/local_keys/pallas_call | solution.py:240
  36.3 3.9 %all-to-all-done.refs_8_ = bf16[16,4,16,256]{3,2,1,0:T(8,128)(2,1)S(1)} async-done(((bf16[16,4,16,256]{3,2,1,0:T(8,128)(2,1)}), bf16[16,4,16,256]{3,2,1,0:T(8,128)(2,1)S(1)}, u32[]{:S(2)}, u32[]{:S(2)}) %all-to-all-start) | async-done | bytes 524320 | tf_op jit(solution)/shard_map/all_to_all | solution.py:501
  40.2 0.0 copy-done.5
  40.2 0.0 copy-done.6
  40.2 0.0 copy-done.9
  40.2 8.8 %remote_keys_and_feed_forward.1 = bf16[128,16,256]{2,1,0:T(8,128)(2,1)} custom-call(s32[17]{0:T(128)S(1)} %pad_add_fusion.numbers_ref, bf16[16,16,256]{2,1,0:T(8,128)(2,1)S(1)} %get-tuple-element.23.refs_0_, bf16[16,16,256]{2,1,0:T(8,128)(2,1)S(1)} %get-tuple-element.26.refs_1_, bf16[16,16,256]{2,1,0:T(8,128)(2,1)S(1)} %get-tuple-element.29.refs_2_, ...), custom_call_target="tpu_custom_call" | custom-call | flops 2415919104 | bytes 6291456 | tf_op jit(solution)/shard_map/remote_keys_and_feed_forward/pallas_call | solution.py:423
  (5 shorter events, 0.0 us)
Async XLA Ops:
  0.0 6.0 %copy-start = (bf16[64,32,256]{2,1,0:T(8,128)(2,1)S(1)}, bf16[64,32,256]{2,1,0:T(8,128)(2,1)}, u32[]{:S(2)}) copy-start(bf16[64,32,256]{2,1,0:T(8,128)(2,1)} %x_ref.4) | copy-start | bytes 3145732
  0.0 6.0 %copy-start.1 = (bf16[256,512]{1,0:T(8,128)(2,1)S(1)}, bf16[256,512]{1,0:T(8,128)(2,1)}, u32[]{:S(2)}) copy-start(bf16[256,512]{1,0:T(8,128)(2,1)} %wkv_ref.7) | copy-start | bytes 786436
  0.0 6.0 %copy-start.2 = (bf16[256,256]{1,0:T(8,128)(2,1)S(1)}, bf16[256,256]{1,0:T(8,128)(2,1)}, u32[]{:S(2)}) copy-start(bf16[256,256]{1,0:T(8,128)(2,1)} %wq_ref.7) | copy-start | bytes 393220
  0.0 6.0 %copy-start.3 = (bf16[256,256]{1,0:T(8,128)(2,1)S(1)}, bf16[256,256]{1,0:T(8,128)(2,1)}, u32[]{:S(2)}) copy-start(bf16[256,256]{1,0:T(8,128)(2,1)} %wo_ref.7) | copy-start | bytes 393220
  2.9 3.0 %copy-start.4 = (f32[256]{0:T(256)S(1)}, f32[256]{0:T(256)}, u32[]{:S(2)}) copy-start(f32[256]{0:T(256)} %param.16) | copy-start | bytes 3076
  2.9 11.9 %collective-permute-start = (bf16[16,16,256]{2,1,0:T(8,128)(2,1)S(1)}, bf16[16,16,256]{2,1,0:T(8,128)(2,1)S(1)}, u32[]{:S(2)}, u32[]{:S(2)}) collective-permute-start(bf16[16,16,256]{2,1,0:T(8,128)(2,1)S(1)} %get-tuple-element.33), channel_id=1, source_target_pairs={{0,1},{1,0},{2,3},{3,2},{4,5},{5,4},{6,7},{7,6},{8,9},{9,8},{10,11... | collective-permute-start | bytes 393224 | tf_op jit(solution)/shard_map/ppermute | solution.py:484
  7.7 7.2 %collective-permute-start.1 = (bf16[16,16,256]{2,1,0:T(8,128)(2,1)S(1)}, bf16[16,16,256]{2,1,0:T(8,128)(2,1)S(1)}, u32[]{:S(2)}, u32[]{:S(2)}) collective-permute-start(bf16[16,16,256]{2,1,0:T(8,128)(2,1)S(1)} %get-tuple-element.34), channel_id=1, source_target_pairs={{0,1},{1,0},{2,3},{3,2},{4,5},{5,4},{6,7},{7,6},{8,9},{9,8},{10,11... | collective-permute-start | bytes 393224 | tf_op jit(solution)/shard_map/ppermute | solution.py:484
  10.0 6.1 %collective-permute-start.2 = (bf16[16,16,256]{2,1,0:T(8,128)(2,1)S(1)}, bf16[16,16,256]{2,1,0:T(8,128)(2,1)S(1)}, u32[]{:S(2)}, u32[]{:S(2)}) collective-permute-start(bf16[16,16,256]{2,1,0:T(8,128)(2,1)S(1)} %get-tuple-element.35), channel_id=1, source_target_pairs={{0,1},{1,0},{2,3},{3,2},{4,5},{5,4},{6,7},{7,6},{8,9},{9,8},{10,11... | collective-permute-start | bytes 393224 | tf_op jit(solution)/shard_map/ppermute | solution.py:484
  11.5 3.0 %copy-start.12 = (s32[16,8,4]{0,2,1:T(4,128)S(1)}, s32[16,8,4]{0,2,1:T(4,128)}, u32[]{:S(2)}) copy-start(s32[16,8,4]{0,2,1:T(4,128)} %param.29) | copy-start | bytes 6148
  13.2 5.1 %collective-permute-start.3 = (bf16[16,16,256]{2,1,0:T(8,128)(2,1)S(1)}, bf16[16,16,256]{2,1,0:T(8,128)(2,1)S(1)}, u32[]{:S(2)}, u32[]{:S(2)}) collective-permute-start(bf16[16,16,256]{2,1,0:T(8,128)(2,1)S(1)} %get-tuple-element.37), channel_id=1, source_target_pairs={{0,1},{1,0},{2,3},{3,2},{4,5},{5,4},{6,7},{7,6},{8,9},{9,8},{10,11... | collective-permute-start | bytes 393224 | tf_op jit(solution)/shard_map/ppermute | solution.py:484
  13.9 0.7 %copy-start.11 = (s32[16,8]{0,1:T(8,128)S(1)}, s32[16,8]{0,1:T(8,128)}, u32[]{:S(2)}) copy-start(s32[16,8]{0,1:T(8,128)} %param.27) | copy-start | bytes 1540
  19.6 7.0 %copy-start.7 = (bf16[256,512]{1,0:T(8,128)(2,1)S(1)}, bf16[256,512]{1,0:T(8,128)(2,1)}, u32[]{:S(2)}) copy-start(bf16[256,512]{1,0:T(8,128)(2,1)} %refs_10_.3) | copy-start | bytes 786436
  19.7 7.0 %copy-start.8 = (bf16[256,256]{1,0:T(8,128)(2,1)S(1)}, bf16[256,256]{1,0:T(8,128)(2,1)}, u32[]{:S(2)}) copy-start(bf16[256,256]{1,0:T(8,128)(2,1)} %refs_9_.1) | copy-start | bytes 393220
  19.7 20.6 %all-to-all-start = ((bf16[16,4,16,256]{3,2,1,0:T(8,128)(2,1)}), bf16[16,4,16,256]{3,2,1,0:T(8,128)(2,1)S(1)}, u32[]{:S(2)}, u32[]{:S(2)}) async-start(bf16[16,4,16,256]{3,2,1,0:T(8,128)(2,1)} %bitcast.12), calls=%async_computation | async-start | bytes 1048576 | tf_op jit(solution)/shard_map/all_to_all | solution.py:501
  26.0 0.7 %copy-start.13 = (s32[1,8]{1,0:T(1,128)S(1)}, s32[1,8]{1,0:T(1,128)}, u32[]{:S(2)}) copy-start(s32[1,8]{1,0:T(1,128)} %param.28) | copy-start | bytes 100
  26.7 0.7 %copy-start.10 = (f32[256]{0:T(256)S(1)}, f32[256]{0:T(256)}, u32[]{:S(2)}) copy-start(f32[256]{0:T(256)} %param.20) | copy-start | bytes 3076
  27.4 12.9 %copy-start.5 = (bf16[256,1024]{1,0:T(8,128)(2,1)S(1)}, bf16[256,1024]{1,0:T(8,128)(2,1)}, u32[]{:S(2)}) copy-start(bf16[256,1024]{1,0:T(8,128)(2,1)} %refs_13_.1) | copy-start | bytes 1572868
  27.4 12.9 %copy-start.6 = (bf16[1024,256]{1,0:T(8,128)(2,1)S(1)}, bf16[1024,256]{1,0:T(8,128)(2,1)}, u32[]{:S(2)}) copy-start(bf16[1024,256]{1,0:T(8,128)(2,1)} %refs_14_.1) | copy-start | bytes 1572868
  27.4 12.9 %copy-start.9 = (bf16[256,256]{1,0:T(8,128)(2,1)S(1)}, bf16[256,256]{1,0:T(8,128)(2,1)}, u32[]{:S(2)}) copy-start(bf16[256,256]{1,0:T(8,128)(2,1)} %refs_12_.1) | copy-start | bytes 393220

commit v8 on v7

--- a/solution.py
+++ b/solution.py
@@ -103,13 +103,9 @@
         out_ref[...] = after.reshape(sensors, steps, width)
         return
     after_s[...] = after.reshape(sensors, steps, width)
-    order = swap16()
     mine = my_ref[0]
     for ref, part in ((keep_ref, mine), (send_ref, 1 - mine)):
-        rows16 = after_s[:, pl.ds(pl.multiple_of(part * 16, 16), 16), :]
-        for b in range(sensors // 16):
-            block = rows16[b * 16 : (b + 1) * 16].reshape(256, width)
-            ref[:, b * 16 : (b + 1) * 16, :] = dot(order, block).astype(BF16).reshape(16, 16, width)
+        ref[...] = after_s[:, pl.ds(pl.multiple_of(part * 16, 16), 16), :]
 
 
 def time_block(tokens, my, gain, wq, wkv, wo, first, count, split):
@@ -120,8 +116,8 @@
     rows = sb * steps
     full = lambda a: pl.BlockSpec(a.shape, lambda i, *_: (0,) * a.ndim)
     if split:
-        out_shape = [jax.ShapeDtypeStruct((16, count, width), BF16)] * 2
-        out_specs = [pl.BlockSpec((16, sb, width), lambda i, *_: (0, i, 0))] * 2
+        out_shape = [jax.ShapeDtypeStruct((count, 16, width), BF16)] * 2
+        out_specs = [pl.BlockSpec((sb, 16, width), lambda i, *_: (i, 0, 0))] * 2
         extra = [pltpu.VMEM((sb, steps, width), BF16)]
     else:
         out_shape = jax.ShapeDtypeStruct((count, steps, width), BF16)
@@ -151,42 +147,40 @@
     )(my, tokens, gain, wq, wkv, wo)
 
 
-def pick_kernel(n, pick_ref, *refs):
-    pieces, (out_hbm, o_s, out_s, sems) = refs[:n], refs[n:]
-    steps, wanted, width = o_s.shape
-    order = swap16()
-    pick = pick_ref[...]
-    for t in range(steps):
-        rows = jnp.concatenate([p[t] for p in pieces], axis=0)
-        o_s[t] = dot(pick, rows).astype(BF16)
+def pick_kernel(n, wanted_ref, *refs):
+    pieces, (out_hbm, x_s, out_s, sems) = refs[:n], refs[n:]
+    place = 0
+    for p in pieces:
+        x_s[place : place + p.shape[0]] = p[...]
+        place += p.shape[0]
     copies = []
-    for b in range(wanted // 16):
+    for b in range(out_s.shape[0] // 16):
+        for j in range(b * 16, (b + 1) * 16):
+            out_s[j] = x_s[wanted_ref[j]]
         here = pl.ds(b * 16, 16)
-        block = o_s[:, b * 16 : (b + 1) * 16, :].reshape(256, width)
-        out_s[b * 16 : (b + 1) * 16] = dot(order, block).astype(BF16).reshape(16, 16, width)
         copies.append(pltpu.make_async_copy(out_s.at[here], out_hbm.at[here], sems.at[b]))
         copies[-1].start()
     for copy in copies:
         copy.wait()
 
 
-def pick_rows(pick, pieces):
-    steps, _, width = pieces[0].shape
-    wanted = pick.shape[0]
-    vmem = pl.BlockSpec(memory_space=pltpu.VMEM)
+def pick_rows(wanted, pieces):
+    _, steps, width = pieces[0].shape
+    count = wanted.shape[0]
+    block = sum(p.shape[0] for p in pieces)
     return pl.pallas_call(
         functools.partial(pick_kernel, len(pieces)),
-        out_shape=pltpu.HBM((wanted, steps, width), BF16),
-        in_specs=[vmem] * (1 + len(pieces)),
+        out_shape=pltpu.HBM((count, steps, width), BF16),
+        in_specs=[pl.BlockSpec(memory_space=pltpu.SMEM)] + [pl.BlockSpec(memory_space=pltpu.VMEM)] * len(pieces),
         out_specs=pl.BlockSpec(memory_space=pl.ANY),
         scratch_shapes=[
-            pltpu.VMEM((steps, wanted, width), BF16),
-            pltpu.VMEM((wanted, steps, width), BF16),
-            pltpu.SemaphoreType.DMA((wanted // 16,)),
+            pltpu.VMEM((block, steps, width), BF16),
+            pltpu.VMEM((count, steps, width), BF16),
+            pltpu.SemaphoreType.DMA((count // 16,)),
         ],
         compiler_params=pltpu.CompilerParams(vmem_limit_bytes=VMEM_LIMIT),
         name="pick_rows",
-    )(pick, *pieces)
+    )(wanted, *pieces)
 
 
 def pair_scores(q, k, masks, pair):
@@ -195,17 +189,25 @@
     return dot_nt(k[:, cols], spread)
 
 
-def local_kernel(n, *refs):
+def local_kernel(n, split, *refs):
     pieces = refs[:n]
-    gain_ref, wq_ref, wkv_ref, qt_ref, ctx_ref, stat_ref, wqt_s, wvt_s = refs[n:]
+    gain_ref, wq_ref, wkv_ref, x_ref, qt_ref, ctx_ref, stat_ref, wqt_s, wvt_s = refs[n:]
     tb, width, block = qt_ref.shape
 
     @pl.when(pl.program_id(0) == 0)
     def _():
         wvt_s[...] = wkv_ref[:, width:].T
+        place = 0
+        if not split:
+            x_ref[...] = pieces[0][...]
+        for p in pieces if split else []:
+            for b in range(0, p.shape[0], 16):
+                turned = dot(swap16(), p[b : b + 16].reshape(256, width)).astype(BF16)
+                x_ref[:, place + b : place + b + 16, :] = turned.reshape(16, 16, width)
+            place += p.shape[0]
         wqt_s[...] = wq_ref[...].T
 
-    x = jnp.concatenate([p[t] for t in range(tb) for p in pieces], axis=0).astype(F32)
+    x = x_ref[pl.ds(pl.program_id(0) * tb, tb)].reshape(tb * block, width).astype(F32)
     normed = rms(x, gain_ref[...])
     q = dot(normed, wq_ref[...]).astype(BF16)
     k = dot(normed, wkv_ref[:, :width]).astype(BF16)
@@ -231,22 +233,25 @@
         ctx_ref[t] = jnp.concatenate(context, axis=0).T
 
 
-def local_part(pieces, gain, wq, wkv):
-    steps, _, width = pieces[0].shape
-    block = sum(p.shape[1] for p in pieces)
+def local_part(pieces, gain, wq, wkv, split):
+    sensors, steps = (0, 1) if split else (1, 0)
+    steps, width = pieces[0].shape[steps], pieces[0].shape[2]
+    block = sum(p.shape[sensors] for p in pieces)
     tb = 4
     full = lambda a: pl.BlockSpec(a.shape, lambda i: (0,) * a.ndim)
     per_t = lambda *shape: pl.BlockSpec((tb,) + shape, lambda i: (i, 0, 0))
     return pl.pallas_call(
-        functools.partial(local_kernel, len(pieces)),
+        functools.partial(local_kernel, len(pieces), split),
         out_shape=[
+            pltpu.HBM((steps, block, width), BF16),
             pltpu.HBM((steps, width, block), BF16),
             pltpu.HBM((steps, block, width), BF16),
             jax.ShapeDtypeStruct((steps, 2 * H, block), F32),
         ],
         grid=(steps // tb,),
-        in_specs=[per_t(p.shape[1], width) for p in pieces] + [full(gain), full(wq), full(wkv)],
+        in_specs=[full(p) for p in pieces] + [full(gain), full(wq), full(wkv)],
         out_specs=[
+            pl.BlockSpec((steps, block, width), lambda i: (0, 0, 0)),
             per_t(width, block),
             per_t(block, width),
             per_t(2 * H, block),
@@ -265,21 +270,10 @@
     return x + x * jnp.tanh(inner)
 
 
-def rows_of(pieces, first, count):
-    parts, start = [], 0
-    for p in pieces:
-        low, high = max(first, start), min(first + count, start + p.shape[1])
-        if low < high:
-            parts.append(p[:, low - start : high - start, :])
-        start += p.shape[1]
-    return jnp.concatenate(parts, axis=1)
-
-
-def finish_kernel(n, split, sb, numbers_ref, *refs):
-    pieces = refs[:n]
-    in_ref, gain_ref, wkv_ref, stat_ref, wo_s, w_in_s, w_out_s = refs[n : n + 7]
-    gain_ffn_hbm, qt_hbm, lctx_hbm, out_hbm = refs[n + 7 : n + 11]
-    raw_s, rn_s, rk_s, rv_s, ctx_s, out_s, qt_s, lctx_s, gain_ffn_ref, sems, out_sems = refs[n + 11 :]
+def finish_kernel(split, sb, numbers_ref, *refs):
+    in_ref, gain_ref, wkv_ref, stat_ref, wo_s, w_in_s, w_out_s = refs[:7]
+    gain_ffn_hbm, qt_hbm, lctx_hbm, x_hbm, out_hbm = refs[7:12]
+    raw_s, rn_s, rk_s, rv_s, ctx_s, out_s, qt_s, lctx_s, x_s, gain_ffn_ref, sems, out_sems = refs[12:]
     steps, width, block = qt_s.shape
     remote = rn_s.shape[1]
     slots = remote // REMOTE_SENSORS
@@ -293,7 +287,7 @@
 
     score_in = [fetch(qt_hbm, qt_s)]
     merge_in = [fetch(lctx_hbm, lctx_s)]
-    ffn_in = [fetch(gain_ffn_hbm, gain_ffn_ref)]
+    ffn_in = [fetch(x_hbm, x_s), fetch(gain_ffn_hbm, gain_ffn_ref)]
 
     order = swap16() if split else None
     lane_head = lax.broadcasted_iota(jnp.int32, (1, 128), 1) // HEAD
@@ -372,7 +366,7 @@
     ready, total, copies = {}, {}, []
 
     def open_rows(first):
-        x = rows_of(pieces, first, sb).reshape(steps * sb, width)
+        x = x_s[:, first : first + sb, :].reshape(steps * sb, width)
         context = ctx_s[:, first : first + sb, :].reshape(steps * sb, width)
         after = x.astype(F32) + dot(context, wo_s[...])
         total[first] = after
@@ -410,20 +404,20 @@
         copy.wait()
 
 
-def finish(numbers, pieces, incoming, local, gain, wkv, wo, gain_ffn, w_in, w_out, split):
-    qt, lctx, stat = local
+def finish(numbers, incoming, local, gain, wkv, wo, gain_ffn, w_in, w_out, split):
+    x, qt, lctx, stat = local
     steps, width, block = qt.shape
     remote = (numbers.shape[0] - 1) // 2 * REMOTE_SENSORS
     sb = 32
     hbm = pl.BlockSpec(memory_space=pl.ANY)
-    near = [*pieces, incoming, gain, wkv, stat, wo, w_in, w_out]
+    near = [incoming, gain, wkv, stat, wo, w_in, w_out]
     pin = lambda arrays: [pltpu.with_memory_space_constraint(a, pltpu.HBM) for a in arrays]
     vmem = pl.BlockSpec(memory_space=pltpu.VMEM)
     buffer = lambda *shape: pltpu.VMEM(shape, BF16)
     return pl.pallas_call(
-        functools.partial(finish_kernel, len(pieces), split, sb),
+        functools.partial(finish_kernel, split, sb),
         out_shape=jax.ShapeDtypeStruct((block, steps, width) if split else (steps, block, width), BF16),
-        in_specs=[pl.BlockSpec(memory_space=pltpu.SMEM)] + [vmem] * len(near) + [hbm] * 3,
+        in_specs=[pl.BlockSpec(memory_space=pltpu.SMEM)] + [vmem] * len(near) + [hbm] * 4,
         out_specs=hbm,
         scratch_shapes=[
             buffer(remote, steps, width),
@@ -434,8 +428,9 @@
             buffer(block, steps, width) if split else buffer(steps, block, width),
             buffer(steps, width, block),
             buffer(steps, block, width),
+            buffer(steps, block, width),
             pltpu.VMEM(gain_ffn.shape, F32),
-            pltpu.SemaphoreType.DMA((3,)),
+            pltpu.SemaphoreType.DMA((4,)),
             pltpu.SemaphoreType.DMA((block // sb,)),
         ],
         compiler_params=pltpu.CompilerParams(vmem_limit_bytes=VMEM_LIMIT),
@@ -443,7 +438,7 @@
             flops=steps * block * width * width * 18, bytes_accessed=steps * block * width * 12, transcendentals=0
         ),
         name="remote_keys_and_feed_forward",
-    )(numbers, *near, *pin([gain_ffn, qt, lctx]))
+    )(numbers, *near, *pin([gain_ffn, qt, lctx, x]))
 
 
 def local(
@@ -492,17 +487,15 @@
     own = lax.dynamic_index_in_dim(neighbour_blocks, block_index, 0, keepdims=False)
     numbers = jnp.concatenate([mine.reshape(1), own, slot_used_mask[0]])
     if split:
-        place = (jnp.arange(block) + mine * sensors_here) % block
-        pick = (wanted[:, None] == place[None, :]).astype(BF16)
-        outgoing = pick_rows(pick, pieces)
+        outgoing = pick_rows((wanted + (tm - mine) * sensors_here) % block, pieces)
     else:
         outgoing = jnp.take(whole, wanted, axis=0)
     outgoing = outgoing.reshape(block_count, REMOTE_SENSORS, group, width)
     incoming = lax.all_to_all(outgoing, "sensor", split_axis=0, concat_axis=0, tiled=True)
     if not split:
         incoming = jnp.take(incoming, own, axis=0).reshape(-1, group, width).transpose(1, 0, 2)
-    near = local_part(pieces, gain_graph, wq_graph, wkv_graph)
-    out = finish(numbers, pieces, incoming, near, gain_graph, wkv_graph, wo_graph, gain_ffn, w_in, w_out, split)
+    near = local_part(pieces, gain_graph, wq_graph, wkv_graph, split)
+    out = finish(numbers, incoming, near, gain_graph, wkv_graph, wo_graph, gain_ffn, w_in, w_out, split)
     return out if split else out.transpose(1, 0, 2)
 
 

time: 49.6 us -> 49.2 us (level)
    pallas_call x4, Pallas kernels: 8 us -> 6.97 us  [time_block(): pl.pallas_call(functools.partial(time_kernel, split), out_shape=out_shape...]
    all_to_all x1, waiting for transfers between devices: 3.91 us -> 3.31 us  [local(): lax.all_to_all(outgoing, 'sensor', split_axis=0, concat_axis=0, tiled=True)]
    pallas_call x2, Pallas kernels: 17.8 us -> 18.4 us  [the longest x1 9.54 us: local_part(): pl.pallas_call(functools.partial(local_kernel, len(pieces), split), out_s...]
    ppermute x4, waiting for transfers between devices: 3.48 us -> 4.04 us  [local(): got.append(lax.ppermute(send, 'tm', [(0, 1), (1, 0)]))]
where the time goes in v8:
time: 49.2 us; the launch traced here: 48.9 us
  Pallas kernels  26.8 us (54%)
  starting transfers between devices  12 us (24%)
  waiting for transfers between devices  7.35 us (15%)
  local copies, waits for them, and re-layouts  2.42 us (5%)
    pallas_call x1, Pallas kernels, local_part(): pl.pallas_call(functools.partial(local_kernel, len(pieces), split), out_s...  9.54 us
    pallas_call x1, Pallas kernels, finish(): pl.pallas_call(functools.partial(finish_kernel, split, sb), out_shape=jax...  8.84 us
    pallas_call x4, Pallas kernels, time_block(): pl.pallas_call(functools.partial(time_kernel, split), out_shape=out_shape...  6.97 us
    all_to_all x1, starting transfers between devices, local(): lax.all_to_all(outgoing, 'sensor', split_axis=0, concat_axis=0, tiled=True)  6.15 us
    ppermute x4, starting transfers between devices, local(): got.append(lax.ppermute(send, 'tm', [(0, 1), (1, 0)]))  5.81 us
    ppermute x4, waiting for transfers between devices, local(): got.append(lax.ppermute(send, 'tm', [(0, 1), (1, 0)]))  4.04 us
    all_to_all x1, waiting for transfers between devices, local(): lax.all_to_all(outgoing, 'sensor', split_axis=0, concat_axis=0, tiled=True)  3.31 us
    unnamed x28, local copies, waits for them, and re-layouts  2.06 us
  transfers between devices with their start and end apart: 5, of which 3 were waited for; matrix products, arithmetic and copies ran while one was open for 1% of the time, Pallas kernels for 28%

profile of v8, /device:TPU:0, one launch (start us, length us, event | category | flops | bytes accessed | tf_op | source)
XLA Modules:
  0.0 48.9 jit_solution(5564794224306052285)
XLA Ops:
  0.0 0.0 copy-start.1
  0.0 0.0 copy-start.2
  0.0 0.0 copy-start.3
  0.0 2.7 %time_block.4 = (bf16[16,16,256]{2,1,0:T(8,128)(2,1)S(1)}, bf16[16,16,256]{2,1,0:T(8,128)(2,1)S(1)}) custom-call(s32[1]{0:T(128)} %bitcast.my_ref, bf16[64,32,256]{2,1,0:T(8,128)(2,1)} %x_ref.4, f32[1,256]{1,0:T(1,128)} %bitcast.6, bf16[256,256]{1,0:T(8,128)(2,1)} %wq_ref.7, bf16[256,512]{1,0:T(8,128)(2,1)} %wkv_ref.7, bf16[256,256]{1,0:T(8,128)(2,1)} %wo_ref.7), custom_call_target="tpu_custom_call" | custom-call | flops 402653184 | bytes 524288 | tf_op jit(solution)/shard_map/time_block/pallas_call | solution.py:126
  2.7 0.0 copy-start.4
  2.7 3.0 %collective-permute-start = (bf16[16,16,256]{2,1,0:T(8,128)(2,1)S(1)}, bf16[16,16,256]{2,1,0:T(8,128)(2,1)S(1)}, u32[]{:S(2)}, u32[]{:S(2)}) collective-permute-start(bf16[16,16,256]{2,1,0:T(8,128)(2,1)S(1)} %get-tuple-element.34), channel_id=1, source_target_pairs={{0,1},{1,0},{2,3},{3,2},{4,5},{5,4},{6,7},{7,6},{8,9},{9,8},{10,11... | collective-permute-start | bytes 393224 | tf_op jit(solution)/shard_map/ppermute | solution.py:479
  5.7 0.0 copy-done
  5.7 0.0 copy-done.1
  5.7 0.0 copy-done.2
  5.7 0.0 copy-done.3
  5.7 0.0 copy-done.4
  5.7 1.4 %time_block.5 = (bf16[16,16,256]{2,1,0:T(8,128)(2,1)S(1)}, bf16[16,16,256]{2,1,0:T(8,128)(2,1)S(1)}) custom-call(s32[1]{0:T(128)} %bitcast.my_ref, bf16[64,32,256]{2,1,0:T(8,128)(2,1)S(1)} %copy-done, f32[1,256]{1,0:T(1,128)S(1)} %bitcast.7, bf16[256,256]{1,0:T(8,128)(2,1)S(1)} %copy-done.2, bf16[256,512]{1,0:T(8,128)(2,1)S(1)} %copy-done.1, ...), custom_call_target="tpu_custom_call" | custom-call | flops 402653184 | bytes 524288 | tf_op jit(solution)/shard_map/time_block/pallas_call | solution.py:126
  7.2 0.6 %collective-permute-start.1 = (bf16[16,16,256]{2,1,0:T(8,128)(2,1)S(1)}, bf16[16,16,256]{2,1,0:T(8,128)(2,1)S(1)}, u32[]{:S(2)}, u32[]{:S(2)}) collective-permute-start(bf16[16,16,256]{2,1,0:T(8,128)(2,1)S(1)} %get-tuple-element.35), channel_id=1, source_target_pairs={{0,1},{1,0},{2,3},{3,2},{4,5},{5,4},{6,7},{7,6},{8,9},{9,8},{10,11... | collective-permute-start | bytes 393224 | tf_op jit(solution)/shard_map/ppermute | solution.py:479
  7.8 1.4 %time_block.6 = (bf16[16,16,256]{2,1,0:T(8,128)(2,1)S(1)}, bf16[16,16,256]{2,1,0:T(8,128)(2,1)S(1)}) custom-call(s32[1]{0:T(128)} %bitcast.my_ref, bf16[64,32,256]{2,1,0:T(8,128)(2,1)S(1)} %copy-done, f32[1,256]{1,0:T(1,128)S(1)} %bitcast.8, bf16[256,256]{1,0:T(8,128)(2,1)S(1)} %copy-done.2, bf16[256,512]{1,0:T(8,128)(2,1)S(1)} %copy-done.1, ...), custom_call_target="tpu_custom_call" | custom-call | flops 402653184 | bytes 524288 | tf_op jit(solution)/shard_map/time_block/pallas_call | solution.py:126
  9.3 1.5 %collective-permute-start.2 = (bf16[16,16,256]{2,1,0:T(8,128)(2,1)S(1)}, bf16[16,16,256]{2,1,0:T(8,128)(2,1)S(1)}, u32[]{:S(2)}, u32[]{:S(2)}) collective-permute-start(bf16[16,16,256]{2,1,0:T(8,128)(2,1)S(1)} %get-tuple-element.36), channel_id=1, source_target_pairs={{0,1},{1,0},{2,3},{3,2},{4,5},{5,4},{6,7},{7,6},{8,9},{9,8},{10,11... | collective-permute-start | bytes 393224 | tf_op jit(solution)/shard_map/ppermute | solution.py:479
  10.8 0.0 copy-start.12
  10.8 1.4 %time_block.7 = (bf16[16,16,256]{2,1,0:T(8,128)(2,1)S(1)}, bf16[16,16,256]{2,1,0:T(8,128)(2,1)S(1)}) custom-call(s32[1]{0:T(128)} %bitcast.my_ref, bf16[64,32,256]{2,1,0:T(8,128)(2,1)S(1)} %copy-done, f32[1,256]{1,0:T(1,128)S(1)} %bitcast.9, bf16[256,256]{1,0:T(8,128)(2,1)S(1)} %copy-done.2, bf16[256,512]{1,0:T(8,128)(2,1)S(1)} %copy-done.1, ...), custom_call_target="tpu_custom_call" | custom-call | flops 402653184 | bytes 524288 | tf_op jit(solution)/shard_map/time_block/pallas_call | solution.py:126
  12.2 0.6 %collective-permute-start.3 = (bf16[16,16,256]{2,1,0:T(8,128)(2,1)S(1)}, bf16[16,16,256]{2,1,0:T(8,128)(2,1)S(1)}, u32[]{:S(2)}, u32[]{:S(2)}) collective-permute-start(bf16[16,16,256]{2,1,0:T(8,128)(2,1)S(1)} %get-tuple-element.38), channel_id=1, source_target_pairs={{0,1},{1,0},{2,3},{3,2},{4,5},{5,4},{6,7},{7,6},{8,9},{9,8},{10,11... | collective-permute-start | bytes 393224 | tf_op jit(solution)/shard_map/ppermute | solution.py:479
  12.9 0.0 copy-start.11
  12.9 0.7 %copy-done.11 = s32[16,8]{0,1:T(8,128)S(1)} copy-done((s32[16,8]{0,1:T(8,128)S(1)}, s32[16,8]{0,1:T(8,128)}, u32[]{:S(2)}) %copy-start.11) | copy-done | bytes 536
  13.6 0.0 copy-done.12
  13.6 0.1 copy.16
  13.7 0.1 add.22
  13.8 0.0 collective-permute-done.refs_4_
  13.8 0.0 collective-permute-done.1.refs_5_
  13.8 2.0 %collective-permute-done.2.refs_6_ = bf16[16,16,256]{2,1,0:T(8,128)(2,1)S(1)} collective-permute-done((bf16[16,16,256]{2,1,0:T(8,128)(2,1)S(1)}, bf16[16,16,256]{2,1,0:T(8,128)(2,1)S(1)}, u32[]{:S(2)}, u32[]{:S(2)}) %collective-permute-start.2) | collective-permute-done | bytes 131104 | tf_op jit(solution)/shard_map/ppermute | solution.py:479
  15.8 2.0 %collective-permute-done.3.refs_7_ = bf16[16,16,256]{2,1,0:T(8,128)(2,1)S(1)} collective-permute-done((bf16[16,16,256]{2,1,0:T(8,128)(2,1)S(1)}, bf16[16,16,256]{2,1,0:T(8,128)(2,1)S(1)}, u32[]{:S(2)}, u32[]{:S(2)}) %collective-permute-start.3) | collective-permute-done | bytes 131104 | tf_op jit(solution)/shard_map/ppermute | solution.py:479
  17.8 1.4 %pick_rows.1 = bf16[64,16,256]{2,1,0:T(8,128)(2,1)} custom-call(s32[64]{0:T(128)S(1)} %and_select_fusion.wanted_ref, bf16[16,16,256]{2,1,0:T(8,128)(2,1)S(1)} %get-tuple-element.24.refs_0_, bf16[16,16,256]{2,1,0:T(8,128)(2,1)S(1)} %get-tuple-element.27.refs_1_, bf16[16,16,256]{2,1,0:T(8,128)(2,1)S(1)} %get-tuple-element.30.refs_2_, ...), custom_call_target="tpu_custom_call" | custom-call | tf_op jit(solution)/shard_map/pick_rows/pallas_call | solution.py:171
  19.3 0.0 copy-start.7
  19.3 0.0 copy-start.8
  19.3 6.1 %all-to-all-start = ((bf16[16,4,16,256]{3,2,1,0:T(8,128)(2,1)}), bf16[16,4,16,256]{3,2,1,0:T(8,128)(2,1)S(1)}, u32[]{:S(2)}, u32[]{:S(2)}) async-start(bf16[16,4,16,256]{3,2,1,0:T(8,128)(2,1)} %bitcast.12), calls=%async_computation | async-start | bytes 1048576 | tf_op jit(solution)/shard_map/all_to_all | solution.py:494
  25.5 0.2 dynamic-slice_reduce_fusion
  25.6 0.0 copy-start.13
  25.6 0.7 %copy-done.13 = s32[1,8]{1,0:T(1,128)S(1)} copy-done((s32[1,8]{1,0:T(1,128)S(1)}, s32[1,8]{1,0:T(1,128)}, u32[]{:S(2)}) %copy-start.13) | copy-done | bytes 56
  26.3 0.1 pad_add_fusion.numbers_ref
  26.4 0.0 copy-start.10
  26.4 0.0 copy-done.7
  26.4 0.0 copy-done.8
  26.4 0.7 %copy-done.10 = f32[256]{0:T(256)S(1)} copy-done((f32[256]{0:T(256)S(1)}, f32[256]{0:T(256)}, u32[]{:S(2)}) %copy-start.10) | copy-done | bytes 1048
  27.1 0.0 copy-start.5
  27.1 0.0 copy-start.6
  27.1 0.0 copy-start.9
  27.1 9.5 %local_keys.1 = (bf16[16,128,256]{2,1,0:T(8,128)(2,1)}, bf16[16,256,128]{2,1,0:T(8,128)(2,1)}, bf16[16,128,256]{2,1,0:T(8,128)(2,1)}, f32[16,16,128]{2,1,0:T(8,128)S(1)}) custom-call(bf16[16,16,256]{2,1,0:T(8,128)(2,1)S(1)} %get-tuple-element.24.refs_0_, bf16[16,16,256]{2,1,0:T(8,128)(2,1)S(1)} %get-tuple-element.27.refs_1_, ...), custom_call_target="tpu_custom_call" | custom-call | flops 1610612736 | bytes 5242880 | tf_op jit(solution)/shard_map/local_keys/pallas_call | solution.py:243
  36.6 3.3 %all-to-all-done.refs_0_ = bf16[16,4,16,256]{3,2,1,0:T(8,128)(2,1)S(1)} async-done(((bf16[16,4,16,256]{3,2,1,0:T(8,128)(2,1)}), bf16[16,4,16,256]{3,2,1,0:T(8,128)(2,1)S(1)}, u32[]{:S(2)}, u32[]{:S(2)}) %all-to-all-start) | async-done | bytes 524320 | tf_op jit(solution)/shard_map/all_to_all | solution.py:494
  39.9 0.0 copy-done.5
  39.9 0.0 copy-done.6
  39.9 0.0 copy-done.9
  39.9 8.8 %remote_keys_and_feed_forward.1 = bf16[128,16,256]{2,1,0:T(8,128)(2,1)} custom-call(s32[17]{0:T(128)S(1)} %pad_add_fusion.numbers_ref, bf16[16,4,16,256]{3,2,1,0:T(8,128)(2,1)S(1)} %all-to-all-done.refs_0_, f32[1,256]{1,0:T(1,128)S(1)} %bitcast.11, bf16[256,512]{1,0:T(8,128)(2,1)S(1)} %copy-done.7, f32[16,16,128]{2,1,0:T(8,128)S(1)} %get-tuple-element.39.refs_3_, ...), custom_call_target="tpu_custom_call" | custom-call | flops 2415919104 | bytes 6291456 | tf_op jit(solution)/shard_map/remote_keys_and_feed_forward/pallas_call | solution.py:417
  (5 shorter events, 0.0 us)
Async XLA Ops:
  0.0 5.7 %copy-start = (bf16[64,32,256]{2,1,0:T(8,128)(2,1)S(1)}, bf16[64,32,256]{2,1,0:T(8,128)(2,1)}, u32[]{:S(2)}) copy-start(bf16[64,32,256]{2,1,0:T(8,128)(2,1)} %x_ref.4) | copy-start | bytes 3145732
  0.0 5.7 %copy-start.1 = (bf16[256,512]{1,0:T(8,128)(2,1)S(1)}, bf16[256,512]{1,0:T(8,128)(2,1)}, u32[]{:S(2)}) copy-start(bf16[256,512]{1,0:T(8,128)(2,1)} %wkv_ref.7) | copy-start | bytes 786436
  0.0 5.7 %copy-start.2 = (bf16[256,256]{1,0:T(8,128)(2,1)S(1)}, bf16[256,256]{1,0:T(8,128)(2,1)}, u32[]{:S(2)}) copy-start(bf16[256,256]{1,0:T(8,128)(2,1)} %wq_ref.7) | copy-start | bytes 393220
  0.0 5.7 %copy-start.3 = (bf16[256,256]{1,0:T(8,128)(2,1)S(1)}, bf16[256,256]{1,0:T(8,128)(2,1)}, u32[]{:S(2)}) copy-start(bf16[256,256]{1,0:T(8,128)(2,1)} %wo_ref.7) | copy-start | bytes 393220
  2.7 3.0 %copy-start.4 = (f32[256]{0:T(256)S(1)}, f32[256]{0:T(256)}, u32[]{:S(2)}) copy-start(f32[256]{0:T(256)} %param.16) | copy-start | bytes 3076
  2.7 11.1 %collective-permute-start = (bf16[16,16,256]{2,1,0:T(8,128)(2,1)S(1)}, bf16[16,16,256]{2,1,0:T(8,128)(2,1)S(1)}, u32[]{:S(2)}, u32[]{:S(2)}) collective-permute-start(bf16[16,16,256]{2,1,0:T(8,128)(2,1)S(1)} %get-tuple-element.34), channel_id=1, source_target_pairs={{0,1},{1,0},{2,3},{3,2},{4,5},{5,4},{6,7},{7,6},{8,9},{9,8},{10,11... | collective-permute-start | bytes 393224 | tf_op jit(solution)/shard_map/ppermute | solution.py:479
  7.2 6.6 %collective-permute-start.1 = (bf16[16,16,256]{2,1,0:T(8,128)(2,1)S(1)}, bf16[16,16,256]{2,1,0:T(8,128)(2,1)S(1)}, u32[]{:S(2)}, u32[]{:S(2)}) collective-permute-start(bf16[16,16,256]{2,1,0:T(8,128)(2,1)S(1)} %get-tuple-element.35), channel_id=1, source_target_pairs={{0,1},{1,0},{2,3},{3,2},{4,5},{5,4},{6,7},{7,6},{8,9},{9,8},{10,11... | collective-permute-start | bytes 393224 | tf_op jit(solution)/shard_map/ppermute | solution.py:479
  9.3 6.5 %collective-permute-start.2 = (bf16[16,16,256]{2,1,0:T(8,128)(2,1)S(1)}, bf16[16,16,256]{2,1,0:T(8,128)(2,1)S(1)}, u32[]{:S(2)}, u32[]{:S(2)}) collective-permute-start(bf16[16,16,256]{2,1,0:T(8,128)(2,1)S(1)} %get-tuple-element.36), channel_id=1, source_target_pairs={{0,1},{1,0},{2,3},{3,2},{4,5},{5,4},{6,7},{7,6},{8,9},{9,8},{10,11... | collective-permute-start | bytes 393224 | tf_op jit(solution)/shard_map/ppermute | solution.py:479
  10.8 2.8 %copy-start.12 = (s32[16,8,4]{0,2,1:T(4,128)S(1)}, s32[16,8,4]{0,2,1:T(4,128)}, u32[]{:S(2)}) copy-start(s32[16,8,4]{0,2,1:T(4,128)} %param.29) | copy-start | bytes 6148
  12.2 5.6 %collective-permute-start.3 = (bf16[16,16,256]{2,1,0:T(8,128)(2,1)S(1)}, bf16[16,16,256]{2,1,0:T(8,128)(2,1)S(1)}, u32[]{:S(2)}, u32[]{:S(2)}) collective-permute-start(bf16[16,16,256]{2,1,0:T(8,128)(2,1)S(1)} %get-tuple-element.38), channel_id=1, source_target_pairs={{0,1},{1,0},{2,3},{3,2},{4,5},{5,4},{6,7},{7,6},{8,9},{9,8},{10,11... | collective-permute-start | bytes 393224 | tf_op jit(solution)/shard_map/ppermute | solution.py:479
  12.9 0.7 %copy-start.11 = (s32[16,8]{0,1:T(8,128)S(1)}, s32[16,8]{0,1:T(8,128)}, u32[]{:S(2)}) copy-start(s32[16,8]{0,1:T(8,128)} %param.27) | copy-start | bytes 1540
  19.3 7.1 %copy-start.7 = (bf16[256,512]{1,0:T(8,128)(2,1)S(1)}, bf16[256,512]{1,0:T(8,128)(2,1)}, u32[]{:S(2)}) copy-start(bf16[256,512]{1,0:T(8,128)(2,1)} %refs_2_.1) | copy-start | bytes 786436
  19.3 7.1 %copy-start.8 = (bf16[256,256]{1,0:T(8,128)(2,1)S(1)}, bf16[256,256]{1,0:T(8,128)(2,1)}, u32[]{:S(2)}) copy-start(bf16[256,256]{1,0:T(8,128)(2,1)} %refs_9_.1) | copy-start | bytes 393220
  19.3 20.6 %all-to-all-start = ((bf16[16,4,16,256]{3,2,1,0:T(8,128)(2,1)}), bf16[16,4,16,256]{3,2,1,0:T(8,128)(2,1)S(1)}, u32[]{:S(2)}, u32[]{:S(2)}) async-start(bf16[16,4,16,256]{3,2,1,0:T(8,128)(2,1)} %bitcast.12), calls=%async_computation | async-start | bytes 1048576 | tf_op jit(solution)/shard_map/all_to_all | solution.py:494
  25.6 0.7 %copy-start.13 = (s32[1,8]{1,0:T(1,128)S(1)}, s32[1,8]{1,0:T(1,128)}, u32[]{:S(2)}) copy-start(s32[1,8]{1,0:T(1,128)} %param.28) | copy-start | bytes 100
  26.4 0.7 %copy-start.10 = (f32[256]{0:T(256)S(1)}, f32[256]{0:T(256)}, u32[]{:S(2)}) copy-start(f32[256]{0:T(256)} %param.20) | copy-start | bytes 3076
  27.1 12.9 %copy-start.5 = (bf16[256,1024]{1,0:T(8,128)(2,1)S(1)}, bf16[256,1024]{1,0:T(8,128)(2,1)}, u32[]{:S(2)}) copy-start(bf16[256,1024]{1,0:T(8,128)(2,1)} %refs_5_.1) | copy-start | bytes 1572868
  27.1 12.9 %copy-start.6 = (bf16[1024,256]{1,0:T(8,128)(2,1)S(1)}, bf16[1024,256]{1,0:T(8,128)(2,1)}, u32[]{:S(2)}) copy-start(bf16[1024,256]{1,0:T(8,128)(2,1)} %refs_6_.1) | copy-start | bytes 1572868
  27.1 12.9 %copy-start.9 = (bf16[256,256]{1,0:T(8,128)(2,1)S(1)}, bf16[256,256]{1,0:T(8,128)(2,1)}, u32[]{:S(2)}) copy-start(bf16[256,256]{1,0:T(8,128)(2,1)} %refs_4_.1) | copy-start | bytes 393220

commit v9 on v8

--- a/solution.py
+++ b/solution.py
@@ -334,7 +334,7 @@
         masked = jnp.where(live[None], scores, NEG)
         ltop = stat_ref[t, :H]
         top = jnp.maximum(jnp.max(masked, axis=1), ltop)
-        e = jnp.exp2((masked - top[:, None, :]) * SCALE)
+        e = jnp.exp2(masked * SCALE - (top * SCALE)[:, None, :])
         keep = jnp.exp2((ltop - top) * SCALE)
         inverse = 1.0 / (jnp.sum(e, axis=1) + stat_ref[t, H:] * keep)
         keep = keep * inverse

time: 49.2 us -> 49.3 us (level)
  no operation moved by 1% of the time
where the time goes in v9:
time: 49.3 us; the launch traced here: 49 us
  Pallas kernels  26.8 us (54%)
  starting transfers between devices  12 us (24%)
  waiting for transfers between devices  7.35 us (15%)
  local copies, waits for them, and re-layouts  2.42 us (5%)
    pallas_call x1, Pallas kernels, local_part(): pl.pallas_call(functools.partial(local_kernel, len(pieces), split), out_s...  9.54 us
    pallas_call x1, Pallas kernels, finish(): pl.pallas_call(functools.partial(finish_kernel, split, sb), out_shape=jax...  8.87 us
    pallas_call x4, Pallas kernels, time_block(): pl.pallas_call(functools.partial(time_kernel, split), out_shape=out_shape...  6.97 us
    all_to_all x1, starting transfers between devices, local(): lax.all_to_all(outgoing, 'sensor', split_axis=0, concat_axis=0, tiled=True)  6.15 us
    ppermute x4, starting transfers between devices, local(): got.append(lax.ppermute(send, 'tm', [(0, 1), (1, 0)]))  5.81 us
    ppermute x4, waiting for transfers between devices, local(): got.append(lax.ppermute(send, 'tm', [(0, 1), (1, 0)]))  4.04 us
    all_to_all x1, waiting for transfers between devices, local(): lax.all_to_all(outgoing, 'sensor', split_axis=0, concat_axis=0, tiled=True)  3.31 us
    unnamed x28, local copies, waits for them, and re-layouts  2.06 us
  transfers between devices with their start and end apart: 5, of which 3 were waited for; matrix products, arithmetic and copies ran while one was open for 1% of the time, Pallas kernels for 28%

profile of v9, /device:TPU:0, one launch (start us, length us, event | category | flops | bytes accessed | tf_op | source)
XLA Modules:
  0.0 49.0 jit_solution(14985997323804540593)
XLA Ops:
  0.0 0.0 copy-start
  0.0 0.0 copy-start.1
  0.0 0.0 copy-start.2
  0.0 0.0 copy-start.3
  0.0 2.7 %time_block.4 = (bf16[16,16,256]{2,1,0:T(8,128)(2,1)S(1)}, bf16[16,16,256]{2,1,0:T(8,128)(2,1)S(1)}) custom-call(s32[1]{0:T(128)} %bitcast.my_ref, bf16[64,32,256]{2,1,0:T(8,128)(2,1)} %x_ref.4, f32[1,256]{1,0:T(1,128)} %bitcast.6, bf16[256,256]{1,0:T(8,128)(2,1)} %wq_ref.7, bf16[256,512]{1,0:T(8,128)(2,1)} %wkv_ref.7, bf16[256,256]{1,0:T(8,128)(2,1)} %wo_ref.7), custom_call_target="tpu_custom_call" | custom-call | flops 402653184 | bytes 524288 | tf_op jit(solution)/shard_map/time_block/pallas_call | solution.py:126
  2.7 0.0 copy-start.4
  2.7 3.0 %collective-permute-start = (bf16[16,16,256]{2,1,0:T(8,128)(2,1)S(1)}, bf16[16,16,256]{2,1,0:T(8,128)(2,1)S(1)}, u32[]{:S(2)}, u32[]{:S(2)}) collective-permute-start(bf16[16,16,256]{2,1,0:T(8,128)(2,1)S(1)} %get-tuple-element.34), channel_id=1, source_target_pairs={{0,1},{1,0},{2,3},{3,2},{4,5},{5,4},{6,7},{7,6},{8,9},{9,8},{10,11... | collective-permute-start | bytes 393224 | tf_op jit(solution)/shard_map/ppermute | solution.py:479
  5.7 0.0 copy-done
  5.7 0.0 copy-done.1
  5.7 0.0 copy-done.2
  5.7 0.0 copy-done.3
  5.7 0.0 copy-done.4
  5.7 1.4 %time_block.5 = (bf16[16,16,256]{2,1,0:T(8,128)(2,1)S(1)}, bf16[16,16,256]{2,1,0:T(8,128)(2,1)S(1)}) custom-call(s32[1]{0:T(128)} %bitcast.my_ref, bf16[64,32,256]{2,1,0:T(8,128)(2,1)S(1)} %copy-done, f32[1,256]{1,0:T(1,128)S(1)} %bitcast.7, bf16[256,256]{1,0:T(8,128)(2,1)S(1)} %copy-done.2, bf16[256,512]{1,0:T(8,128)(2,1)S(1)} %copy-done.1, ...), custom_call_target="tpu_custom_call" | custom-call | flops 402653184 | bytes 524288 | tf_op jit(solution)/shard_map/time_block/pallas_call | solution.py:126
  7.2 0.6 %collective-permute-start.1 = (bf16[16,16,256]{2,1,0:T(8,128)(2,1)S(1)}, bf16[16,16,256]{2,1,0:T(8,128)(2,1)S(1)}, u32[]{:S(2)}, u32[]{:S(2)}) collective-permute-start(bf16[16,16,256]{2,1,0:T(8,128)(2,1)S(1)} %get-tuple-element.35), channel_id=1, source_target_pairs={{0,1},{1,0},{2,3},{3,2},{4,5},{5,4},{6,7},{7,6},{8,9},{9,8},{10,11... | collective-permute-start | bytes 393224 | tf_op jit(solution)/shard_map/ppermute | solution.py:479
  7.8 1.4 %time_block.6 = (bf16[16,16,256]{2,1,0:T(8,128)(2,1)S(1)}, bf16[16,16,256]{2,1,0:T(8,128)(2,1)S(1)}) custom-call(s32[1]{0:T(128)} %bitcast.my_ref, bf16[64,32,256]{2,1,0:T(8,128)(2,1)S(1)} %copy-done, f32[1,256]{1,0:T(1,128)S(1)} %bitcast.8, bf16[256,256]{1,0:T(8,128)(2,1)S(1)} %copy-done.2, bf16[256,512]{1,0:T(8,128)(2,1)S(1)} %copy-done.1, ...), custom_call_target="tpu_custom_call" | custom-call | flops 402653184 | bytes 524288 | tf_op jit(solution)/shard_map/time_block/pallas_call | solution.py:126
  9.3 1.5 %collective-permute-start.2 = (bf16[16,16,256]{2,1,0:T(8,128)(2,1)S(1)}, bf16[16,16,256]{2,1,0:T(8,128)(2,1)S(1)}, u32[]{:S(2)}, u32[]{:S(2)}) collective-permute-start(bf16[16,16,256]{2,1,0:T(8,128)(2,1)S(1)} %get-tuple-element.36), channel_id=1, source_target_pairs={{0,1},{1,0},{2,3},{3,2},{4,5},{5,4},{6,7},{7,6},{8,9},{9,8},{10,11... | collective-permute-start | bytes 393224 | tf_op jit(solution)/shard_map/ppermute | solution.py:479
  10.8 0.0 copy-start.12
  10.8 1.4 %time_block.7 = (bf16[16,16,256]{2,1,0:T(8,128)(2,1)S(1)}, bf16[16,16,256]{2,1,0:T(8,128)(2,1)S(1)}) custom-call(s32[1]{0:T(128)} %bitcast.my_ref, bf16[64,32,256]{2,1,0:T(8,128)(2,1)S(1)} %copy-done, f32[1,256]{1,0:T(1,128)S(1)} %bitcast.9, bf16[256,256]{1,0:T(8,128)(2,1)S(1)} %copy-done.2, bf16[256,512]{1,0:T(8,128)(2,1)S(1)} %copy-done.1, ...), custom_call_target="tpu_custom_call" | custom-call | flops 402653184 | bytes 524288 | tf_op jit(solution)/shard_map/time_block/pallas_call | solution.py:126
  12.2 0.6 %collective-permute-start.3 = (bf16[16,16,256]{2,1,0:T(8,128)(2,1)S(1)}, bf16[16,16,256]{2,1,0:T(8,128)(2,1)S(1)}, u32[]{:S(2)}, u32[]{:S(2)}) collective-permute-start(bf16[16,16,256]{2,1,0:T(8,128)(2,1)S(1)} %get-tuple-element.38), channel_id=1, source_target_pairs={{0,1},{1,0},{2,3},{3,2},{4,5},{5,4},{6,7},{7,6},{8,9},{9,8},{10,11... | collective-permute-start | bytes 393224 | tf_op jit(solution)/shard_map/ppermute | solution.py:479
  12.9 0.0 copy-start.11
  12.9 0.7 %copy-done.11 = s32[16,8]{0,1:T(8,128)S(1)} copy-done((s32[16,8]{0,1:T(8,128)S(1)}, s32[16,8]{0,1:T(8,128)}, u32[]{:S(2)}) %copy-start.11) | copy-done | bytes 536
  13.6 0.0 copy-done.12
  13.6 0.1 copy.16
  13.7 0.1 add.22
  13.8 0.0 collective-permute-done.refs_4_
  13.8 0.0 collective-permute-done.1.refs_5_
  13.8 2.0 %collective-permute-done.2.refs_6_ = bf16[16,16,256]{2,1,0:T(8,128)(2,1)S(1)} collective-permute-done((bf16[16,16,256]{2,1,0:T(8,128)(2,1)S(1)}, bf16[16,16,256]{2,1,0:T(8,128)(2,1)S(1)}, u32[]{:S(2)}, u32[]{:S(2)}) %collective-permute-start.2) | collective-permute-done | bytes 131104 | tf_op jit(solution)/shard_map/ppermute | solution.py:479
  15.8 2.0 %collective-permute-done.3.refs_7_ = bf16[16,16,256]{2,1,0:T(8,128)(2,1)S(1)} collective-permute-done((bf16[16,16,256]{2,1,0:T(8,128)(2,1)S(1)}, bf16[16,16,256]{2,1,0:T(8,128)(2,1)S(1)}, u32[]{:S(2)}, u32[]{:S(2)}) %collective-permute-start.3) | collective-permute-done | bytes 131104 | tf_op jit(solution)/shard_map/ppermute | solution.py:479
  17.8 1.4 %pick_rows.1 = bf16[64,16,256]{2,1,0:T(8,128)(2,1)} custom-call(s32[64]{0:T(128)S(1)} %and_select_fusion.wanted_ref, bf16[16,16,256]{2,1,0:T(8,128)(2,1)S(1)} %get-tuple-element.24.refs_0_, bf16[16,16,256]{2,1,0:T(8,128)(2,1)S(1)} %get-tuple-element.27.refs_1_, bf16[16,16,256]{2,1,0:T(8,128)(2,1)S(1)} %get-tuple-element.30.refs_2_, ...), custom_call_target="tpu_custom_call" | custom-call | tf_op jit(solution)/shard_map/pick_rows/pallas_call | solution.py:171
  19.3 0.0 copy-start.7
  19.3 0.0 copy-start.8
  19.3 6.1 %all-to-all-start = ((bf16[16,4,16,256]{3,2,1,0:T(8,128)(2,1)}), bf16[16,4,16,256]{3,2,1,0:T(8,128)(2,1)S(1)}, u32[]{:S(2)}, u32[]{:S(2)}) async-start(bf16[16,4,16,256]{3,2,1,0:T(8,128)(2,1)} %bitcast.12), calls=%async_computation | async-start | bytes 1048576 | tf_op jit(solution)/shard_map/all_to_all | solution.py:494
  25.5 0.2 dynamic-slice_reduce_fusion
  25.6 0.0 copy-start.13
  25.6 0.7 %copy-done.13 = s32[1,8]{1,0:T(1,128)S(1)} copy-done((s32[1,8]{1,0:T(1,128)S(1)}, s32[1,8]{1,0:T(1,128)}, u32[]{:S(2)}) %copy-start.13) | copy-done | bytes 56
  26.3 0.1 pad_add_fusion.numbers_ref
  26.4 0.0 copy-start.10
  26.4 0.0 copy-done.7
  26.4 0.0 copy-done.8
  26.4 0.7 %copy-done.10 = f32[256]{0:T(256)S(1)} copy-done((f32[256]{0:T(256)S(1)}, f32[256]{0:T(256)}, u32[]{:S(2)}) %copy-start.10) | copy-done | bytes 1048
  27.1 0.0 copy-start.5
  27.1 0.0 copy-start.6
  27.1 9.5 %local_keys.1 = (bf16[16,128,256]{2,1,0:T(8,128)(2,1)}, bf16[16,256,128]{2,1,0:T(8,128)(2,1)}, bf16[16,128,256]{2,1,0:T(8,128)(2,1)}, f32[16,16,128]{2,1,0:T(8,128)S(1)}) custom-call(bf16[16,16,256]{2,1,0:T(8,128)(2,1)S(1)} %get-tuple-element.24.refs_0_, bf16[16,16,256]{2,1,0:T(8,128)(2,1)S(1)} %get-tuple-element.27.refs_1_, ...), custom_call_target="tpu_custom_call" | custom-call | flops 1610612736 | bytes 5242880 | tf_op jit(solution)/shard_map/local_keys/pallas_call | solution.py:243
  36.6 3.3 %all-to-all-done.refs_0_ = bf16[16,4,16,256]{3,2,1,0:T(8,128)(2,1)S(1)} async-done(((bf16[16,4,16,256]{3,2,1,0:T(8,128)(2,1)}), bf16[16,4,16,256]{3,2,1,0:T(8,128)(2,1)S(1)}, u32[]{:S(2)}, u32[]{:S(2)}) %all-to-all-start) | async-done | bytes 524320 | tf_op jit(solution)/shard_map/all_to_all | solution.py:494
  39.9 0.0 copy-done.5
  39.9 0.0 copy-done.6
  39.9 0.0 copy-done.9
  39.9 8.9 %remote_keys_and_feed_forward.1 = bf16[128,16,256]{2,1,0:T(8,128)(2,1)} custom-call(s32[17]{0:T(128)S(1)} %pad_add_fusion.numbers_ref, bf16[16,4,16,256]{3,2,1,0:T(8,128)(2,1)S(1)} %all-to-all-done.refs_0_, f32[1,256]{1,0:T(1,128)S(1)} %bitcast.11, bf16[256,512]{1,0:T(8,128)(2,1)S(1)} %copy-done.7, f32[16,16,128]{2,1,0:T(8,128)S(1)} %get-tuple-element.39.refs_3_, ...), custom_call_target="tpu_custom_call" | custom-call | flops 2415919104 | bytes 6291456 | tf_op jit(solution)/shard_map/remote_keys_and_feed_forward/pallas_call | solution.py:417
  (5 shorter events, 0.0 us)
Async XLA Ops:
  0.0 5.7 %copy-start = (bf16[64,32,256]{2,1,0:T(8,128)(2,1)S(1)}, bf16[64,32,256]{2,1,0:T(8,128)(2,1)}, u32[]{:S(2)}) copy-start(bf16[64,32,256]{2,1,0:T(8,128)(2,1)} %x_ref.4) | copy-start | bytes 3145732
  0.0 5.7 %copy-start.1 = (bf16[256,512]{1,0:T(8,128)(2,1)S(1)}, bf16[256,512]{1,0:T(8,128)(2,1)}, u32[]{:S(2)}) copy-start(bf16[256,512]{1,0:T(8,128)(2,1)} %wkv_ref.7) | copy-start | bytes 786436
  0.0 5.7 %copy-start.2 = (bf16[256,256]{1,0:T(8,128)(2,1)S(1)}, bf16[256,256]{1,0:T(8,128)(2,1)}, u32[]{:S(2)}) copy-start(bf16[256,256]{1,0:T(8,128)(2,1)} %wq_ref.7) | copy-start | bytes 393220
  0.0 5.7 %copy-start.3 = (bf16[256,256]{1,0:T(8,128)(2,1)S(1)}, bf16[256,256]{1,0:T(8,128)(2,1)}, u32[]{:S(2)}) copy-start(bf16[256,256]{1,0:T(8,128)(2,1)} %wo_ref.7) | copy-start | bytes 393220
  2.7 3.0 %copy-start.4 = (f32[256]{0:T(256)S(1)}, f32[256]{0:T(256)}, u32[]{:S(2)}) copy-start(f32[256]{0:T(256)} %param.16) | copy-start | bytes 3076
  2.7 11.1 %collective-permute-start = (bf16[16,16,256]{2,1,0:T(8,128)(2,1)S(1)}, bf16[16,16,256]{2,1,0:T(8,128)(2,1)S(1)}, u32[]{:S(2)}, u32[]{:S(2)}) collective-permute-start(bf16[16,16,256]{2,1,0:T(8,128)(2,1)S(1)} %get-tuple-element.34), channel_id=1, source_target_pairs={{0,1},{1,0},{2,3},{3,2},{4,5},{5,4},{6,7},{7,6},{8,9},{9,8},{10,11... | collective-permute-start | bytes 393224 | tf_op jit(solution)/shard_map/ppermute | solution.py:479
  7.2 6.6 %collective-permute-start.1 = (bf16[16,16,256]{2,1,0:T(8,128)(2,1)S(1)}, bf16[16,16,256]{2,1,0:T(8,128)(2,1)S(1)}, u32[]{:S(2)}, u32[]{:S(2)}) collective-permute-start(bf16[16,16,256]{2,1,0:T(8,128)(2,1)S(1)} %get-tuple-element.35), channel_id=1, source_target_pairs={{0,1},{1,0},{2,3},{3,2},{4,5},{5,4},{6,7},{7,6},{8,9},{9,8},{10,11... | collective-permute-start | bytes 393224 | tf_op jit(solution)/shard_map/ppermute | solution.py:479
  9.3 6.5 %collective-permute-start.2 = (bf16[16,16,256]{2,1,0:T(8,128)(2,1)S(1)}, bf16[16,16,256]{2,1,0:T(8,128)(2,1)S(1)}, u32[]{:S(2)}, u32[]{:S(2)}) collective-permute-start(bf16[16,16,256]{2,1,0:T(8,128)(2,1)S(1)} %get-tuple-element.36), channel_id=1, source_target_pairs={{0,1},{1,0},{2,3},{3,2},{4,5},{5,4},{6,7},{7,6},{8,9},{9,8},{10,11... | collective-permute-start | bytes 393224 | tf_op jit(solution)/shard_map/ppermute | solution.py:479
  10.8 2.8 %copy-start.12 = (s32[16,8,4]{0,2,1:T(4,128)S(1)}, s32[16,8,4]{0,2,1:T(4,128)}, u32[]{:S(2)}) copy-start(s32[16,8,4]{0,2,1:T(4,128)} %param.29) | copy-start | bytes 6148
  12.2 5.6 %collective-permute-start.3 = (bf16[16,16,256]{2,1,0:T(8,128)(2,1)S(1)}, bf16[16,16,256]{2,1,0:T(8,128)(2,1)S(1)}, u32[]{:S(2)}, u32[]{:S(2)}) collective-permute-start(bf16[16,16,256]{2,1,0:T(8,128)(2,1)S(1)} %get-tuple-element.38), channel_id=1, source_target_pairs={{0,1},{1,0},{2,3},{3,2},{4,5},{5,4},{6,7},{7,6},{8,9},{9,8},{10,11... | collective-permute-start | bytes 393224 | tf_op jit(solution)/shard_map/ppermute | solution.py:479
  12.9 0.7 %copy-start.11 = (s32[16,8]{0,1:T(8,128)S(1)}, s32[16,8]{0,1:T(8,128)}, u32[]{:S(2)}) copy-start(s32[16,8]{0,1:T(8,128)} %param.27) | copy-start | bytes 1540
  19.3 7.1 %copy-start.7 = (bf16[256,512]{1,0:T(8,128)(2,1)S(1)}, bf16[256,512]{1,0:T(8,128)(2,1)}, u32[]{:S(2)}) copy-start(bf16[256,512]{1,0:T(8,128)(2,1)} %refs_2_.1) | copy-start | bytes 786436
  19.3 7.1 %copy-start.8 = (bf16[256,256]{1,0:T(8,128)(2,1)S(1)}, bf16[256,256]{1,0:T(8,128)(2,1)}, u32[]{:S(2)}) copy-start(bf16[256,256]{1,0:T(8,128)(2,1)} %refs_9_.1) | copy-start | bytes 393220
  19.3 20.6 %all-to-all-start = ((bf16[16,4,16,256]{3,2,1,0:T(8,128)(2,1)}), bf16[16,4,16,256]{3,2,1,0:T(8,128)(2,1)S(1)}, u32[]{:S(2)}, u32[]{:S(2)}) async-start(bf16[16,4,16,256]{3,2,1,0:T(8,128)(2,1)} %bitcast.12), calls=%async_computation | async-start | bytes 1048576 | tf_op jit(solution)/shard_map/all_to_all | solution.py:494
  25.6 0.7 %copy-start.13 = (s32[1,8]{1,0:T(1,128)S(1)}, s32[1,8]{1,0:T(1,128)}, u32[]{:S(2)}) copy-start(s32[1,8]{1,0:T(1,128)} %param.28) | copy-start | bytes 100
  26.4 0.7 %copy-start.10 = (f32[256]{0:T(256)S(1)}, f32[256]{0:T(256)}, u32[]{:S(2)}) copy-start(f32[256]{0:T(256)} %param.20) | copy-start | bytes 3076
  27.1 12.9 %copy-start.5 = (bf16[256,1024]{1,0:T(8,128)(2,1)S(1)}, bf16[256,1024]{1,0:T(8,128)(2,1)}, u32[]{:S(2)}) copy-start(bf16[256,1024]{1,0:T(8,128)(2,1)} %refs_5_.1) | copy-start | bytes 1572868
  27.1 12.9 %copy-start.6 = (bf16[1024,256]{1,0:T(8,128)(2,1)S(1)}, bf16[1024,256]{1,0:T(8,128)(2,1)}, u32[]{:S(2)}) copy-start(bf16[1024,256]{1,0:T(8,128)(2,1)} %refs_6_.1) | copy-start | bytes 1572868
  27.1 12.9 %copy-start.9 = (bf16[256,256]{1,0:T(8,128)(2,1)S(1)}, bf16[256,256]{1,0:T(8,128)(2,1)}, u32[]{:S(2)}) copy-start(bf16[256,256]{1,0:T(8,128)(2,1)} %refs_4_.1) | copy-start | bytes 393220
